TPU v7x, 32 devices: a whole 2x2x4 slice. The times are simulated.
32 devices in a mesh: stream: 2 (over core), blk: 16 (over z, y, x).
Axes of the slice: x: 2, y: 2, z: 4, core: 2. Of those that a mesh axis runs over, the one named last changes fastest.
Arguments:
- inputs: bfloat16 [2, 2, 2048, 1536], P(None, 'stream', 'blk'), may hold values from -6 to 6
- cotangent: bfloat16 [2, 2, 2048, 1536], P(None, 'stream', 'blk'), may hold values from -6 to 6
- seq_lengths: int32 [2, 2, 9], P(None, 'stream'), may hold values from 1 to 1984, as said below
- gain_attn: bfloat16 [1536], P(('stream', 'blk')), may hold values from 0.5 to 1.5
- gain_ffn: bfloat16 [1536], P(('stream', 'blk')), may hold values from 0.5 to 1.5
- w_query: bfloat16 [1536, 1536], P(('stream', 'blk')), may hold values from -0.15625 to 0.15625
- w_key: bfloat16 [1536, 768], P(('stream', 'blk')), may hold values from -0.15625 to 0.15625
- w_value: bfloat16 [1536, 768], P(('stream', 'blk')), may hold values from -0.15625 to 0.15625
- w_out: bfloat16 [1536, 1536], P(('stream', 'blk')), may hold values from -0.625 to 0.625
- w_gate: bfloat16 [1536, 4096], P(('stream', 'blk')), may hold values from -0.15625 to 0.15625
- w_up: bfloat16 [1536, 4096], P(('stream', 'blk')), may hold values from -0.15625 to 0.15625
- w_down: bfloat16 [4096, 1536], P(('stream', 'blk')), may hold values from -0.09375 to 0.09375
Outputs:
- output: bfloat16 [2, 2, 2048, 1536], P(None, 'stream', 'blk')
- input_grad: float32 [2, 2, 2048, 1536], P(None, 'stream', 'blk')
- grad_gain_attn: float32 [1536], P(('stream', 'blk'))
- grad_gain_ffn: float32 [1536], P(('stream', 'blk'))
- grad_w_query: float32 [1536, 1536], P(('stream', 'blk'))
- grad_w_key: float32 [1536, 768], P(('stream', 'blk'))
- grad_w_value: float32 [1536, 768], P(('stream', 'blk'))
- grad_w_out: float32 [1536, 1536], P(('stream', 'blk'))
- grad_w_gate: float32 [1536, 4096], P(('stream', 'blk'))
- grad_w_up: float32 [1536, 4096], P(('stream', 'blk'))
- grad_w_down: float32 [4096, 1536], P(('stream', 'blk'))
Inputs may be any that keep to these rules, and one draw needn't show every extreme that they name: `seq_lengths`: the lengths of a pack sum to 2048; one sequence of each pack, at a place drawn from the seed, is the longest. In the packs of even-numbered micro-batches each other sequence holds at most (127) // 8 positions and together they hold a fixed number. In the packs of odd-numbered micro-batches each other sequence holds 64 to 192 positions and the longest holds exactly 1024.
All inputs are finite; a program needn't handle non-finite values.
Results may differ from a plain program's by a relative error of at most 0.019.
Values may be sent and summed in bfloat16 or wider, within the bound.
No kernel may reach another device: no remote copies, remote signals or barrier semaphores. Data moves between devices by JAX's collectives and lax.ppermute only.
A program may use at most 640 MiB of HBM per device.

v0:
```python
import math

import jax
import jax.numpy as jnp
from jax import lax
from jax.sharding import PartitionSpec as P

HQ = 16
HK = 8
DH = 96


epsilon = 1e-05
rope_base = 100000.0
masked_score = -1e30


def rms_scale(values):
    return lax.rsqrt(jnp.mean(values * values, axis=-1, keepdims=True) + epsilon)


def norm_back(values, scale_rows, gain_row, grad_normed):
    grad_gain = jnp.sum(grad_normed * values * scale_rows, axis=0)
    weighted = grad_normed * gain_row
    grad_values = scale_rows * weighted - values * scale_rows**3 * jnp.mean(
        values * weighted, axis=-1, keepdims=True
    )
    return (grad_gain, grad_values)


def rope_tables(rope_place):
    half_width = DH // 2
    frequency = rope_base ** (-2.0 * jnp.arange(half_width, dtype=jnp.float32) / DH)
    angles = rope_place.astype(jnp.float32)[:, None] * frequency[None, :]
    return (jnp.cos(angles)[:, None, :], jnp.sin(angles)[:, None, :])


def rotate(values, cos_table, sin_table):
    half_width = values.shape[-1] // 2
    first_half = values[..., :half_width]
    second_half = values[..., half_width:]
    return jnp.concatenate(
        [
            first_half * cos_table - second_half * sin_table,
            second_half * cos_table + first_half * sin_table,
        ],
        axis=-1,
    )


def on_device(
    inputs,
    cotangent,
    seq_lengths,
    gain_attn,
    gain_ffn,
    w_query,
    w_key,
    w_value,
    w_out,
    w_gate,
    w_up,
    w_down,
):
    shards = (gain_attn, gain_ffn, w_query, w_key, w_value, w_out, w_gate, w_up, w_down)
    micro_count = inputs.shape[0]
    tok_rows = inputs.shape[2]
    pack_len = tok_rows * lax.axis_size("blk")
    per_group = HQ // HK
    score_scale = 1.0 / math.sqrt(DH)
    positions = lax.axis_index("blk") * tok_rows + jnp.arange(tok_rows, dtype=jnp.int32)
    last_row = positions[tok_rows - 1]
    running = [jnp.zeros(shard.shape, jnp.float32) for shard in shards]
    grad_terms = [None] * len(shards)

    def collect(slot, term):
        grad_terms[slot] = term

    outputs = []
    input_grads = []
    for micro_index in range(micro_count):
        gathered = (
            lax.all_gather(gain_attn, ("stream", "blk"), axis=0, tiled=True),
            lax.all_gather(gain_ffn, ("stream", "blk"), axis=0, tiled=True),
            lax.all_gather(w_query, ("stream", "blk"), axis=0, tiled=True),
            lax.all_gather(w_key, ("stream", "blk"), axis=0, tiled=True),
            lax.all_gather(w_value, ("stream", "blk"), axis=0, tiled=True),
            lax.all_gather(w_out, ("stream", "blk"), axis=0, tiled=True),
            lax.all_gather(w_gate, ("stream", "blk"), axis=0, tiled=True),
            lax.all_gather(w_up, ("stream", "blk"), axis=0, tiled=True),
            lax.all_gather(w_down, ("stream", "blk"), axis=0, tiled=True),
        )
        gain_one = gathered[0].astype(jnp.float32)
        gain_two = gathered[1].astype(jnp.float32)
        full_query, full_key, full_value, full_out, full_gate, full_up, full_down = gathered[2:]
        lengths = seq_lengths[micro_index, 0]
        seq_ends = jnp.cumsum(lengths)
        seq_begin = jnp.sum(
            jnp.where(seq_ends[None, :] <= positions[:, None], lengths[None, :], 0), axis=1
        )
        first_begin = seq_begin[0]
        cos_table, sin_table = rope_tables(positions - seq_begin)
        layer_in = inputs[micro_index, 0].astype(jnp.float32)
        scale_one = rms_scale(layer_in)
        normed_one = (layer_in * scale_one * gain_one).astype(jnp.bfloat16)
        query_pre = jnp.dot(normed_one, full_query, preferred_element_type=jnp.float32)
        key_pre = jnp.dot(normed_one, full_key, preferred_element_type=jnp.float32)
        value_pre = jnp.dot(normed_one, full_value, preferred_element_type=jnp.float32)
        query_rot = rotate(query_pre.reshape(tok_rows, HQ, DH), cos_table, sin_table).astype(
            jnp.bfloat16
        )
        key_rot = (
            rotate(key_pre.reshape(tok_rows, HK, DH), cos_table, sin_table)
            .reshape(tok_rows, HK * DH)
            .astype(jnp.bfloat16)
        )
        value_low = value_pre.astype(jnp.bfloat16)
        query_heads = query_rot.reshape(tok_rows, HK, per_group, DH)

        def block_mask(piece_start, piece_rows):
            key_place = jnp.arange(piece_rows, dtype=jnp.int32)
            allowed = (key_place[None, :] <= positions[:, None]) & (
                key_place[None, :] >= seq_begin[:, None]
            )
            useful = (piece_start <= last_row) & (piece_start + piece_rows - 1 >= first_begin)
            return (allowed, useful)

        initial = (
            jnp.full((HK, per_group, tok_rows), masked_score, jnp.float32),
            jnp.zeros((HK, per_group, tok_rows), jnp.float32),
            jnp.zeros((tok_rows, HK, per_group, DH), jnp.float32),
        )
        key_piece = lax.all_gather(key_rot, "blk", axis=0, tiled=True)
        value_piece = lax.all_gather(value_low, "blk", axis=0, tiled=True)
        attend_piece_rows = key_piece.shape[0]
        attend_allowed, attend_useful = block_mask(jnp.int32(0), attend_piece_rows)

        def update(state):
            top_score, row_total, accumulated = state
            scores = (
                jnp.einsum(
                    "qhgd,khd->hgqk",
                    query_heads,
                    key_piece.reshape(attend_piece_rows, HK, DH),
                    preferred_element_type=jnp.float32,
                )
                * score_scale
            )
            scores = jnp.where(attend_allowed, scores, masked_score)
            new_top = jnp.maximum(top_score, jnp.max(scores, axis=-1))
            weights = jnp.where(attend_allowed, jnp.exp(scores - new_top[..., None]), 0.0)
            row_total = jnp.sum(weights, axis=-1)
            mixed_values = jnp.einsum(
                "hgqk,khd->qhgd",
                weights.astype(jnp.bfloat16),
                value_piece.reshape(attend_piece_rows, HK, DH),
                preferred_element_type=jnp.float32,
            )
            accumulated = mixed_values
            return (new_top, row_total, accumulated)

        top_score, row_total, accumulated = lax.cond(
            attend_useful, update, lambda state: state, initial
        )
        attended = (accumulated / jnp.transpose(row_total, (2, 0, 1))[..., None]).reshape(
            tok_rows, HQ * DH
        )
        log_total = top_score + jnp.log(row_total)
        attn_low = attended.astype(jnp.bfloat16)
        middle = layer_in + jnp.dot(attn_low, full_out, preferred_element_type=jnp.float32)
        scale_two = rms_scale(middle)
        normed_two = (middle * scale_two * gain_two).astype(jnp.bfloat16)
        gate_pre = jnp.dot(normed_two, full_gate, preferred_element_type=jnp.float32)
        up_pre = jnp.dot(normed_two, full_up, preferred_element_type=jnp.float32)
        sigmoid_gate = jax.nn.sigmoid(gate_pre)
        silu_gate = gate_pre * sigmoid_gate
        hidden = (silu_gate * up_pre).astype(jnp.bfloat16)
        result = middle + jnp.dot(hidden, full_down, preferred_element_type=jnp.float32)
        outputs.append(result.astype(jnp.bfloat16))
        grad_y = cotangent[micro_index, 0].astype(jnp.float32)
        grad_mlp = grad_y.astype(jnp.bfloat16)
        collect(8, jnp.dot(hidden.T, grad_mlp, preferred_element_type=jnp.float32))
        grad_hidden = jnp.dot(grad_mlp, full_down.T, preferred_element_type=jnp.float32)
        grad_gate = (
            grad_hidden * up_pre * sigmoid_gate * (1.0 + gate_pre * (1.0 - sigmoid_gate))
        ).astype(jnp.bfloat16)
        grad_up = (grad_hidden * silu_gate).astype(jnp.bfloat16)
        collect(6, jnp.dot(normed_two.T, grad_gate, preferred_element_type=jnp.float32))
        collect(7, jnp.dot(normed_two.T, grad_up, preferred_element_type=jnp.float32))
        grad_normed_two = jnp.dot(
            grad_gate, full_gate.T, preferred_element_type=jnp.float32
        ) + jnp.dot(grad_up, full_up.T, preferred_element_type=jnp.float32)
        grad_gain_two, grad_middle_norm = norm_back(middle, scale_two, gain_two, grad_normed_two)
        collect(1, grad_gain_two)
        grad_middle = grad_y + grad_middle_norm
        grad_branch = grad_middle.astype(jnp.bfloat16)
        collect(5, jnp.dot(attn_low.T, grad_branch, preferred_element_type=jnp.float32))
        grad_attn = jnp.dot(grad_branch, full_out.T, preferred_element_type=jnp.float32).astype(
            jnp.bfloat16
        )
        grad_heads = grad_attn.reshape(tok_rows, HK, per_group, DH)
        row_delta = jnp.transpose(
            jnp.sum(
                (grad_attn.astype(jnp.float32) * attended).reshape(tok_rows, HK, per_group, DH),
                axis=-1,
            ),
            (1, 2, 0),
        )

        def attend_back(carried, pieces, piece_start):
            key_piece, value_piece = pieces
            piece_rows = key_piece.shape[0]
            allowed, useful = block_mask(piece_start, piece_rows)

            def update(state):
                key_heads = key_piece.reshape(piece_rows, HK, DH)
                value_heads = value_piece.reshape(piece_rows, HK, DH)
                scores = (
                    jnp.einsum(
                        "qhgd,khd->hgqk", query_heads, key_heads, preferred_element_type=jnp.float32
                    )
                    * score_scale
                )
                weights = jnp.where(allowed, jnp.exp(scores - log_total[..., None]), 0.0)
                weights_low = weights.astype(jnp.bfloat16)
                grad_probs = jnp.einsum(
                    "qhgd,khd->hgqk", grad_heads, value_heads, preferred_element_type=jnp.float32
                )
                grad_scores = (weights * (grad_probs - row_delta[..., None])).astype(jnp.bfloat16)
                grad_query = (
                    jnp.einsum(
                        "hgqk,khd->qhgd", grad_scores, key_heads, preferred_element_type=jnp.float32
                    ).reshape(tok_rows, HQ * DH)
                    * score_scale
                )
                key_terms = (
                    jnp.einsum(
                        "hgqk,qhgd->khd",
                        grad_scores,
                        query_heads,
                        preferred_element_type=jnp.float32,
                    ).reshape(piece_rows, HK * DH)
                    * score_scale
                )
                value_terms = jnp.einsum(
                    "hgqk,qhgd->khd", weights_low, grad_heads, preferred_element_type=jnp.float32
                ).reshape(piece_rows, HK * DH)
                return (grad_query, key_terms, value_terms)

            return lax.cond(useful, update, lambda state: state, carried)

        initial_back = (
            jnp.zeros((tok_rows, HQ * DH), jnp.float32),
            jnp.zeros((pack_len, HK * DH), jnp.float32),
            jnp.zeros((pack_len, HK * DH), jnp.float32),
        )
        grad_query, grad_keys, grad_values = attend_back(
            initial_back,
            (
                lax.all_gather(key_rot, "blk", axis=0, tiled=True),
                lax.all_gather(value_low, "blk", axis=0, tiled=True),
            ),
            jnp.int32(0),
        )
        own_keys, own_values = (
            lax.psum_scatter(grad_keys, "blk", scatter_dimension=0, tiled=True),
            lax.psum_scatter(grad_values, "blk", scatter_dimension=0, tiled=True),
        )
        grad_query_pre = (
            rotate(grad_query.reshape(tok_rows, HQ, DH), cos_table, -sin_table)
            .reshape(tok_rows, HQ * DH)
            .astype(jnp.bfloat16)
        )
        grad_key_pre = (
            rotate(own_keys.reshape(tok_rows, HK, DH), cos_table, -sin_table)
            .reshape(tok_rows, HK * DH)
            .astype(jnp.bfloat16)
        )
        grad_value_low = own_values.astype(jnp.bfloat16)
        collect(2, jnp.dot(normed_one.T, grad_query_pre, preferred_element_type=jnp.float32))
        collect(3, jnp.dot(normed_one.T, grad_key_pre, preferred_element_type=jnp.float32))
        collect(4, jnp.dot(normed_one.T, grad_value_low, preferred_element_type=jnp.float32))
        grad_normed_one = jnp.dot(grad_query_pre, full_query.T, preferred_element_type=jnp.float32)
        grad_normed_one = grad_normed_one + jnp.dot(
            grad_key_pre, full_key.T, preferred_element_type=jnp.float32
        )
        grad_normed_one = grad_normed_one + jnp.dot(
            grad_value_low, full_value.T, preferred_element_type=jnp.float32
        )
        grad_gain_one, grad_in_norm = norm_back(layer_in, scale_one, gain_one, grad_normed_one)
        collect(0, grad_gain_one)
        input_grads.append(grad_middle + grad_in_norm)
        partial_grads = (
            lax.psum_scatter(grad_terms[0], ("stream", "blk"), scatter_dimension=0, tiled=True),
            lax.psum_scatter(grad_terms[1], ("stream", "blk"), scatter_dimension=0, tiled=True),
            lax.psum_scatter(grad_terms[2], ("stream", "blk"), scatter_dimension=0, tiled=True),
            lax.psum_scatter(grad_terms[3], ("stream", "blk"), scatter_dimension=0, tiled=True),
            lax.psum_scatter(grad_terms[4], ("stream", "blk"), scatter_dimension=0, tiled=True),
            lax.psum_scatter(grad_terms[5], ("stream", "blk"), scatter_dimension=0, tiled=True),
            lax.psum_scatter(grad_terms[6], ("stream", "blk"), scatter_dimension=0, tiled=True),
            lax.psum_scatter(grad_terms[7], ("stream", "blk"), scatter_dimension=0, tiled=True),
            lax.psum_scatter(grad_terms[8], ("stream", "blk"), scatter_dimension=0, tiled=True),
        )
        for slot in range(len(shards)):
            running[slot] = running[slot] + partial_grads[slot]
    totals = tuple(running)
    return (jnp.stack(outputs)[:, None], jnp.stack(input_grads)[:, None]) + tuple(totals)


def solution(mesh):
    placed = (
        P(None, "stream", "blk", None),
        P(None, "stream", "blk", None),
        P(None, "stream", None),
        P(("stream", "blk")),
        P(("stream", "blk")),
        P(("stream", "blk"), None),
        P(("stream", "blk"), None),
        P(("stream", "blk"), None),
        P(("stream", "blk"), None),
        P(("stream", "blk"), None),
        P(("stream", "blk"), None),
        P(("stream", "blk"), None),
    )
    return jax.shard_map(
        on_device,
        mesh=mesh,
        in_specs=placed,
        out_specs=(
            P(None, "stream", "blk", None),
            P(None, "stream", "blk", None),
            P(("stream", "blk")),
            P(("stream", "blk")),
            P(("stream", "blk"), None),
            P(("stream", "blk"), None),
            P(("stream", "blk"), None),
            P(("stream", "blk"), None),
            P(("stream", "blk"), None),
            P(("stream", "blk"), None),
            P(("stream", "blk"), None),
        ),
        check_vma=False,
    )
```

profile of v0, /device:TPU:0, one launch (start us, length us, event | category | flops | bytes accessed | tf_op | source)
XLA Modules:
  0.0 2854.9 jit_solution(11664646725005866057)
XLA Ops:
  12.2 42.2 %all-reduce.5 = (bf16[1536]{0:T(1024)(128)(2,1)S(1)}, bf16[1536]{0:T(1024)(128)(2,1)S(1)}) all-reduce(bf16[1536]{0:T(1024)(128)(2,1)S(1)} %dynamic-update-slice, bf16[1536]{0:T(1024)(128)(2,1)S(1)} %dynamic-update-slice.1), channel_id=1, replica_groups=mesh['stream'=2,'blk'=16] {'stream','blk'}, use_global_device_ids=true, to_apply=%add | all-reduce | flops 3072 | bytes 12288
  76.4 53.6 %all-gather.18.cloned.1.call-done = bf16[1536,768]{1,0:T(8,128)(2,1)} async-done(((bf16[48,768]{1,0:T(8,128)(2,1)}), bf16[1536,768]{1,0:T(8,128)(2,1)}) %all-gather.18.cloned.1.call-update) | async-done | bytes 2359312 | tf_op jit(solution)/shard_map/all_gather | solution.py:87
  142.2 53.2 %all-gather.16.cloned.1.call-done = bf16[1536,1536]{1,0:T(8,128)(2,1)} async-done(((bf16[48,1536]{1,0:T(8,128)(2,1)}), bf16[1536,1536]{1,0:T(8,128)(2,1)}) %all-gather.16.cloned.1.call-update) | async-done | bytes 4718608 | tf_op jit(solution)/shard_map/all_gather | solution.py:85
  208.6 65.3 %all-gather.30.cloned.1.call-done = bf16[2048,768]{0,1:T(8,128)(2,1)} async-done(((bf16[128,768]{0,1:T(8,128)(2,1)}), bf16[2048,768]{0,1:T(8,128)(2,1)}) %all-gather.30.cloned.1.call-update) | async-done | bytes 3145744 | tf_op jit(solution)/shard_map/all_gather | solution.py:133
  273.9 69.6 %all-gather.32.cloned.1.call-done = bf16[2048,768]{1,0:T(8,128)(2,1)} async-done(((bf16[128,768]{1,0:T(8,128)(2,1)}), bf16[2048,768]{1,0:T(8,128)(2,1)}) %all-gather.32.cloned.1.call-update) | async-done | bytes 3145744 | tf_op jit(solution)/shard_map/all_gather | solution.py:134
  371.2 50.5 %all-gather.14.cloned.1.call-done = bf16[2048,768]{0,1:T(8,128)(2,1)} async-done(((bf16[128,768]{0,1:T(8,128)(2,1)}), bf16[2048,768]{0,1:T(8,128)(2,1)}) %all-gather.14.cloned.1.call-update) | async-done | bytes 3145744 | tf_op jit(solution)/shard_map/all_gather | solution.py:133
  421.6 69.7 %all-gather.20.cloned.1.call-done = bf16[2048,768]{1,0:T(8,128)(2,1)} async-done(((bf16[128,768]{1,0:T(8,128)(2,1)}), bf16[2048,768]{1,0:T(8,128)(2,1)}) %all-gather.20.cloned.1.call-update) | async-done | bytes 3145744 | tf_op jit(solution)/shard_map/all_gather | solution.py:134
  518.1 38.2 %all-gather.22.cloned.1.call-done = bf16[1536,1536]{1,0:T(8,128)(2,1)} async-done(((bf16[48,1536]{1,0:T(8,128)(2,1)}), bf16[1536,1536]{1,0:T(8,128)(2,1)}) %all-gather.22.cloned.1.call-update) | async-done | bytes 4718608 | tf_op jit(solution)/shard_map/all_gather | solution.py:88
  564.1 90.0 %all-gather.24.cloned.1.call-done = bf16[1536,4096]{1,0:T(8,128)(2,1)} async-done(((bf16[48,4096]{1,0:T(8,128)(2,1)}), bf16[1536,4096]{1,0:T(8,128)(2,1)}) %all-gather.24.cloned.1.call-update) | async-done | bytes 12582928 | tf_op jit(solution)/shard_map/all_gather | solution.py:89
  661.8 89.3 %all-gather.26.cloned.1.call-done = bf16[1536,4096]{1,0:T(8,128)(2,1)} async-done(((bf16[48,4096]{1,0:T(8,128)(2,1)}), bf16[1536,4096]{1,0:T(8,128)(2,1)}) %all-gather.26.cloned.1.call-update) | async-done | bytes 12582928 | tf_op jit(solution)/shard_map/all_gather | solution.py:90
  758.8 89.4 %all-gather.28.cloned.1.call-done = bf16[4096,1536]{1,0:T(8,128)(2,1)} async-done(((bf16[128,1536]{1,0:T(8,128)(2,1)}), bf16[4096,1536]{1,0:T(8,128)(2,1)}) %all-gather.28.cloned.1.call-update) | async-done | bytes 12582928 | tf_op jit(solution)/shard_map/all_gather | solution.py:91
  933.3 53.8 %conditional.7 = (f32[2048,768]{0,1:T(8,128)}, f32[2048,768]{0,1:T(8,128)}, f32[128,16,48]{0,2,1:T(8,128)}, f32[128,16,48]{0,2,1:T(8,128)}) conditional(s32[]{:T(128)} %bitcast.82, () %tuple.62, (pred[128,2048]{0,1:T(8,128)(4,1)S(1)}, bf16[2048,768]{0,1:T(8,128)(2,1)S(1)}, bf16[128,8,2,96]{0,3,2,1:T(8,128)(2,1)}, f32[8,2,128]{2,1,0:T(2,128)}, ...), branch_computations={%region_25.26_spmd, %region_26.27_spmd} | conditional | flops 4070246400 | bytes 142655552 | solution.py:250
  998.5 52.8 %conditional.6 = (f32[2048,768]{0,1:T(8,128)}, f32[2048,768]{0,1:T(8,128)}, f32[128,16,48]{0,2,1:T(8,128)}, f32[128,16,48]{0,2,1:T(8,128)}) conditional(s32[]{:T(128)} %bitcast.64, () %tuple.60, (pred[128,2048]{0,1:T(8,128)(4,1)}, bf16[2048,768]{0,1:T(8,128)(2,1)S(1)}, bf16[128,8,2,96]{0,3,2,1:T(8,128)(2,1)S(1)}, f32[8,2,128]{2,1,0:T(2,128)}, ...), branch_computations={%region_18.19_spmd, %region_19.20_spmd} | conditional | flops 4070246400 | bytes 142688352 | solution.py:250
  1071.1 60.7 %reduce-scatter.16.cloned.1.call-done = f32[128,768]{0,1:T(8,128)} async-done(((f32[2048,768]{0,1:T(8,128)}), f32[128,768]{0,1:T(8,128)}) %reduce-scatter.16.cloned.1.call-update) | async-done | bytes 393232 | tf_op jit(solution)/shard_map/reduce_scatter | solution.py:266
  1132.8 149.4 %reduce-scatter.12.cloned.1.call-done = f32[128,768]{0,1:T(8,128)} async-done(((f32[2048,768]{0,1:T(8,128)}), f32[128,768]{0,1:T(8,128)}) %reduce-scatter.12.cloned.1.call-update) | async-done | bytes 393232 | tf_op jit(solution)/shard_map/reduce_scatter | solution.py:266
  1287.3 145.2 %reduce-scatter.14.cloned.1.call-done = f32[128,768]{0,1:T(8,128)} async-done(((f32[2048,768]{0,1:T(8,128)}), f32[128,768]{0,1:T(8,128)}) %reduce-scatter.14.cloned.1.call-update) | async-done | bytes 393232 | tf_op jit(solution)/shard_map/reduce_scatter | solution.py:267
  1436.5 146.4 %reduce-scatter.18.cloned.1.call-done = f32[128,768]{0,1:T(8,128)} async-done(((f32[2048,768]{0,1:T(8,128)}), f32[128,768]{0,1:T(8,128)}) %reduce-scatter.18.cloned.1.call-update) | async-done | bytes 393232 | tf_op jit(solution)/shard_map/reduce_scatter | solution.py:267
  1701.1 40.4 %all-reduce.4 = (f32[1536]{0:T(1024)S(1)}, f32[1536]{0:T(1024)S(1)}) all-reduce(f32[1536]{0:T(1024)S(1)} %add.260, f32[1536]{0:T(1024)S(1)} %add.261), channel_id=15, replica_groups=mesh['stream'=2,'blk'=16] {'stream','blk'}, use_global_device_ids=true, to_apply=%region_31.32.clone | all-reduce | flops 3072 | bytes 24576
  1745.5 120.8 %reduce-scatter.26.cloned.1.call-done = f32[48,1536]{1,0:T(8,128)} async-done(((f32[1536,1536]{1,0:T(8,128)}), f32[48,1536]{1,0:T(8,128)}) %reduce-scatter.26.cloned.1.call-update) | async-done | bytes 294928 | tf_op jit(solution)/shard_map/reduce_scatter | solution.py:299
  1866.3 111.9 %reduce-scatter.22.cloned.1.call-done = f32[48,768]{1,0:T(8,128)} async-done(((f32[1536,768]{1,0:T(8,128)}), f32[48,768]{1,0:T(8,128)}) %reduce-scatter.22.cloned.1.call-update) | async-done | bytes 147472 | tf_op jit(solution)/shard_map/reduce_scatter | solution.py:297
  1978.2 113.1 %reduce-scatter.24.cloned.1.call-done = f32[48,768]{1,0:T(8,128)} async-done(((f32[1536,768]{1,0:T(8,128)}), f32[48,768]{1,0:T(8,128)}) %reduce-scatter.24.cloned.1.call-update) | async-done | bytes 147472 | tf_op jit(solution)/shard_map/reduce_scatter | solution.py:298
  2091.3 251.4 %reduce-scatter.28.cloned.1.call-done = f32[48,4096]{1,0:T(8,128)} async-done(((f32[1536,4096]{1,0:T(8,128)}), f32[48,4096]{1,0:T(8,128)}) %reduce-scatter.28.cloned.1.call-update) | async-done | bytes 786448 | tf_op jit(solution)/shard_map/reduce_scatter | solution.py:300
  2342.7 253.2 %reduce-scatter.30.cloned.1.call-done = f32[48,4096]{1,0:T(8,128)} async-done(((f32[1536,4096]{1,0:T(8,128)}), f32[48,4096]{1,0:T(8,128)}) %reduce-scatter.30.cloned.1.call-update) | async-done | bytes 786448 | tf_op jit(solution)/shard_map/reduce_scatter | solution.py:301
  2595.8 252.0 %reduce-scatter.32.cloned.1.call-done = f32[128,1536]{1,0:T(8,128)} async-done(((f32[4096,1536]{1,0:T(8,128)}), f32[128,1536]{1,0:T(8,128)}) %reduce-scatter.32.cloned.1.call-update) | async-done | bytes 786448 | tf_op jit(solution)/shard_map/reduce_scatter | solution.py:302
  (341 shorter events, 533.9 us)
Async XLA Ops:
  7.2 63.7 %all-gather.12.cloned.1.call-start = ((), (), s32[]{:S(2)}) async-start(), calls=%async_computation.11 | async-start | bytes 2433024 | tf_op jit(solution)/shard_map/all_gather | solution.py:86
  7.9 122.1 %all-gather.18.cloned.1.call-start = ((), (), s32[]{:S(2)}) async-start(), calls=%async_computation.14 | async-start | bytes 2433024 | tf_op jit(solution)/shard_map/all_gather | solution.py:87
  8.7 186.7 %all-gather.16.cloned.1.call-start = ((), (), s32[]{:S(2)}) async-start(), calls=%async_computation.13 | async-start | bytes 4866048 | tf_op jit(solution)/shard_map/all_gather | solution.py:85
  9.4 264.5 %all-gather.30.cloned.1.call-start = ((), (), s32[]{:S(2)}) async-start(), calls=%async_computation.20 | async-start | bytes 3342336 | tf_op jit(solution)/shard_map/all_gather | solution.py:133
  76.4 267.1 %all-gather.32.cloned.1.call-start = ((), (), s32[]{:S(2)}) async-start(), calls=%async_computation.21 | async-start | bytes 3342336 | tf_op jit(solution)/shard_map/all_gather | solution.py:134
  132.9 288.7 %all-gather.14.cloned.1.call-start = ((), (), s32[]{:S(2)}) async-start(), calls=%async_computation.12 | async-start | bytes 3342336 | tf_op jit(solution)/shard_map/all_gather | solution.py:133
  134.6 356.8 %all-gather.20.cloned.1.call-start = ((), (), s32[]{:S(2)}) async-start(), calls=%async_computation.15 | async-start | bytes 3342336 | tf_op jit(solution)/shard_map/all_gather | solution.py:134
  137.5 418.8 %all-gather.22.cloned.1.call-start = ((), (), s32[]{:S(2)}) async-start(), calls=%async_computation.16 | async-start | bytes 4866048 | tf_op jit(solution)/shard_map/all_gather | solution.py:88
  138.3 515.8 %all-gather.24.cloned.1.call-start = ((), (), s32[]{:S(2)}) async-start(), calls=%async_computation.17 | async-start | bytes 12976128 | tf_op jit(solution)/shard_map/all_gather | solution.py:89
  139.0 612.0 %all-gather.26.cloned.1.call-start = ((), (), s32[]{:S(2)}) async-start(), calls=%async_computation.18 | async-start | bytes 12976128 | tf_op jit(solution)/shard_map/all_gather | solution.py:90
  139.6 708.6 %all-gather.28.cloned.1.call-start = ((), (), s32[]{:S(2)}) async-start(), calls=%async_computation.19 | async-start | bytes 12976128 | tf_op jit(solution)/shard_map/all_gather | solution.py:91
  140.3 991.4 %reduce-scatter.16.cloned.1.call-start = ((), (), s32[]{:S(2)}) async-start(), calls=%async_computation.24 | async-start | bytes 6684672 | tf_op jit(solution)/shard_map/reduce_scatter | solution.py:266
  142.2 349.2 %copy-start.32 = (pred[128,2048]{0,1:T(8,128)(4,1)}, pred[128,2048]{0,1:T(8,128)(4,1)S(1)}, u32[]{:S(2)}) copy-start(pred[128,2048]{0,1:T(8,128)(4,1)S(1)} %get-tuple-element.373) | copy-start | bytes 786436
  208.6 282.7 %copy-start.27 = (bf16[128,8,2,96]{0,3,2,1:T(8,128)(2,1)}, bf16[128,8,2,96]{0,3,2,1:T(8,128)(2,1)S(1)}, u32[]{:S(2)}) copy-start(bf16[128,8,2,96]{0,3,2,1:T(8,128)(2,1)S(1)} %pad_maximum_fusion) | copy-start | bytes 1179652
  987.1 295.1 %reduce-scatter.12.cloned.1.call-start = ((), (), s32[]{:S(2)}) async-start(), calls=%async_computation.22 | async-start | bytes 6684672 | tf_op jit(solution)/shard_map/reduce_scatter | solution.py:266
  1051.4 381.1 %reduce-scatter.14.cloned.1.call-start = ((), (), s32[]{:S(2)}) async-start(), calls=%async_computation.23 | async-start | bytes 6684672 | tf_op jit(solution)/shard_map/reduce_scatter | solution.py:267
  1052.0 530.9 %reduce-scatter.18.cloned.1.call-start = ((), (), s32[]{:S(2)}) async-start(), calls=%async_computation.25 | async-start | bytes 6684672 | tf_op jit(solution)/shard_map/reduce_scatter | solution.py:267
  1052.6 692.9 %reduce-scatter.20.cloned.1.call-start = ((), (), s32[]{:S(2)}) async-start(), calls=%async_computation.26 | async-start | bytes 9732096 | tf_op jit(solution)/shard_map/reduce_scatter | solution.py:296
  1063.3 803.0 %reduce-scatter.26.cloned.1.call-start = ((), (), s32[]{:S(2)}) async-start(), calls=%async_computation.29 | async-start | bytes 9732096 | tf_op jit(solution)/shard_map/reduce_scatter | solution.py:299
  1071.0 907.2 %reduce-scatter.22.cloned.1.call-start = ((), (), s32[]{:S(2)}) async-start(), calls=%async_computation.27 | async-start | bytes 4866048 | tf_op jit(solution)/shard_map/reduce_scatter | solution.py:297
  1287.3 804.0 %reduce-scatter.24.cloned.1.call-start = ((), (), s32[]{:S(2)}) async-start(), calls=%async_computation.28 | async-start | bytes 4866048 | tf_op jit(solution)/shard_map/reduce_scatter | solution.py:298
  1588.5 754.2 %reduce-scatter.28.cloned.1.call-start = ((), (), s32[]{:S(2)}) async-start(), calls=%async_computation.30 | async-start | bytes 25952256 | tf_op jit(solution)/shard_map/reduce_scatter | solution.py:300
  1618.1 977.8 %reduce-scatter.30.cloned.1.call-start = ((), (), s32[]{:S(2)}) async-start(), calls=%async_computation.31 | async-start | bytes 25952256 | tf_op jit(solution)/shard_map/reduce_scatter | solution.py:301
  1646.8 1201.1 %reduce-scatter.32.cloned.1.call-start = ((), (), s32[]{:S(2)}) async-start(), calls=%async_computation.32 | async-start | bytes 25952256 | tf_op jit(solution)/shard_map/reduce_scatter | solution.py:302
  (77 other events, 2700.7 us)
Sparse Core Ops, SparseCore 0:
  10.9 59.9 all-gather.11
  73.8 56.1 all-gather.17
  132.9 62.4 all-gather.15
  198.5 75.3 all-gather.29
  277.1 66.3 all-gather.31
  346.6 75.0 all-gather.13
  425.0 66.3 all-gather.19
  494.2 62.0 all-gather.21
  559.2 94.7 all-gather.23
  656.8 94.2 all-gather.25
  753.9 94.2 all-gather.27
  987.2 144.4 reduce-scatter.15
  1137.0 145.1 reduce-scatter.11
  1287.3 145.1 reduce-scatter.13
  1437.6 145.3 reduce-scatter.17
  1589.3 134.6 reduce-scatter.19
  1731.3 134.9 reduce-scatter.25
  1872.2 105.9 reduce-scatter.21
  1985.1 106.0 reduce-scatter.23
  2098.1 244.4 reduce-scatter.27
  2350.8 244.9 reduce-scatter.29
  2602.8 244.9 reduce-scatter.31
where the time goes:
time: 2860 us; the launch traced here: 2850 us
  waiting for transfers between devices  2290 us (80%)
  matrix products  365 us (13%)
  blocking collectives  82.6 us (3%)
  local copies, waits for them, and re-layouts  60.3 us (2%)
  other arithmetic  36 us (1%)
    reduce_scatter x2, waiting for transfers between devices, on_device(): lax.psum_scatter(grad_values, 'blk', scatter_dimension=0, tiled=True)  292 us
    reduce_scatter x1, waiting for transfers between devices, on_device(): lax.psum_scatter(grad_terms[7], ('stream', 'blk'), scatter_dimension=0, t...  253 us
    reduce_scatter x1, waiting for transfers between devices, on_device(): lax.psum_scatter(grad_terms[8], ('stream', 'blk'), scatter_dimension=0, t...  252 us
    reduce_scatter x1, waiting for transfers between devices, on_device(): lax.psum_scatter(grad_terms[6], ('stream', 'blk'), scatter_dimension=0, t...  251 us
    reduce_scatter x2, waiting for transfers between devices, on_device(): lax.psum_scatter(grad_keys, 'blk', scatter_dimension=0, tiled=True)  210 us
    all_gather x2, waiting for transfers between devices, on_device(): value_piece = lax.all_gather(value_low, 'blk', axis=0, tiled=True)  139 us
    reduce_scatter x1, waiting for transfers between devices, on_device(): lax.psum_scatter(grad_terms[5], ('stream', 'blk'), scatter_dimension=0, t...  121 us
    all_gather x2, waiting for transfers between devices, on_device(): key_piece = lax.all_gather(key_rot, 'blk', axis=0, tiled=True)  116 us
  transfers between devices with their start and end apart: 22, of which 21 were waited for; matrix products, arithmetic and copies ran while one was open for 11% of the time, Pallas kernels for 0%

commit v1 on v0

v1 whole, which is shorter than its diff:
```python
import math

import jax
import jax.numpy as jnp
import numpy as np
from jax import lax
from jax.experimental import pallas as pl
from jax.experimental.pallas import tpu as pltpu
from jax.sharding import Mesh
from jax.sharding import PartitionSpec as P

HQ = 16
HK = 8
DH = 96
PLANE = 4
LANES = 128
VMEM_BYTES = 50 * 1024 * 1024

epsilon = 1e-05
rope_base = 100000.0
masked_score = -1e30
score_scale = 1.0 / math.sqrt(DH)
exp2_scale = score_scale * math.log2(math.e)

f32 = jnp.float32
bf16 = jnp.bfloat16


def spread(heads):
    table = np.zeros((heads * DH, heads * LANES), np.float32)
    for head in range(heads):
        for i in range(DH):
            lane = i if i < DH // 2 else i + (LANES - DH) // 2
            table[head * DH + i, head * LANES + lane] = 1.0
    return jnp.asarray(table, bf16)


def rms_scale(values):
    return lax.rsqrt(jnp.mean(values * values, axis=-1, keepdims=True) + epsilon)


def dot(a, b):
    return jnp.dot(a, b, preferred_element_type=f32)


def dot_nt(a, b):
    return lax.dot_general(a, b, (((1,), (1,)), ((), ())), preferred_element_type=f32)


def dot_tn(a, b):
    return lax.dot_general(a, b, (((0,), (0,)), ((), ())), preferred_element_type=f32)


def project_kernel(x_ref, gain_ref, w_ref, cos_ref, sin_ref, e_ref, n_ref, q_ref, kv_ref):
    x = x_ref[...].astype(f32)
    normed = (x * rms_scale(x) * gain_ref[...]).astype(bf16)
    n_ref[...] = normed
    pre = dot(normed, w_ref[...])
    cos, sin = cos_ref[...], sin_ref[...]
    parts = []
    for head in range(8):
        piece = pre[:, head * LANES : (head + 1) * LANES]
        if head < 6:
            piece = piece * cos + pltpu.roll(piece, LANES // 2, 1) * sin
        parts.append(piece.astype(bf16))
    q_ref[...] = jnp.concatenate(parts[:4], axis=1)
    kv_ref[...] = dot_nt(jnp.concatenate(parts[4:], axis=1), e_ref[...]).astype(bf16)


def project(x, gain, w_pad, cos, sin, e4):
    rows, width = x.shape
    step = min(256, rows)
    out_w = w_pad.shape[1]
    whole = lambda a: pl.BlockSpec(a.shape, lambda i: (0,) * a.ndim)
    by_row = lambda c: pl.BlockSpec((step, c), lambda i: (i, 0))
    return pl.pallas_call(
        project_kernel,
        grid=(rows // step,),
        in_specs=[by_row(width), whole(gain), whole(w_pad), by_row(LANES), by_row(LANES), whole(e4)],
        out_specs=[by_row(width), by_row(4 * LANES), by_row(4 * DH)],
        out_shape=[
            jax.ShapeDtypeStruct((rows, width), bf16),
            jax.ShapeDtypeStruct((rows, 4 * LANES), bf16),
            jax.ShapeDtypeStruct((rows, 4 * DH), bf16),
        ],
        compiler_params=pltpu.CompilerParams(vmem_limit_bytes=VMEM_BYTES),
        cost_estimate=pl.CostEstimate(
            flops=2 * rows * width * out_w, bytes_accessed=2 * (2 * rows * width + width * out_w), transcendentals=0
        ),
        name="project",
    )(x, gain, w_pad, cos, sin, e4)


def allowed_of(info_ref, k, chunk, qpos_ref, qbeg_ref, kpos_ref):
    kpos = kpos_ref[...] + (info_ref[0] - k) * chunk
    return (kpos <= qpos_ref[...]) & (kpos >= qbeg_ref[0])


def useful_of(info_ref, m, k, chunk):
    z = info_ref[0]
    return (k <= z) & ((z - k + 1) * chunk - 1 >= info_ref[1 + m])


def stack_heads(block, h):
    return jnp.concatenate(
        [block[:, (2 * h) * LANES : (2 * h + 1) * LANES], block[:, (2 * h + 1) * LANES : (2 * h + 2) * LANES]], axis=0
    )


def attend_kernel(
    info_ref, q_ref, kv_ref, qpos_ref, qbeg_ref, kpos_ref, e_ref, att_ref, low_ref, lse_ref, top_s, acc_s
):
    m, k, last = pl.program_id(0), pl.program_id(1), pl.num_programs(1) - 1
    chunk = kv_ref.shape[2]

    @pl.when(k == 0)
    def _():
        top_s[...] = jnp.full(top_s.shape, masked_score, f32)
        acc_s[...] = jnp.zeros(acc_s.shape, f32)

    @pl.when(useful_of(info_ref, m, k, chunk))
    def _():
        allowed = allowed_of(info_ref, k, chunk, qpos_ref, qbeg_ref, kpos_ref)
        kv = kv_ref[0, 0]
        q = q_ref[0]
        one_lane = (lax.broadcasted_iota(jnp.int32, (1, LANES), 1) == DH // 2).astype(f32)
        for h in range(2):
            keys = dot(kv, e_ref[:, h * LANES : (h + 1) * LANES]).astype(bf16)
            vals = (dot(kv, e_ref[:, (2 + h) * LANES : (3 + h) * LANES]) + one_lane).astype(bf16)
            s = jnp.where(allowed, dot_nt(keys, stack_heads(q, h)), masked_score)
            old = top_s[h]
            new = jnp.maximum(old, jnp.max(s, axis=0, keepdims=True))
            w = jnp.where(allowed, jnp.exp2((s - new) * exp2_scale), 0.0).astype(bf16)
            acc_s[h] = acc_s[h] * jnp.exp2((old - new) * exp2_scale) + dot_tn(vals, w)
            top_s[h] = new

    @pl.when(k == last)
    def _():
        parts = []
        for h in range(2):
            acc = acc_s[h]
            total = acc[DH // 2 : DH // 2 + 1, :]
            lse_ref[0, h] = top_s[h] * exp2_scale + jnp.log2(total)
            flat = (acc / total).T
            rows = flat.shape[0] // 2
            parts += [flat[:rows], flat[rows:]]
        att = jnp.concatenate(parts, axis=1)
        att_ref[0] = att
        low_ref[0] = dot_nt(att.astype(bf16), e_ref[...]).astype(bf16)


def attend(info, q, kv, qpos, qbeg, kpos, e4):
    micro, rows, _ = q.shape
    chunks, _, chunk, width = kv.shape
    return pl.pallas_call(
        attend_kernel,
        grid_spec=pltpu.PrefetchScalarGridSpec(
            num_scalar_prefetch=1,
            grid=(micro, chunks),
            in_specs=[
                pl.BlockSpec((1, rows, 4 * LANES), lambda m, k, i: (m, 0, 0)),
                pl.BlockSpec((1, 1, chunk, width), lambda m, k, i: (k, m, 0, 0)),
                pl.BlockSpec((1, 2 * rows), lambda m, k, i: (0, 0)),
                pl.BlockSpec((1, 1, 2 * rows), lambda m, k, i: (m, 0, 0)),
                pl.BlockSpec((chunk, 1), lambda m, k, i: (0, 0)),
                pl.BlockSpec(e4.shape, lambda m, k, i: (0, 0)),
            ],
            out_specs=[
                pl.BlockSpec((1, rows, 4 * LANES), lambda m, k, i: (m, 0, 0)),
                pl.BlockSpec((1, rows, 4 * DH), lambda m, k, i: (m, 0, 0)),
                pl.BlockSpec((1, 2, 1, 2 * rows), lambda m, k, i: (m, 0, 0, 0)),
            ],
            scratch_shapes=[pltpu.VMEM((2, 1, 2 * rows), f32), pltpu.VMEM((2, LANES, 2 * rows), f32)],
        ),
        out_shape=[
            jax.ShapeDtypeStruct((micro, rows, 4 * LANES), f32),
            jax.ShapeDtypeStruct((micro, rows, 4 * DH), bf16),
            jax.ShapeDtypeStruct((micro, 2, 1, 2 * rows), f32),
        ],
        compiler_params=pltpu.CompilerParams(vmem_limit_bytes=VMEM_BYTES),
        cost_estimate=pl.CostEstimate(
            flops=micro * chunks * 16 * rows * chunk * LANES,
            bytes_accessed=4 * micro * rows * 4 * LANES + 2 * kv.size,
            transcendentals=micro * chunks * 4 * rows * chunk,
        ),
        name="attend",
    )(info, q, kv, qpos, qbeg, kpos, e4)


def attend_back_kernel(
    info_ref, q_ref, kv_ref, g_ref, att_ref, lse_ref, qpos_ref, qbeg_ref, kpos_ref, cos_ref, sin_ref, cosk_ref,
    sink_ref, e_ref, dq_ref, dkv_ref, delta_s, go_s, dq_s,
):
    m, k, last = pl.program_id(0), pl.program_id(1), pl.num_programs(1) - 1
    chunk = kv_ref.shape[2]
    useful = useful_of(info_ref, m, k, chunk)

    @pl.when(k == 0)
    def _():
        dq_s[...] = jnp.zeros(dq_s.shape, f32)
        go = dot(g_ref[0], e_ref[...])
        for h in range(2):
            go_h = stack_heads(go, h)
            go_s[h] = go_h.astype(bf16)
            prod = go_h * stack_heads(att_ref[0], h)
            delta_s[h] = jnp.sum(prod.T, axis=0, keepdims=True)

    @pl.when(useful)
    def _():
        allowed = allowed_of(info_ref, k, chunk, qpos_ref, qbeg_ref, kpos_ref)
        kv = kv_ref[0, 0]
        q = q_ref[0]
        cosk, sink = cosk_ref[0, 0], sink_ref[0, 0]
        grad_keys, grad_vals = [], []
        for h in range(2):
            keys = dot(kv, e_ref[:, h * LANES : (h + 1) * LANES]).astype(bf16)
            vals = dot(kv, e_ref[:, (2 + h) * LANES : (3 + h) * LANES]).astype(bf16)
            q_h = stack_heads(q, h)
            go_h = go_s[h]
            s = dot_nt(keys, q_h)
            w = jnp.where(allowed, jnp.exp2(s * exp2_scale - lse_ref[0, h]), 0.0)
            grad_vals.append(dot(w.astype(bf16), go_h).astype(bf16))
            ds = (w * (dot_nt(vals, go_h) - delta_s[h])).astype(bf16)
            dq_s[h] = dq_s[h] + dot_tn(keys, ds)
            gk = dot(ds, q_h) * score_scale
            gk = gk * cosk + pltpu.roll(gk * sink, LANES // 2, 1)
            grad_keys.append(gk.astype(bf16))
        dkv_ref[0, 0] = dot_nt(jnp.concatenate(grad_keys + grad_vals, axis=1), e_ref[...]).astype(bf16)

    @pl.when(jnp.logical_not(useful))
    def _():
        dkv_ref[...] = jnp.zeros(dkv_ref.shape, bf16)

    @pl.when(k == last)
    def _():
        cos, sin = cos_ref[0, 0], sin_ref[0, 0]
        parts = []
        for h in range(2):
            flat = dq_s[h].T * score_scale
            rows = flat.shape[0] // 2
            for piece in (flat[:rows], flat[rows:]):
                parts.append((piece * cos + pltpu.roll(piece * sin, LANES // 2, 1)).astype(bf16))
        dq_ref[0] = dot_nt(jnp.concatenate(parts, axis=1), e_ref[...]).astype(bf16)


def attend_back(info, q, kv, g, att, lse, qpos, qbeg, kpos, cos, sin, e4):
    micro, rows, _ = q.shape
    chunks, _, chunk, width = kv.shape
    per_micro = lambda c: pl.BlockSpec((1, rows, c), lambda m, k, i: (m, 0, 0))
    return pl.pallas_call(
        attend_back_kernel,
        grid_spec=pltpu.PrefetchScalarGridSpec(
            num_scalar_prefetch=1,
            grid=(micro, chunks),
            in_specs=[
                per_micro(4 * LANES),
                pl.BlockSpec((1, 1, chunk, width), lambda m, k, i: (k, m, 0, 0)),
                per_micro(4 * DH),
                per_micro(4 * LANES),
                pl.BlockSpec((1, 2, 1, 2 * rows), lambda m, k, i: (m, 0, 0, 0)),
                pl.BlockSpec((1, 2 * rows), lambda m, k, i: (0, 0)),
                pl.BlockSpec((1, 1, 2 * rows), lambda m, k, i: (m, 0, 0)),
                pl.BlockSpec((chunk, 1), lambda m, k, i: (0, 0)),
                pl.BlockSpec((1, 1, chunk, LANES), lambda m, k, i: (0, m, 0, 0)),
                pl.BlockSpec((1, 1, chunk, LANES), lambda m, k, i: (0, m, 0, 0)),
                pl.BlockSpec((1, 1, chunk, LANES), lambda m, k, i: (k, m, 0, 0)),
                pl.BlockSpec((1, 1, chunk, LANES), lambda m, k, i: (k, m, 0, 0)),
                pl.BlockSpec(e4.shape, lambda m, k, i: (0, 0)),
            ],
            out_specs=[
                per_micro(4 * DH),
                pl.BlockSpec((1, 1, chunk, width), lambda m, k, i: (k, m, 0, 0)),
            ],
            scratch_shapes=[
                pltpu.VMEM((2, 1, 2 * rows), f32),
                pltpu.VMEM((2, 2 * rows, LANES), bf16),
                pltpu.VMEM((2, LANES, 2 * rows), f32),
            ],
        ),
        out_shape=[
            jax.ShapeDtypeStruct((micro, rows, 4 * DH), bf16),
            jax.ShapeDtypeStruct(kv.shape, bf16),
        ],
        compiler_params=pltpu.CompilerParams(vmem_limit_bytes=VMEM_BYTES),
        cost_estimate=pl.CostEstimate(
            flops=micro * chunks * 40 * rows * chunk * LANES,
            bytes_accessed=8 * micro * rows * 4 * LANES + 4 * kv.size,
            transcendentals=micro * chunks * 4 * rows * chunk,
        ),
        name="attend_back",
    )(info, q, kv, g, att, lse, qpos, qbeg, kpos, cos, sin, cos, sin, e4)


def beside(value, bit):
    return lax.ppermute(value, "plane", [(i, i ^ bit) for i in range(PLANE)])


def other_core(value):
    return lax.ppermute(value, "stream", [(0, 1), (1, 0)])


def along(value, step, wrap):
    size = lax.axis_size("zed")
    pairs = [(i, (i + step) % size) for i in range(size) if wrap or 0 <= i + step < size]
    return lax.ppermute(value, "zed", pairs)


def plane_gather(own):
    first, second = own[0], own[1]
    first = jnp.stack([first, beside(first, 1)])
    second = jnp.stack([second, beside(second, 2)])
    first_more, second_more = beside(first, 2), beside(second, 1)
    return jnp.stack(
        [
            jnp.concatenate([first, first_more]),
            jnp.stack([second[0], second_more[0], second[1], second_more[1]]),
        ]
    )


def plane_sum(terms):
    first, second = terms[0], terms[1]
    got_first = beside(jnp.stack([first[1], first[3]]).astype(bf16), 1)
    got_second = beside(second[2:4].astype(bf16), 2)
    more_first = beside((first[2] + got_first[1]).astype(bf16), 2)
    more_second = beside((second[1] + got_second[1]).astype(bf16), 1)
    return jnp.stack([first[0] + got_first[0] + more_first, second[0] + got_second[0] + more_second])


def weight_gather(blocks):
    size = lax.axis_size("zed")
    s, z = lax.axis_index("stream"), lax.axis_index("zed")
    fulls = []
    for block in blocks:
        full = jnp.zeros((2 * size,) + block.shape, block.dtype)
        for k in range(size):
            place = lax.rem(z - k + size, size)
            full = lax.dynamic_update_slice(full, block[None], (s * size + place, 0, 0))
            full = lax.dynamic_update_slice(full, other_core(block)[None], ((1 - s) * size + place, 0, 0))
            if k < size - 1:
                block = along(block, 1, True)
        fulls.append(full.reshape((-1,) + block.shape[1:]))
    return fulls


def weight_scatter(full, kind):
    size = lax.axis_size("zed")
    s, z = lax.axis_index("stream"), lax.axis_index("zed")
    full = full.reshape((2, size, -1) + full.shape[1:])
    mine = lax.dynamic_index_in_dim(full, s, 0, keepdims=False)
    theirs = lax.dynamic_index_in_dim(full, 1 - s, 0, keepdims=False)
    half = (mine.astype(f32) + other_core(theirs).astype(f32)).astype(kind)
    total = lax.dynamic_index_in_dim(half, lax.rem(z + 1, size), 0, keepdims=False).astype(f32)
    for k in range(size - 2, -1, -1):
        moved = along(total.astype(kind), -1, True).astype(f32)
        total = moved + lax.dynamic_index_in_dim(half, lax.rem(z - k + size, size), 0, keepdims=False).astype(f32)
    return total


def plane_swap(value, split, concat):
    return lax.all_to_all(value, "plane", split_axis=split, concat_axis=concat, tiled=True)


def on_device(inputs, cotangent, seq_lengths, gain_attn, gain_ffn, w_query, w_key, w_value, w_out, w_gate, w_up, w_down):
    size = lax.axis_size("zed")
    z, p = lax.axis_index("zed"), lax.axis_index("plane")
    micro, _, tok_rows, width = inputs.shape
    chunk = PLANE * tok_rows
    tokens = micro * chunk
    shard_rows = w_query.shape[0]
    ff_block = w_down.shape[0]
    ff_blocks = 2 * size
    ff_part = ff_blocks * ff_block
    q_part, kv_part = HQ * DH // PLANE, HK * DH // PLANE
    out_part = width // PLANE
    e4, e8 = spread(4), spread(8)

    def by_part(weight):
        return weight.reshape(shard_rows, PLANE, -1)

    def by_ff_part(weight):
        return weight.reshape(shard_rows, ff_blocks, PLANE, ff_block).transpose(0, 2, 1, 3).reshape(shard_rows, PLANE, -1)

    own_in = inputs[:, 0]
    own_cot = cotangent[:, 0]
    gathered_in = plane_gather(own_in).reshape(tokens, width)
    qkv_bundle = jnp.concatenate([by_part(w_query), by_part(w_key), by_part(w_value)], axis=2).reshape(shard_rows, -1)
    qkv_block = plane_swap(qkv_bundle, 1, 0)
    gains = jnp.stack([gain_attn, gain_ffn])
    gains_one = jnp.stack([gains, beside(gains, 1)])
    gains_all = jnp.concatenate([gains_one, beside(gains_one, 2)])
    gains_all = jnp.take(gains_all, jnp.arange(PLANE) ^ p, axis=0)
    full_qkv, full_gains = weight_gather([qkv_block, gains_all.reshape(PLANE, 2 * shard_rows)])
    full_gains = full_gains.reshape(-1, 2, shard_rows).transpose(1, 0, 2).reshape(2, width).astype(f32)
    gain_one, gain_two = full_gains[0:1], full_gains[1:2]
    ffn_bundle = jnp.concatenate([by_ff_part(w_gate), by_ff_part(w_up), by_part(w_out)], axis=2).reshape(shard_rows, -1)
    ffn_block = plane_swap(ffn_bundle, 1, 0)
    full_gu, full_oc, full_down = weight_gather([ffn_block[:, : 2 * ff_part], ffn_block[:, 2 * ff_part :], w_down])
    full_out = plane_swap(full_oc, 0, 1)
    gathered_cot = plane_gather(own_cot).reshape(tokens, width)

    slot_place = ((jnp.arange(PLANE, dtype=jnp.int32) ^ p)[:, None] * tok_rows + jnp.arange(tok_rows, dtype=jnp.int32)[None, :]).reshape(chunk)
    chunk_place = (z - jnp.arange(size, dtype=jnp.int32))[:, None] * chunk + slot_place[None, :]
    lengths = seq_lengths[:, 0]
    seq_ends = jnp.cumsum(lengths, axis=1)
    begins = jnp.sum(
        jnp.where(seq_ends[:, None, None, :] <= chunk_place[None, :, :, None], lengths[:, None, None, :], 0), axis=-1
    )
    own_begin = begins[:, 0]
    lane = np.arange(LANES)
    place_in_half = lane % (LANES // 2)
    real = place_in_half < DH // 2
    frequency = jnp.where(
        real, rope_base ** (-2.0 * jnp.asarray(np.minimum(place_in_half, DH // 2 - 1), f32) / DH), 0.0
    )
    rope_place = (chunk_place[None] - begins).astype(f32)
    angles = jnp.maximum(rope_place, 0.0).transpose(1, 0, 2)[..., None] * frequency
    cos = jnp.where(real, jnp.cos(angles), 0.0)
    sin = jnp.sin(angles) * jnp.asarray(np.where(real, np.where(lane < LANES // 2, -1.0, 1.0), 0.0), f32)
    info = jnp.concatenate([jnp.reshape(z, (1,)).astype(jnp.int32), jnp.min(own_begin, axis=1)])
    qpos = jnp.tile(chunk_place[0], 2)[None]
    qbeg = jnp.tile(own_begin, (1, 2))[:, None]
    kpos = slot_place[:, None]

    w_pad = dot(full_qkv, e8).astype(bf16)
    normed_one, q_rot, kv_own = project(
        gathered_in, gain_one, w_pad, cos[0].reshape(tokens, LANES), sin[0].reshape(tokens, LANES), e4
    )
    q_rot = q_rot.reshape(micro, chunk, 4 * LANES)
    kv_piece = kv_own.reshape(micro, chunk, 4 * DH)
    kv_pieces = [kv_piece]
    for _ in range(size - 1):
        kv_piece = along(kv_piece, 1, False)
        kv_pieces.append(kv_piece)
    kv_all = jnp.stack(kv_pieces)
    attended, attn_low, lse = attend(info, q_rot, kv_all, qpos, qbeg, kpos, e4)
    attn_low = attn_low.reshape(tokens, q_part)
    branch = plane_sum(dot(attn_low, full_out).reshape(micro, PLANE, tok_rows, width))
    layer_in = own_in.astype(f32)
    middle = layer_in + branch

    scale_two = rms_scale(middle)
    normed_two = plane_gather((middle * scale_two * gain_two).astype(bf16)).reshape(tokens, width)
    pre = dot(normed_two, full_gu)
    gate_pre, up_pre = pre[:, :ff_part], pre[:, ff_part:]
    sigmoid_gate = jax.nn.sigmoid(gate_pre)
    silu_gate = gate_pre * sigmoid_gate
    hidden = (silu_gate * up_pre).astype(bf16)
    grad_hidden = dot_nt(gathered_cot, full_down)
    grad_gate = (grad_hidden * up_pre * sigmoid_gate * (1.0 + gate_pre * (1.0 - sigmoid_gate))).astype(bf16)
    grad_up = (grad_hidden * silu_gate).astype(bf16)
    grad_gu = jnp.concatenate([grad_gate, grad_up], axis=1)
    grad_normed_two = plane_sum(dot_nt(grad_gu, full_gu).reshape(micro, PLANE, tok_rows, width))
    result = middle + plane_sum(dot(hidden, full_down).reshape(micro, PLANE, tok_rows, width))
    output = result.astype(bf16)
    term_gu = dot_tn(normed_two, grad_gu).astype(bf16)
    term_down = dot_tn(hidden, gathered_cot).astype(bf16)

    grad_y = own_cot.astype(f32)
    grad_gain_two = jnp.sum(grad_normed_two * middle * scale_two, axis=(0, 1))
    weighted = grad_normed_two * gain_two
    grad_middle = (
        grad_y
        + scale_two * weighted
        - middle * scale_two**3 * jnp.mean(middle * weighted, axis=-1, keepdims=True)
    )
    grad_branch = plane_gather(grad_middle.astype(bf16)).reshape(tokens, width)
    term_out = plane_swap(dot_tn(attn_low, grad_branch).astype(bf16), 1, 0)
    grad_attn = dot_nt(grad_branch, full_out).astype(bf16).reshape(micro, chunk, q_part)

    grad_query, grad_kv = attend_back(info, q_rot, kv_all, grad_attn, attended, lse, qpos, qbeg, kpos, cos, sin, e4)
    own_kv = grad_kv[size - 1].astype(f32)
    for k in range(size - 2, -1, -1):
        own_kv = along(own_kv.astype(bf16), -1, False).astype(f32) + grad_kv[k].astype(f32)
    grad_qkv = jnp.concatenate([grad_query.reshape(tokens, q_part), own_kv.astype(bf16).reshape(tokens, 2 * kv_part)], axis=1)
    grad_normed_part = dot_nt(grad_qkv, full_qkv)
    full_in = gathered_in.astype(f32)
    grad_gain_one = jnp.sum(grad_normed_part * full_in * rms_scale(full_in), axis=0)
    grad_normed_one = plane_sum(grad_normed_part.reshape(micro, PLANE, tok_rows, width))
    term_qkv = dot_tn(normed_one, grad_qkv).astype(bf16)
    scale_one = rms_scale(layer_in)
    weighted = grad_normed_one * gain_one
    input_grad = (
        grad_middle
        + scale_one * weighted
        - layer_in * scale_one**3 * jnp.mean(layer_in * weighted, axis=-1, keepdims=True)
    )

    def from_parts(term):
        return term.reshape(shard_rows, PLANE, -1)

    def from_ff_parts(term):
        return term.reshape(shard_rows, PLANE, ff_blocks, ff_block).transpose(0, 2, 1, 3).reshape(shard_rows, -1)

    sum_gu = plane_swap(weight_scatter(term_gu, bf16).astype(bf16), 0, 1).astype(f32).reshape(shard_rows, PLANE, 2, ff_part)
    sum_down = weight_scatter(term_down, bf16)
    sum_out = plane_swap(weight_scatter(term_out, bf16).astype(bf16), 0, 1).astype(f32)
    sum_qkv = from_parts(plane_swap(weight_scatter(term_qkv, bf16).astype(bf16), 0, 1).astype(f32))
    gain_terms = jnp.stack([grad_gain_one, grad_gain_two]).reshape(2, ff_blocks, PLANE, shard_rows).transpose(1, 2, 0, 3)
    gain_sum = weight_scatter(gain_terms.reshape(ff_blocks * PLANE, 2 * shard_rows), f32)
    for bit in (1, 2):
        gain_sum = gain_sum + beside(gain_sum, bit)
    gain_own = lax.dynamic_index_in_dim(gain_sum, p, 0, keepdims=False).reshape(2, shard_rows)
    return (
        output[:, None],
        input_grad[:, None],
        gain_own[0],
        gain_own[1],
        sum_qkv[:, :, :q_part].reshape(shard_rows, -1),
        sum_qkv[:, :, q_part : q_part + kv_part].reshape(shard_rows, -1),
        sum_qkv[:, :, q_part + kv_part :].reshape(shard_rows, -1),
        sum_out,
        from_ff_parts(sum_gu[:, :, 0]),
        from_ff_parts(sum_gu[:, :, 1]),
        sum_down,
    )


def solution(mesh):
    blocks = mesh.shape["blk"]
    grid = Mesh(mesh.devices.reshape(2, blocks // PLANE, PLANE), ("stream", "zed", "plane"))
    tokens = P(None, "stream", ("zed", "plane"), None)
    vector = P(("stream", "zed", "plane"))
    matrix = P(("stream", "zed", "plane"), None)
    return jax.shard_map(
        on_device,
        mesh=grid,
        in_specs=(tokens, tokens, P(None, "stream", None), vector, vector) + (matrix,) * 7,
        out_specs=(tokens, tokens, vector, vector) + (matrix,) * 7,
        check_vma=False,
    )
```

time: 2860 us -> 736 us (0.26)
  waiting for transfers between devices: 2290 us -> 286 us
  matrix products: 365 us -> 74.4 us
  starting transfers between devices: 1.46 us -> 173 us
  blocking collectives: 82.6 us -> 0 us
  other arithmetic: 36 us -> 75.8 us
  Pallas kernels: 0 us -> 39.6 us
    reduce_scatter x11 -> x0, waiting for transfers between devices: 1600 us -> none  [the longest x2 292 us: on_device(): lax.psum_scatter(grad_values, 'blk', scatter_dimension=0, tiled=True)]
    all_gather x11 -> x0, waiting for transfers between devices: 682 us -> none  [the longest x2 139 us: on_device(): value_piece = lax.all_gather(value_low, 'blk', axis=0, tiled=True)]
    dot_general x56 -> x12, matrix products: 365 us -> 74.4 us  [the longest x4 32.2 us: dot_nt(): lax.dot_general(a, b, (((1,), (1,)), ((), ())), preferred_element_type=f32)]
    ppermute x0 -> x97, waiting for transfers between devices: none -> 285 us  [the longest x36 155 us: along(): return lax.ppermute(value, 'zed', pairs)]
    ppermute x0 -> x97, starting transfers between devices: none -> 145 us  [the longest x36 102 us: along(): return lax.ppermute(value, 'zed', pairs)]
    unnamed x2 -> x0, blocking collectives: 82.6 us -> none
    pallas_call x0 -> x3, Pallas kernels: none -> 39.6 us  [the longest x1 19.6 us: attend_back(): pl.pallas_call(attend_back_kernel, grid_spec=pltpu.PrefetchScalarGridSpec...]
  transfers between devices with their start and end apart: 22 -> 104, of which waited for: 21 -> 47; matrix products, arithmetic and copies ran while one was open for 11% -> 22% of each run, Pallas kernels for 0% -> 5%
where the time goes in v1:
time: 736 us; the launch traced here: 725 us
  waiting for transfers between devices  286 us (39%)
  starting transfers between devices  173 us (24%)
  other arithmetic  75.8 us (10%)
  matrix products  74.4 us (10%)
  local copies, waits for them, and re-layouts  73.6 us (10%)
  Pallas kernels  39.6 us (5%)
    ppermute x36, waiting for transfers between devices, along(): return lax.ppermute(value, 'zed', pairs)  155 us
    ppermute x36, waiting for transfers between devices, beside(): return lax.ppermute(value, 'plane', [(i, i ^ bit) for i in range(PLANE)])  126 us
    ppermute x36, starting transfers between devices, along(): return lax.ppermute(value, 'zed', pairs)  102 us
    ppermute x36, starting transfers between devices, beside(): return lax.ppermute(value, 'plane', [(i, i ^ bit) for i in range(PLANE)])  42 us
    dot_general x4, matrix products, dot_nt(): lax.dot_general(a, b, (((1,), (1,)), ((), ())), preferred_element_type=f32)  32.2 us
    all_to_all x7, starting transfers between devices, plane_swap(): lax.all_to_all(value, 'plane', split_axis=split, concat_axis=concat, tile...  27.6 us
    dot_general x4, matrix products, dot(): return jnp.dot(a, b, preferred_element_type=f32)  23 us
    pallas_call x1, Pallas kernels, attend_back(): pl.pallas_call(attend_back_kernel, grid_spec=pltpu.PrefetchScalarGridSpec...  19.6 us
  transfers between devices with their start and end apart: 104, of which 47 were waited for; matrix products, arithmetic and copies ran while one was open for 22% of the time, Pallas kernels for 5%

profile of v1, /device:TPU:0, one launch (start us, length us, event | category | flops | bytes accessed | tf_op | source)
XLA Modules:
  0.0 724.7 jit_solution(6958238482903368419)
XLA Ops:
  152.6 8.1 %project.1 = (bf16[1024,1536]{1,0:T(8,128)(2,1)}, bf16[1024,512]{1,0:T(8,128)(2,1)S(1)}, bf16[1024,384]{1,0:T(8,128)(2,1)S(1)}) custom-call(bf16[1024,1536]{1,0:T(8,128)(2,1)} %bitcast.589, f32[1,1536]{1,0:T(1,128)S(1)} %slice.369.gain_ref, bf16[1536,1024]{1,0:T(8,128)(2,1)} %convolution_convert_fusion.1.w_ref, f32[1024,128]{1,0:T(8,128)S(1)} %bitcast.567, ...), custom_call_target="tpu_custom_call" | custom-call | flops 3221225472 | bytes 9437184 | tf_op jit(solution)/shard_map/project/pallas_call | solution.py:76
  160.7 10.5 %collective-permute-done.50 = bf16[128,1536]{1,0:T(8,128)(2,1)} collective-permute-done((bf16[128,1536]{1,0:T(8,128)(2,1)}, bf16[128,1536]{1,0:T(8,128)(2,1)}, u32[]{:S(2)}, u32[]{:S(2)}) %collective-permute-start.50) | collective-permute-done | bytes 393248 | tf_op jit(solution)/shard_map/ppermute | solution.py:305
  177.8 11.1 %collective-permute-done.20 = bf16[2,512,384]{2,1,0:T(8,128)(2,1)S(1)} collective-permute-done((bf16[2,512,384]{2,1,0:T(8,128)(2,1)S(1)}, bf16[2,512,384]{2,1,0:T(8,128)(2,1)S(1)}, u32[]{:S(2)}, u32[]{:S(2)}) %collective-permute-start.20) | collective-permute-done | bytes 786464 | tf_op jit(solution)/shard_map/ppermute | solution.py:305
  221.4 10.2 %collective-permute-done.22 = bf16[2,512,384]{2,1,0:T(8,128)(2,1)} collective-permute-done((bf16[2,512,384]{2,1,0:T(8,128)(2,1)}, bf16[2,512,384]{2,1,0:T(8,128)(2,1)}, u32[]{:S(2)}, u32[]{:S(2)}) %collective-permute-start.22) | collective-permute-done | bytes 786464 | tf_op jit(solution)/shard_map/ppermute | solution.py:305
  234.7 11.9 %attend.1 = (f32[2,512,512]{2,1,0:T(8,128)}, bf16[2,512,384]{2,1,0:T(8,128)(2,1)S(1)}, f32[2,2,1,1024]{3,2,1,0:T(1,128)S(1)}) custom-call(s32[3]{0:T(128)S(1)} %pad_add_fusion.info_ref, bf16[2,512,512]{2,1,0:T(8,128)(2,1)S(1)} %bitcast.570, bf16[4,2,512,384]{3,2,1,0:T(8,128)(2,1)} %pad_maximum_fusion.2.kv_ref, s32[1,1024]{1,0:T(1,128)S(1)} %bitcast.568, ...), custom_call_target="tpu_custom_call" | custom-call | flops 4294967296 | bytes 5242880 | tf_op jit(solution)/shard_map/attend/pallas_call | solution.py:155
  263.9 14.3 %collective-permute-done.32 = bf16[2,128,1536]{2,1,0:T(8,128)(2,1)S(1)} collective-permute-done((bf16[2,128,1536]{2,1,0:T(8,128)(2,1)S(1)}, bf16[2,128,1536]{2,1,0:T(8,128)(2,1)S(1)}, u32[]{:S(2)}, u32[]{:S(2)}) %collective-permute-start.32) | collective-permute-done | bytes 786464 | tf_op jit(solution)/shard_map/ppermute | solution.py:295
  278.2 8.0 %collective-permute-done.31 = bf16[128,1536]{1,0:T(8,128)(2,1)S(1)} collective-permute-done((bf16[128,1536]{1,0:T(8,128)(2,1)S(1)}, bf16[128,1536]{1,0:T(8,128)(2,1)S(1)}, u32[]{:S(2)}, u32[]{:S(2)}) %collective-permute-start.31) | collective-permute-done | bytes 393248 | tf_op jit(solution)/shard_map/ppermute | solution.py:295
  289.3 8.9 %collective-permute-done.33 = bf16[128,1536]{1,0:T(8,128)(2,1)S(1)} collective-permute-done((bf16[128,1536]{1,0:T(8,128)(2,1)S(1)}, bf16[128,1536]{1,0:T(8,128)(2,1)S(1)}, u32[]{:S(2)}, u32[]{:S(2)}) %collective-permute-start.33) | collective-permute-done | bytes 393248 | tf_op jit(solution)/shard_map/ppermute | solution.py:295
  312.1 15.7 %collective-permute-done.37 = bf16[2,128,1536]{2,1,0:T(8,128)(2,1)S(1)} collective-permute-done((bf16[2,128,1536]{2,1,0:T(8,128)(2,1)S(1)}, bf16[2,128,1536]{2,1,0:T(8,128)(2,1)S(1)}, u32[]{:S(2)}, u32[]{:S(2)}) %collective-permute-start.37) | collective-permute-done | bytes 786464 | tf_op jit(solution)/shard_map/ppermute | solution.py:295
  328.6 9.1 %fusion.100 = f32[1024,2048]{1,0:T(8,128)} fusion(bf16[1024,1536]{1,0:T(8,128)(2,1)S(1)} %bitcast.596, bf16[1536,2048]{1,0:T(8,128)(2,1)S(1)} %bitcast.581), kind=kOutput, calls=%fused_computation.323 | convolution fusion | flops 6442450944 | bytes 17825792 | tf_op jit(solution)/shard_map/dot_general | solution.py:43
  337.7 9.6 %multiply_convert_fusion.1 = (bf16[1024,1024]{1,0:T(8,128)(2,1)S(1)}, bf16[1024,1024]{1,0:T(8,128)(2,1)}, bf16[1024,1024]{1,0:T(8,128)(2,1)}) fusion(f32[1024,2048]{1,0:T(8,128)} %fusion.100, bf16[1024,1536]{1,0:T(8,128)(2,1)S(1)} %bitcast.590, bf16[1024,1536]{1,0:T(8,128)(2,1)} %bitcast.102), kind=kOutput, calls=%fused_computation.8 | convolution fusion | flops 3236954112 | bytes 20971520 | tf_op jit(solution)/shard_map/dot_general | solution.py:47
  347.3 9.0 %convolution_convert_fusion = bf16[1536,2048]{1,0:T(8,128)(2,1)S(1)} fusion(bf16[1024,1536]{1,0:T(8,128)(2,1)} %bitcast.597, bf16[1024,1024]{1,0:T(8,128)(2,1)} %get-tuple-element.99, bf16[1024,1024]{1,0:T(8,128)(2,1)S(1)} %get-tuple-element.98), kind=kOutput, calls=%fused_computation.1 | convolution fusion | flops 6453985280 | bytes 13631488 | tf_op jit(solution)/shard_map/dot_general | solution.py:51
  356.3 11.1 %fusion.98 = (bf16[1024,1536]{1,0:T(8,128)(2,1)}, f32[1024,1536]{1,0:T(8,128)}) fusion(bf16[1536,2048]{1,0:T(8,128)(2,1)S(1)} %bitcast.582, bf16[1024,1024]{1,0:T(8,128)(2,1)} %get-tuple-element.99, bf16[1024,1024]{1,0:T(8,128)(2,1)S(1)} %get-tuple-element.98), kind=kOutput, calls=%fused_computation.321 | convolution fusion | flops 6452412416 | bytes 19922944 | tf_op jit(solution)/shard_map/dot_general | solution.py:47
  388.3 10.6 %collective-permute-done.62 = bf16[2,128,1536]{2,1,0:T(8,128)(2,1)S(1)} collective-permute-done((bf16[2,128,1536]{2,1,0:T(8,128)(2,1)S(1)}, bf16[2,128,1536]{2,1,0:T(8,128)(2,1)S(1)}, u32[]{:S(2)}, u32[]{:S(2)}) %collective-permute-start.62) | collective-permute-done | bytes 786464 | tf_op jit(solution)/shard_map/ppermute | solution.py:295
  404.4 12.6 %collective-permute-done.52 = bf16[2,128,1536]{2,1,0:T(8,128)(2,1)S(1)} collective-permute-done((bf16[2,128,1536]{2,1,0:T(8,128)(2,1)S(1)}, bf16[2,128,1536]{2,1,0:T(8,128)(2,1)S(1)}, u32[]{:S(2)}, u32[]{:S(2)}) %collective-permute-start.52) | collective-permute-done | bytes 786464 | tf_op jit(solution)/shard_map/ppermute | solution.py:295
  484.6 19.6 %attend_back.1 = (bf16[2,512,384]{2,1,0:T(8,128)(2,1)S(1)}, bf16[4,2,512,384]{3,2,1,0:T(8,128)(2,1)}) custom-call(s32[3]{0:T(128)S(1)} %pad_add_fusion.info_ref, bf16[2,512,512]{2,1,0:T(8,128)(2,1)S(1)} %bitcast.571, bf16[4,2,512,384]{3,2,1,0:T(8,128)(2,1)} %pad_maximum_fusion.2.kv_ref, bf16[2,512,384]{2,1,0:T(8,128)(2,1)S(1)} %bitcast.574, ...), custom_call_target="tpu_custom_call" | custom-call | flops 10737418240 | bytes 10485760 | tf_op jit(solution)/shard_map/attend_back/pallas_call | solution.py:250
  513.2 11.8 %collective-permute-start.90 = (bf16[192,2048]{1,0:T(8,128)(2,1)S(1)}, bf16[192,2048]{1,0:T(8,128)(2,1)S(1)}, u32[]{:S(2)}, u32[]{:S(2)}) collective-permute-start(bf16[192,2048]{1,0:T(8,128)(2,1)S(1)} %dynamic-slice_bitcast_fusion.3), channel_id=1, source_target_pairs={{0,12},{4,0},{8,4},{12,8},{1,13},{5,1},{9,5},{13,9},{2,14},{6,2},{... | collective-permute-start | bytes 2359304 | tf_op jit(solution)/shard_map/ppermute | solution.py:305
  532.3 11.5 %collective-permute-start.86 = (bf16[192,384]{1,0:T(8,128)(2,1)S(1)}, bf16[192,384]{1,0:T(8,128)(2,1)S(1)}, u32[]{:S(2)}, u32[]{:S(2)}) collective-permute-start(bf16[192,384]{1,0:T(8,128)(2,1)S(1)} %dynamic-slice_bitcast_fusion.7), channel_id=1, source_target_pairs={{0,12},{4,0},{8,4},{12,8},{1,13},{5,1},{9,5},{13,9},{2,14},{6,2},{... | collective-permute-start | bytes 442376 | tf_op jit(solution)/shard_map/ppermute | solution.py:305
  545.9 13.8 %collective-permute-done.86 = bf16[192,384]{1,0:T(8,128)(2,1)S(1)} collective-permute-done((bf16[192,384]{1,0:T(8,128)(2,1)S(1)}, bf16[192,384]{1,0:T(8,128)(2,1)S(1)}, u32[]{:S(2)}, u32[]{:S(2)}) %collective-permute-start.86) | collective-permute-done | bytes 147488 | tf_op jit(solution)/shard_map/ppermute | solution.py:305
  559.7 10.7 %collective-permute-start.87 = (bf16[192,384]{1,0:T(8,128)(2,1)S(1)}, bf16[192,384]{1,0:T(8,128)(2,1)S(1)}, u32[]{:S(2)}, u32[]{:S(2)}) collective-permute-start(bf16[192,384]{1,0:T(8,128)(2,1)S(1)} %fusion.58), channel_id=1, source_target_pairs={{0,12},{4,0},{8,4},{12,8},{1,13},{5,1},{9,5},{13,9},{2,14},{6,2},{... | collective-permute-start | bytes 442376 | tf_op jit(solution)/shard_map/ppermute | solution.py:305
  580.1 17.1 %collective-permute-done.88 = bf16[192,384]{1,0:T(8,128)(2,1)S(1)} collective-permute-done((bf16[192,384]{1,0:T(8,128)(2,1)S(1)}, bf16[192,384]{1,0:T(8,128)(2,1)S(1)}, u32[]{:S(2)}, u32[]{:S(2)}) %collective-permute-start.88) | collective-permute-done | bytes 147488 | tf_op jit(solution)/shard_map/ppermute | solution.py:305
  622.7 11.3 %collective-permute-done.77 = f32[4,96]{1,0:T(4,128)S(1)} collective-permute-done((f32[4,96]{1,0:T(4,128)S(1)}, f32[4,96]{1,0:T(4,128)S(1)}, u32[]{:S(2)}, u32[]{:S(2)}) %collective-permute-start.77) | collective-permute-done | bytes 1568 | tf_op jit(solution)/shard_map/ppermute | solution.py:305
  647.6 15.3 %collective-permute-done.80 = f32[4,96]{1,0:T(4,128)S(1)} collective-permute-done((f32[4,96]{1,0:T(4,128)S(1)}, f32[4,96]{1,0:T(4,128)S(1)}, u32[]{:S(2)}, u32[]{:S(2)}) %collective-permute-start.80) | collective-permute-done | bytes 1568 | tf_op jit(solution)/shard_map/ppermute | solution.py:295
  680.5 8.1 %collective-permute-done.72 = bf16[128,1536]{1,0:T(8,128)(2,1)S(1)} collective-permute-done((bf16[128,1536]{1,0:T(8,128)(2,1)S(1)}, bf16[128,1536]{1,0:T(8,128)(2,1)S(1)}, u32[]{:S(2)}, u32[]{:S(2)}) %collective-permute-start.72) | collective-permute-done | bytes 393248 | tf_op jit(solution)/shard_map/ppermute | solution.py:295
  (558 shorter events, 442.5 us)
Async XLA Ops:
  0.7 70.4 %collective-permute-start.46 = (bf16[128,1536]{1,0:T(8,128)(2,1)}, bf16[128,1536]{1,0:T(8,128)(2,1)}, u32[]{:S(2)}, u32[]{:S(2)}) collective-permute-start(bf16[128,1536]{1,0:T(8,128)(2,1)} %param.28), channel_id=1, source_target_pairs={{0,4},{4,8},{8,12},{12,0},{1,5},{5,9},{9,13},{13,1},{2,6},{6,10},{... | collective-permute-start | bytes 1179656 | tf_op jit(solution)/shard_map/ppermute | solution.py:305
  3.7 63.5 %collective-permute-start.45 = (bf16[128,1536]{1,0:T(8,128)(2,1)}, bf16[128,1536]{1,0:T(8,128)(2,1)}, u32[]{:S(2)}, u32[]{:S(2)}) collective-permute-start(bf16[128,1536]{1,0:T(8,128)(2,1)} %param.28), channel_id=1, source_target_pairs={{0,16},{16,0},{1,17},{17,1},{2,18},{18,2},{3,19},{19,3},{4,20},{20... | collective-permute-start | bytes 1179656 | tf_op jit(solution)/shard_map/ppermute | solution.py:299
  10.0 50.5 %all-to-all-start = ((bf16[48,4,768]{2,0,1:T(8,128)(2,1)}), bf16[48,4,768]{2,0,1:T(8,128)(2,1)}, u32[]{:S(2)}, u32[]{:S(2)}) async-start(bf16[48,4,768]{2,0,1:T(8,128)(2,1)} %copy.115), calls=%async_computation | async-start | bytes 589824 | tf_op jit(solution)/shard_map/all_to_all | solution.py:361
  15.1 57.8 %collective-permute-start.56 = (bf16[128,1536]{1,0:T(8,128)(2,1)}, bf16[128,1536]{1,0:T(8,128)(2,1)}, u32[]{:S(2)}, u32[]{:S(2)}) collective-permute-start(bf16[128,1536]{1,0:T(8,128)(2,1)} %get-tuple-element.143), channel_id=1, source_target_pairs={{0,1},{1,0},{2,3},{3,2},{4,5},{5,4},{6,7},{7,6},{8,9},{9,8},{10,11... | collective-permute-start | bytes 1179656 | tf_op jit(solution)/shard_map/ppermute | solution.py:295
  74.9 125.4 %collective-permute-start.57 = (bf16[2,128,1536]{2,1,0:T(8,128)(2,1)}, bf16[2,128,1536]{2,1,0:T(8,128)(2,1)}, u32[]{:S(2)}, u32[]{:S(2)}) collective-permute-start(bf16[2,128,1536]{2,1,0:T(8,128)(2,1)} %pad_maximum_fusion.19), channel_id=1, source_target_pairs={{0,2},{1,3},{2,0},{3,1},{4,6},{5,7},{6,4},{7,5},{8,10},{9,11},{10,... | collective-permute-start | bytes 2359304 | tf_op jit(solution)/shard_map/ppermute | solution.py:295
  76.9 97.4 %collective-permute-start.59 = (bf16[2,128,1536]{2,1,0:T(8,128)(2,1)}, bf16[2,128,1536]{2,1,0:T(8,128)(2,1)}, u32[]{:S(2)}, u32[]{:S(2)}) collective-permute-start(bf16[2,128,1536]{2,1,0:T(8,128)(2,1)} %pad_maximum_fusion.20), channel_id=1, source_target_pairs={{0,1},{1,0},{2,3},{3,2},{4,5},{5,4},{6,7},{7,6},{8,9},{9,8},{10,11... | collective-permute-start | bytes 2359304 | tf_op jit(solution)/shard_map/ppermute | solution.py:295
  86.2 54.9 %collective-permute-start.1 = (bf16[2,128,1536]{2,1,0:T(8,128)(2,1)S(1)}, bf16[2,128,1536]{2,1,0:T(8,128)(2,1)}, u32[]{:S(2)}, u32[]{:S(2)}) collective-permute-start(bf16[2,128,1536]{2,1,0:T(8,128)(2,1)S(1)} %pad_maximum_fusion.13), channel_id=1, source_target_pairs={{0,2},{1,3},{2,0},{3,1},{4,6},{5,7},{6,4},{7,5},{8,10},{9,11},{10,... | collective-permute-start | bytes 2359304 | tf_op jit(solution)/shard_map/ppermute | solution.py:295
  140.2 76.7 %collective-permute-start.38 = (bf16[192,2048]{1,0:T(8,128)(2,1)}, bf16[192,2048]{1,0:T(8,128)(2,1)}, u32[]{:S(2)}, u32[]{:S(2)}) collective-permute-start(bf16[192,2048]{1,0:T(8,128)(2,1)} %slice.481), channel_id=1, source_target_pairs={{0,16},{16,0},{1,17},{17,1},{2,18},{18,2},{3,19},{19,3},{4,20},{20... | collective-permute-start | bytes 2359304 | tf_op jit(solution)/shard_map/ppermute | solution.py:299
  141.1 75.0 %collective-permute-start.39 = (bf16[192,2048]{1,0:T(8,128)(2,1)}, bf16[192,2048]{1,0:T(8,128)(2,1)}, u32[]{:S(2)}, u32[]{:S(2)}) collective-permute-start(bf16[192,2048]{1,0:T(8,128)(2,1)} %slice.481), channel_id=1, source_target_pairs={{0,4},{4,8},{8,12},{12,0},{1,5},{5,9},{9,13},{13,1},{2,6},{6,10},{... | collective-permute-start | bytes 2359304 | tf_op jit(solution)/shard_map/ppermute | solution.py:305
  194.9 56.4 %collective-permute-start.51 = (bf16[128,1536]{1,0:T(8,128)(2,1)}, bf16[128,1536]{1,0:T(8,128)(2,1)}, u32[]{:S(2)}, u32[]{:S(2)}) collective-permute-start(bf16[128,1536]{1,0:T(8,128)(2,1)} %collective-permute-done.50), channel_id=1, source_target_pairs={{0,16},{16,0},{1,17},{17,1},{2,18},{18,2},{3,19},{19,3},{4,20},{20... | collective-permute-start | bytes 1179656 | tf_op jit(solution)/shard_map/ppermute | solution.py:299
  216.2 37.0 %collective-permute-start.41 = (bf16[192,2048]{1,0:T(8,128)(2,1)}, bf16[192,2048]{1,0:T(8,128)(2,1)}, u32[]{:S(2)}, u32[]{:S(2)}) collective-permute-start(bf16[192,2048]{1,0:T(8,128)(2,1)} %collective-permute-done.39), channel_id=1, source_target_pairs={{0,4},{4,8},{8,12},{12,0},{1,5},{5,9},{9,13},{13,1},{2,6},{6,10},{... | collective-permute-start | bytes 2359304 | tf_op jit(solution)/shard_map/ppermute | solution.py:305
  216.9 45.9 %collective-permute-start.40 = (bf16[192,2048]{1,0:T(8,128)(2,1)}, bf16[192,2048]{1,0:T(8,128)(2,1)}, u32[]{:S(2)}, u32[]{:S(2)}) collective-permute-start(bf16[192,2048]{1,0:T(8,128)(2,1)} %collective-permute-done.39), channel_id=1, source_target_pairs={{0,16},{16,0},{1,17},{17,1},{2,18},{18,2},{3,19},{19,3},{4,20},{20... | collective-permute-start | bytes 2359304 | tf_op jit(solution)/shard_map/ppermute | solution.py:299
  253.1 36.1 %collective-permute-start.43 = (bf16[192,2048]{1,0:T(8,128)(2,1)}, bf16[192,2048]{1,0:T(8,128)(2,1)S(1)}, u32[]{:S(2)}, u32[]{:S(2)}) collective-permute-start(bf16[192,2048]{1,0:T(8,128)(2,1)} %collective-permute-done.41), channel_id=1, source_target_pairs={{0,4},{4,8},{8,12},{12,0},{1,5},{5,9},{9,13},{13,1},{2,6},{6,10},{... | collective-permute-start | bytes 2359304 | tf_op jit(solution)/shard_map/ppermute | solution.py:305
  257.8 43.4 %collective-permute-start.42 = (bf16[192,2048]{1,0:T(8,128)(2,1)}, bf16[192,2048]{1,0:T(8,128)(2,1)S(1)}, u32[]{:S(2)}, u32[]{:S(2)}) collective-permute-start(bf16[192,2048]{1,0:T(8,128)(2,1)} %collective-permute-done.41), channel_id=1, source_target_pairs={{0,16},{16,0},{1,17},{17,1},{2,18},{18,2},{3,19},{19,3},{4,20},{20... | collective-permute-start | bytes 2359304 | tf_op jit(solution)/shard_map/ppermute | solution.py:299
  385.3 54.8 %collective-permute-start.93 = (bf16[4,128,1536]{2,1,0:T(8,128)(2,1)}, bf16[4,128,1536]{2,1,0:T(8,128)(2,1)}, u32[]{:S(2)}, u32[]{:S(2)}) collective-permute-start(bf16[4,128,1536]{2,1,0:T(8,128)(2,1)} %dynamic-slice_bitcast_fusion.1), channel_id=1, source_target_pairs={{0,16},{16,0},{1,17},{17,1},{2,18},{18,2},{3,19},{19,3},{4,20},{20... | collective-permute-start | bytes 4718600 | tf_op jit(solution)/shard_map/ppermute | solution.py:299
  388.1 120.6 %collective-permute-start.89 = (bf16[4,192,2048]{2,1,0:T(8,128)(2,1)}, bf16[4,192,2048]{2,1,0:T(8,128)(2,1)}, u32[]{:S(2)}, u32[]{:S(2)}) collective-permute-start(bf16[4,192,2048]{2,1,0:T(8,128)(2,1)} %dynamic-slice_bitcast_fusion), channel_id=1, source_target_pairs={{0,16},{16,0},{1,17},{17,1},{2,18},{18,2},{3,19},{19,3},{4,20},{20... | collective-permute-start | bytes 9437192 | tf_op jit(solution)/shard_map/ppermute | solution.py:299
  399.0 34.0 %collective-permute-start.54 = (bf16[2,128,1536]{2,1,0:T(8,128)(2,1)}, bf16[2,128,1536]{2,1,0:T(8,128)(2,1)}, u32[]{:S(2)}, u32[]{:S(2)}) collective-permute-start(bf16[2,128,1536]{2,1,0:T(8,128)(2,1)} %bitcast.108), channel_id=1, source_target_pairs={{0,2},{1,3},{2,0},{3,1},{4,6},{5,7},{6,4},{7,5},{8,10},{9,11},{10,... | collective-permute-start | bytes 2359304 | tf_op jit(solution)/shard_map/ppermute | solution.py:295
  468.1 75.7 %collective-permute-start.96 = (bf16[128,1536]{1,0:T(8,128)(2,1)}, bf16[128,1536]{1,0:T(8,128)(2,1)}, u32[]{:S(2)}, u32[]{:S(2)}) collective-permute-start(bf16[128,1536]{1,0:T(8,128)(2,1)} %fusion.51), channel_id=1, source_target_pairs={{0,12},{4,0},{8,4},{12,8},{1,13},{5,1},{9,5},{13,9},{2,14},{6,2},{... | collective-permute-start | bytes 1179656 | tf_op jit(solution)/shard_map/ppermute | solution.py:305
  513.2 65.7 %collective-permute-start.90 = (bf16[192,2048]{1,0:T(8,128)(2,1)S(1)}, bf16[192,2048]{1,0:T(8,128)(2,1)S(1)}, u32[]{:S(2)}, u32[]{:S(2)}) collective-permute-start(bf16[192,2048]{1,0:T(8,128)(2,1)S(1)} %dynamic-slice_bitcast_fusion.3), channel_id=1, source_target_pairs={{0,12},{4,0},{8,4},{12,8},{1,13},{5,1},{9,5},{13,9},{2,14},{6,2},{... | collective-permute-start | bytes 2359304 | tf_op jit(solution)/shard_map/ppermute | solution.py:305
  529.7 40.6 %collective-permute-start.69 = (bf16[2,512,384]{2,1,0:T(8,128)(2,1)S(1)}, bf16[2,512,384]{2,1,0:T(8,128)(2,1)S(1)}, u32[]{:S(2)}, u32[]{:S(2)}) collective-permute-start(bf16[2,512,384]{2,1,0:T(8,128)(2,1)S(1)} %fusion.29), channel_id=1, source_target_pairs={{4,0},{8,4},{12,8},{5,1},{9,5},{13,9},{6,2},{10,6},{14,10},{7,3},{... | collective-permute-start | bytes 2359304 | tf_op jit(solution)/shard_map/ppermute | solution.py:305
  579.2 33.4 %collective-permute-start.91 = (bf16[192,2048]{1,0:T(8,128)(2,1)S(1)}, bf16[192,2048]{1,0:T(8,128)(2,1)}, u32[]{:S(2)}, u32[]{:S(2)}) collective-permute-start(bf16[192,2048]{1,0:T(8,128)(2,1)S(1)} %fusion.26), channel_id=1, source_target_pairs={{0,12},{4,0},{8,4},{12,8},{1,13},{5,1},{9,5},{13,9},{2,14},{6,2},{... | collective-permute-start | bytes 2359304 | tf_op jit(solution)/shard_map/ppermute | solution.py:305
  614.3 49.1 %collective-permute-start.92 = (bf16[192,2048]{1,0:T(8,128)(2,1)S(1)}, bf16[192,2048]{1,0:T(8,128)(2,1)S(1)}, u32[]{:S(2)}, u32[]{:S(2)}) collective-permute-start(bf16[192,2048]{1,0:T(8,128)(2,1)S(1)} %fusion.25), channel_id=1, source_target_pairs={{0,12},{4,0},{8,4},{12,8},{1,13},{5,1},{9,5},{13,9},{2,14},{6,2},{... | collective-permute-start | bytes 2359304 | tf_op jit(solution)/shard_map/ppermute | solution.py:305
  642.6 32.1 %collective-permute-start.81 = (bf16[4,192,768]{2,1,0:T(8,128)(2,1)S(1)}, bf16[4,192,768]{2,1,0:T(8,128)(2,1)}, u32[]{:S(2)}, u32[]{:S(2)}) collective-permute-start(bf16[4,192,768]{2,1,0:T(8,128)(2,1)S(1)} %dynamic-slice_bitcast_fusion.2), channel_id=1, source_target_pairs={{0,16},{16,0},{1,17},{17,1},{2,18},{18,2},{3,19},{19,3},{4,20},{20... | collective-permute-start | bytes 3538952 | tf_op jit(solution)/shard_map/ppermute | solution.py:299
  665.8 40.2 %all-to-all-start.6 = ((bf16[4,48,2048]{2,1,0:T(8,128)(2,1)}), bf16[4,48,2048]{2,1,0:T(8,128)(2,1)S(1)}, u32[]{:S(2)}, u32[]{:S(2)}) async-start(bf16[4,48,2048]{2,1,0:T(8,128)(2,1)} %bitcast.200), calls=%async_computation.6 | async-start | bytes 1572864 | tf_op jit(solution)/shard_map/all_to_all | solution.py:361
  (148 other events, 2293.4 us)

commit v2 on v1

--- a/solution.py
+++ b/solution.py
@@ -327,34 +327,46 @@
     return jnp.stack([first[0] + got_first[0] + more_first, second[0] + got_second[0] + more_second])
 
 
+def after(value, *earlier):
+    return lax.optimization_barrier((value,) + earlier)[0]
+
+
 def weight_gather(blocks):
     size = lax.axis_size("zed")
     s, z = lax.axis_index("stream"), lax.axis_index("zed")
-    fulls = []
-    for block in blocks:
-        full = jnp.zeros((2 * size,) + block.shape, block.dtype)
-        for k in range(size):
-            place = lax.rem(z - k + size, size)
-            full = lax.dynamic_update_slice(full, block[None], (s * size + place, 0, 0))
-            full = lax.dynamic_update_slice(full, other_core(block)[None], ((1 - s) * size + place, 0, 0))
-            if k < size - 1:
-                block = along(block, 1, True)
-        fulls.append(full.reshape((-1,) + block.shape[1:]))
-    return fulls
-
-
-def weight_scatter(full, kind):
+    fulls = [jnp.zeros((2 * size,) + block.shape, block.dtype) for block in blocks]
+    for k in range(size):
+        place = lax.rem(z - k + size, size)
+        for i, block in enumerate(blocks):
+            full = lax.dynamic_update_slice(fulls[i], block[None], (s * size + place, 0, 0))
+            fulls[i] = lax.dynamic_update_slice(full, other_core(block)[None], ((1 - s) * size + place, 0, 0))
+        if k < size - 1:
+            blocks = lax.optimization_barrier([along(block, 1, True) for block in blocks])
+    return [full.reshape((-1,) + full.shape[2:]) for full in fulls], blocks[0]
+
+
+def core_scatter(fulls, kinds):
     size = lax.axis_size("zed")
-    s, z = lax.axis_index("stream"), lax.axis_index("zed")
-    full = full.reshape((2, size, -1) + full.shape[1:])
-    mine = lax.dynamic_index_in_dim(full, s, 0, keepdims=False)
-    theirs = lax.dynamic_index_in_dim(full, 1 - s, 0, keepdims=False)
-    half = (mine.astype(f32) + other_core(theirs).astype(f32)).astype(kind)
-    total = lax.dynamic_index_in_dim(half, lax.rem(z + 1, size), 0, keepdims=False).astype(f32)
-    for k in range(size - 2, -1, -1):
-        moved = along(total.astype(kind), -1, True).astype(f32)
-        total = moved + lax.dynamic_index_in_dim(half, lax.rem(z - k + size, size), 0, keepdims=False).astype(f32)
-    return total
+    s = lax.axis_index("stream")
+    halves = []
+    for full, kind in zip(fulls, kinds):
+        full = full.reshape((2, size, -1) + full.shape[1:])
+        mine = lax.dynamic_index_in_dim(full, s, 0, keepdims=False)
+        theirs = lax.dynamic_index_in_dim(full, 1 - s, 0, keepdims=False)
+        halves.append((mine.astype(f32) + other_core(theirs).astype(f32)).astype(kind))
+    return lax.optimization_barrier(halves)
+
+
+def ring_scatter(halves, totals, k):
+    size = lax.axis_size("zed")
+    z = lax.axis_index("zed")
+    new = []
+    for i, half in enumerate(halves):
+        own = lax.dynamic_index_in_dim(half, lax.rem(z - k + size, size), 0, keepdims=False).astype(f32)
+        if totals is not None:
+            own = along(totals[i], -1, True).astype(f32) + own
+        new.append(own if k == 0 else own.astype(half.dtype))
+    return lax.optimization_barrier(new)
 
 
 def plane_swap(value, split, concat):
@@ -383,21 +395,21 @@
 
     own_in = inputs[:, 0]
     own_cot = cotangent[:, 0]
-    gathered_in = plane_gather(own_in).reshape(tokens, width)
     qkv_bundle = jnp.concatenate([by_part(w_query), by_part(w_key), by_part(w_value)], axis=2).reshape(shard_rows, -1)
     qkv_block = plane_swap(qkv_bundle, 1, 0)
     gains = jnp.stack([gain_attn, gain_ffn])
     gains_one = jnp.stack([gains, beside(gains, 1)])
     gains_all = jnp.concatenate([gains_one, beside(gains_one, 2)])
     gains_all = jnp.take(gains_all, jnp.arange(PLANE) ^ p, axis=0)
-    full_qkv, full_gains = weight_gather([qkv_block, gains_all.reshape(PLANE, 2 * shard_rows)])
+    (full_qkv, full_gains), qkv_there = weight_gather([qkv_block, gains_all.reshape(PLANE, 2 * shard_rows)])
     full_gains = full_gains.reshape(-1, 2, shard_rows).transpose(1, 0, 2).reshape(2, width).astype(f32)
     gain_one, gain_two = full_gains[0:1], full_gains[1:2]
     ffn_bundle = jnp.concatenate([by_ff_part(w_gate), by_ff_part(w_up), by_part(w_out)], axis=2).reshape(shard_rows, -1)
-    ffn_block = plane_swap(ffn_bundle, 1, 0)
-    full_gu, full_oc, full_down = weight_gather([ffn_block[:, : 2 * ff_part], ffn_block[:, 2 * ff_part :], w_down])
+    ffn_block = plane_swap(after(ffn_bundle, qkv_block), 1, 0)
+    gathered_in = plane_gather(after(own_in, qkv_block)).reshape(tokens, width)
+    (full_oc,), out_there = weight_gather([after(ffn_block[:, 2 * ff_part :], qkv_there)])
     full_out = plane_swap(full_oc, 0, 1)
-    gathered_cot = plane_gather(own_cot).reshape(tokens, width)
+    gathered_cot = plane_gather(after(own_cot, gathered_in)).reshape(tokens, width)
 
     slot_place = ((jnp.arange(PLANE, dtype=jnp.int32) ^ p)[:, None] * tok_rows + jnp.arange(tok_rows, dtype=jnp.int32)[None, :]).reshape(chunk)
     chunk_place = (z - jnp.arange(size, dtype=jnp.int32))[:, None] * chunk + slot_place[None, :]
@@ -427,12 +439,14 @@
         gathered_in, gain_one, w_pad, cos[0].reshape(tokens, LANES), sin[0].reshape(tokens, LANES), e4
     )
     q_rot = q_rot.reshape(micro, chunk, 4 * LANES)
-    kv_piece = kv_own.reshape(micro, chunk, 4 * DH)
+    kv_piece = after(kv_own.reshape(micro, chunk, 4 * DH), out_there)
     kv_pieces = [kv_piece]
     for _ in range(size - 1):
         kv_piece = along(kv_piece, 1, False)
         kv_pieces.append(kv_piece)
     kv_all = jnp.stack(kv_pieces)
+    gu_block, down_block = lax.optimization_barrier((ffn_block[:, : 2 * ff_part], w_down, kv_piece))[:2]
+    (full_gu, full_down), _ = weight_gather([gu_block, down_block])
     attended, attn_low, lse = attend(info, q_rot, kv_all, qpos, qbeg, kpos, e4)
     attn_low = attn_low.reshape(tokens, q_part)
     branch = plane_sum(dot(attn_low, full_out).reshape(micro, PLANE, tok_rows, width))
@@ -451,10 +465,11 @@
     grad_up = (grad_hidden * silu_gate).astype(bf16)
     grad_gu = jnp.concatenate([grad_gate, grad_up], axis=1)
     grad_normed_two = plane_sum(dot_nt(grad_gu, full_gu).reshape(micro, PLANE, tok_rows, width))
-    result = middle + plane_sum(dot(hidden, full_down).reshape(micro, PLANE, tok_rows, width))
-    output = result.astype(bf16)
     term_gu = dot_tn(normed_two, grad_gu).astype(bf16)
     term_down = dot_tn(hidden, gathered_cot).astype(bf16)
+    ffn_halves = core_scatter([term_gu, term_down], [bf16, bf16])
+    ffn_totals = ring_scatter(ffn_halves, None, size - 1)
+    result_terms = dot(hidden, full_down)
 
     grad_y = own_cot.astype(f32)
     grad_gain_two = jnp.sum(grad_normed_two * middle * scale_two, axis=(0, 1))
@@ -466,12 +481,21 @@
     )
     grad_branch = plane_gather(grad_middle.astype(bf16)).reshape(tokens, width)
     term_out = plane_swap(dot_tn(attn_low, grad_branch).astype(bf16), 1, 0)
-    grad_attn = dot_nt(grad_branch, full_out).astype(bf16).reshape(micro, chunk, q_part)
+    ffn_totals = ring_scatter(ffn_halves, ffn_totals, size - 2)
+    grad_attn = after(dot_nt(grad_branch, full_out).astype(bf16), ffn_totals[0]).reshape(micro, chunk, q_part)
 
     grad_query, grad_kv = attend_back(info, q_rot, kv_all, grad_attn, attended, lse, qpos, qbeg, kpos, cos, sin, e4)
-    own_kv = grad_kv[size - 1].astype(f32)
+    result_terms = after(result_terms, grad_query)
+    result = middle + plane_sum(result_terms.reshape(micro, PLANE, tok_rows, width))
+    output = result.astype(bf16)
+    own_kv = grad_kv[size - 1]
     for k in range(size - 2, -1, -1):
-        own_kv = along(own_kv.astype(bf16), -1, False).astype(f32) + grad_kv[k].astype(f32)
+        if k > 0:
+            ffn_totals = ring_scatter(ffn_halves, ffn_totals, k - 1)
+            own_kv = after(own_kv, ffn_totals[0])
+        own_kv = along(own_kv, -1, False).astype(f32) + grad_kv[k].astype(f32)
+        own_kv = own_kv.astype(bf16)
+    sum_gu, sum_down = ffn_totals
     grad_qkv = jnp.concatenate([grad_query.reshape(tokens, q_part), own_kv.astype(bf16).reshape(tokens, 2 * kv_part)], axis=1)
     grad_normed_part = dot_nt(grad_qkv, full_qkv)
     full_in = gathered_in.astype(f32)
@@ -486,18 +510,19 @@
         - layer_in * scale_one**3 * jnp.mean(layer_in * weighted, axis=-1, keepdims=True)
     )
 
-    def from_parts(term):
-        return term.reshape(shard_rows, PLANE, -1)
-
     def from_ff_parts(term):
         return term.reshape(shard_rows, PLANE, ff_blocks, ff_block).transpose(0, 2, 1, 3).reshape(shard_rows, -1)
 
-    sum_gu = plane_swap(weight_scatter(term_gu, bf16).astype(bf16), 0, 1).astype(f32).reshape(shard_rows, PLANE, 2, ff_part)
-    sum_down = weight_scatter(term_down, bf16)
-    sum_out = plane_swap(weight_scatter(term_out, bf16).astype(bf16), 0, 1).astype(f32)
-    sum_qkv = from_parts(plane_swap(weight_scatter(term_qkv, bf16).astype(bf16), 0, 1).astype(f32))
+    sum_gu = plane_swap(sum_gu.astype(bf16), 0, 1).astype(f32).reshape(shard_rows, PLANE, 2, ff_part)
     gain_terms = jnp.stack([grad_gain_one, grad_gain_two]).reshape(2, ff_blocks, PLANE, shard_rows).transpose(1, 2, 0, 3)
-    gain_sum = weight_scatter(gain_terms.reshape(ff_blocks * PLANE, 2 * shard_rows), f32)
+    gain_terms = gain_terms.reshape(ff_blocks * PLANE, 2 * shard_rows)
+    last_halves = core_scatter([term_qkv, term_out, gain_terms], [bf16, bf16, f32])
+    last_totals = None
+    for k in range(size - 1, -1, -1):
+        last_totals = ring_scatter(last_halves, last_totals, k)
+    sum_qkv, sum_out, gain_sum = last_totals
+    sum_qkv, sum_out = lax.optimization_barrier((sum_qkv.astype(bf16), sum_out.astype(bf16)))
+    sum_qkv = plane_swap(jnp.concatenate([sum_qkv, sum_out], axis=1), 0, 1).astype(f32).reshape(shard_rows, PLANE, -1)
     for bit in (1, 2):
         gain_sum = gain_sum + beside(gain_sum, bit)
     gain_own = lax.dynamic_index_in_dim(gain_sum, p, 0, keepdims=False).reshape(2, shard_rows)
@@ -508,8 +533,8 @@
         gain_own[1],
         sum_qkv[:, :, :q_part].reshape(shard_rows, -1),
         sum_qkv[:, :, q_part : q_part + kv_part].reshape(shard_rows, -1),
-        sum_qkv[:, :, q_part + kv_part :].reshape(shard_rows, -1),
-        sum_out,
+        sum_qkv[:, :, q_part + kv_part : q_part + 2 * kv_part].reshape(shard_rows, -1),
+        sum_qkv[:, :, q_part + 2 * kv_part :].reshape(shard_rows, -1),
         from_ff_parts(sum_gu[:, :, 0]),
         from_ff_parts(sum_gu[:, :, 1]),
         sum_down,

time: 736 us -> 661 us (0.90)
  waiting for transfers between devices: 286 us -> 243 us
  starting transfers between devices: 173 us -> 148 us
    ppermute x36, waiting for transfers between devices: 126 us -> 74.3 us  [beside(): return lax.ppermute(value, 'plane', [(i, i ^ bit) for i in range(PLANE)])]
    ppermute x36, starting transfers between devices: 102 us -> 82.1 us  [along(): return lax.ppermute(value, 'zed', pairs)]
    all_to_all x7 -> x6, starting transfers between devices: 27.6 us -> 24.9 us  [plane_swap(): lax.all_to_all(value, 'plane', split_axis=split, concat_axis=concat, tile...]
    convert_element_type x20 -> x18, other arithmetic: 21.8 us -> 23.3 us  [the longest x4 9.67 us: core_scatter(): (mine.astype(f32) + other_core(theirs).astype(f32)).astype(kind)]
  transfers between devices with their start and end apart: 104 -> 103, of which waited for: 47 -> 42; matrix products, arithmetic and copies ran while one was open for 22% -> 24% of each run, Pallas kernels for 5% -> 6%
where the time goes in v2:
time: 661 us; the launch traced here: 653 us
  waiting for transfers between devices  243 us (37%)
  starting transfers between devices  148 us (22%)
  other arithmetic  75.8 us (11%)
  local copies, waits for them, and re-layouts  72.7 us (11%)
  matrix products  72 us (11%)
  Pallas kernels  39.4 us (6%)
    ppermute x36, waiting for transfers between devices, along(): return lax.ppermute(value, 'zed', pairs)  159 us
    ppermute x36, starting transfers between devices, along(): return lax.ppermute(value, 'zed', pairs)  82.1 us
    ppermute x36, waiting for transfers between devices, beside(): return lax.ppermute(value, 'plane', [(i, i ^ bit) for i in range(PLANE)])  74.3 us
    ppermute x36, starting transfers between devices, beside(): return lax.ppermute(value, 'plane', [(i, i ^ bit) for i in range(PLANE)])  37.4 us
    dot_general x4, matrix products, dot_nt(): lax.dot_general(a, b, (((1,), (1,)), ((), ())), preferred_element_type=f32)  28.7 us
    all_to_all x6, starting transfers between devices, plane_swap(): lax.all_to_all(value, 'plane', split_axis=split, concat_axis=concat, tile...  24.9 us
    dot_general x4, matrix products, dot(): return jnp.dot(a, b, preferred_element_type=f32)  22.3 us
    dot_general x4, matrix products, dot_tn(): lax.dot_general(a, b, (((0,), (0,)), ((), ())), preferred_element_type=f32)  20.9 us
  transfers between devices with their start and end apart: 103, of which 42 were waited for; matrix products, arithmetic and copies ran while one was open for 24% of the time, Pallas kernels for 6%

profile of v2, /device:TPU:0, one launch (start us, length us, event | category | flops | bytes accessed | tf_op | source)
XLA Modules:
  0.0 653.4 jit_solution(8901289344886609056)
XLA Ops:
  12.7 7.4 %fusion.6 = (f32[4,2,512,128]{3,2,1,0:T(8,128)S(1)}, f32[4,2,512,128]{3,2,1,0:T(8,128)S(1)}) fusion(f32[128]{0:T(128)S(1)} %copy-done.52, f32[128]{0:T(128)S(1)} %copy-done.53, f32[4,2,512]{2,1,0:T(2,128)S(1)} %copy.75, pred[128]{0:T(512)(128)(4,1)S(1)} %copy-done.51), kind=kLoop, calls=%fused_computation.33 | loop fusion | flops 1572864 | bytes 4211840 | tf_op jit(solution)/shard_map/mul | solution.py:431
  97.4 8.1 %project.1 = (bf16[1024,1536]{1,0:T(8,128)(2,1)}, bf16[1024,512]{1,0:T(8,128)(2,1)S(1)}, bf16[1024,384]{1,0:T(8,128)(2,1)S(1)}) custom-call(bf16[1024,1536]{1,0:T(8,128)(2,1)} %bitcast.533, f32[1,1536]{1,0:T(1,128)S(1)} %slice.358.gain_ref, bf16[1536,1024]{1,0:T(8,128)(2,1)} %convolution_convert_fusion.1.w_ref, f32[1024,128]{1,0:T(8,128)S(1)} %bitcast.507, ...), custom_call_target="tpu_custom_call" | custom-call | flops 3221225472 | bytes 9437184 | tf_op jit(solution)/shard_map/project/pallas_call | solution.py:76
  114.7 12.7 %collective-permute-done.23 = bf16[2,512,384]{2,1,0:T(8,128)(2,1)} collective-permute-done((bf16[2,512,384]{2,1,0:T(8,128)(2,1)S(1)}, bf16[2,512,384]{2,1,0:T(8,128)(2,1)}, u32[]{:S(2)}, u32[]{:S(2)}) %collective-permute-start.23) | collective-permute-done | bytes 786464 | tf_op jit(solution)/shard_map/ppermute | solution.py:305
  140.7 8.3 %collective-permute-done.24 = bf16[2,512,384]{2,1,0:T(8,128)(2,1)} collective-permute-done((bf16[2,512,384]{2,1,0:T(8,128)(2,1)}, bf16[2,512,384]{2,1,0:T(8,128)(2,1)}, u32[]{:S(2)}, u32[]{:S(2)}) %collective-permute-start.24) | collective-permute-done | bytes 786464 | tf_op jit(solution)/shard_map/ppermute | solution.py:305
  177.6 11.6 %attend.1 = (f32[2,512,512]{2,1,0:T(8,128)}, bf16[2,512,384]{2,1,0:T(8,128)(2,1)S(1)}, f32[2,2,1,1024]{3,2,1,0:T(1,128)S(1)}) custom-call(s32[3]{0:T(128)S(1)} %pad_add_fusion.info_ref, bf16[2,512,512]{2,1,0:T(8,128)(2,1)S(1)} %bitcast.511, bf16[4,2,512,384]{3,2,1,0:T(8,128)(2,1)} %pad_maximum_fusion.2.kv_ref, s32[1,1024]{1,0:T(1,128)S(1)} %bitcast.509, ...), custom_call_target="tpu_custom_call" | custom-call | flops 4294967296 | bytes 5242880 | tf_op jit(solution)/shard_map/attend/pallas_call | solution.py:155
  200.5 11.6 %collective-permute-done.30 = bf16[2,128,1536]{2,1,0:T(8,128)(2,1)S(1)} collective-permute-done((bf16[2,128,1536]{2,1,0:T(8,128)(2,1)S(1)}, bf16[2,128,1536]{2,1,0:T(8,128)(2,1)S(1)}, u32[]{:S(2)}, u32[]{:S(2)}) %collective-permute-start.30) | collective-permute-done | bytes 786464 | tf_op jit(solution)/shard_map/ppermute | solution.py:295
  216.8 8.7 %collective-permute-done.31 = bf16[128,1536]{1,0:T(8,128)(2,1)S(1)} collective-permute-done((bf16[128,1536]{1,0:T(8,128)(2,1)S(1)}, bf16[128,1536]{1,0:T(8,128)(2,1)S(1)}, u32[]{:S(2)}, u32[]{:S(2)}) %collective-permute-start.31) | collective-permute-done | bytes 393248 | tf_op jit(solution)/shard_map/ppermute | solution.py:295
  226.4 11.8 %collective-permute-done.42 = bf16[192,2048]{1,0:T(8,128)(2,1)S(1)} collective-permute-done((bf16[192,2048]{1,0:T(8,128)(2,1)S(1)}, bf16[192,2048]{1,0:T(8,128)(2,1)S(1)}, u32[]{:S(2)}, u32[]{:S(2)}) %collective-permute-start.42) | collective-permute-done | bytes 786464 | tf_op jit(solution)/shard_map/ppermute | solution.py:305
  242.1 10.1 %collective-permute-done.34 = bf16[128,1536]{1,0:T(8,128)(2,1)S(1)} collective-permute-done((bf16[128,1536]{1,0:T(8,128)(2,1)S(1)}, bf16[128,1536]{1,0:T(8,128)(2,1)S(1)}, u32[]{:S(2)}, u32[]{:S(2)}) %collective-permute-start.34) | collective-permute-done | bytes 393248 | tf_op jit(solution)/shard_map/ppermute | solution.py:295
  254.2 14.2 %collective-permute-done.45 = bf16[192,2048]{1,0:T(8,128)(2,1)S(1)} collective-permute-done((bf16[192,2048]{1,0:T(8,128)(2,1)S(1)}, bf16[192,2048]{1,0:T(8,128)(2,1)S(1)}, u32[]{:S(2)}, u32[]{:S(2)}) %collective-permute-start.45) | collective-permute-done | bytes 786464 | tf_op jit(solution)/shard_map/ppermute | solution.py:305
  272.9 9.3 %fusion.90 = f32[1024,2048]{1,0:T(8,128)} fusion(bf16[1024,1536]{1,0:T(8,128)(2,1)S(1)} %bitcast.538, bf16[1536,2048]{1,0:T(8,128)(2,1)S(1)} %bitcast.520), kind=kOutput, calls=%fused_computation.309 | convolution fusion | flops 6442450944 | bytes 17825792 | tf_op jit(solution)/shard_map/dot_general | solution.py:43
  282.2 9.2 %multiply_convert_fusion.1 = (bf16[1024,1024]{1,0:T(8,128)(2,1)}, bf16[1024,1024]{1,0:T(8,128)(2,1)}, bf16[1024,1024]{1,0:T(8,128)(2,1)}) fusion(f32[1024,2048]{1,0:T(8,128)} %fusion.90, bf16[1024,1536]{1,0:T(8,128)(2,1)S(1)} %bitcast.534, bf16[1024,1536]{1,0:T(8,128)(2,1)S(1)} %bitcast.542), kind=kOutput, calls=%fused_computation.8 | convolution fusion | flops 3236954112 | bytes 20971520 | tf_op jit(solution)/shard_map/dot_general | solution.py:47
  291.4 10.9 %fusion.89 = (bf16[1024,1536]{1,0:T(8,128)(2,1)}, f32[1024,1536]{1,0:T(8,128)}) fusion(bf16[1536,2048]{1,0:T(8,128)(2,1)S(1)} %bitcast.521, bf16[1024,1024]{1,0:T(8,128)(2,1)} %get-tuple-element.133, bf16[1024,1024]{1,0:T(8,128)(2,1)} %get-tuple-element.132), kind=kOutput, calls=%fused_computation.308 | convolution fusion | flops 6452412416 | bytes 19922944 | tf_op jit(solution)/shard_map/dot_general | solution.py:47
  308.4 9.4 %convolution_convert_fusion = bf16[1536,2048]{1,0:T(8,128)(2,1)S(1)} fusion(bf16[1024,1536]{1,0:T(8,128)(2,1)S(1)} %bitcast.539, bf16[1024,1024]{1,0:T(8,128)(2,1)} %get-tuple-element.133, bf16[1024,1024]{1,0:T(8,128)(2,1)} %get-tuple-element.132), kind=kOutput, calls=%fused_computation.1 | convolution fusion | flops 6453985280 | bytes 13631488 | tf_op jit(solution)/shard_map/dot_general | solution.py:51
  351.9 11.0 %collective-permute-done.63 = bf16[2,128,1536]{2,1,0:T(8,128)(2,1)S(1)} collective-permute-done((bf16[2,128,1536]{2,1,0:T(8,128)(2,1)S(1)}, bf16[2,128,1536]{2,1,0:T(8,128)(2,1)S(1)}, u32[]{:S(2)}, u32[]{:S(2)}) %collective-permute-start.63) | collective-permute-done | bytes 786464 | tf_op jit(solution)/shard_map/ppermute | solution.py:295
  389.9 11.5 %collective-permute-done.66 = bf16[192,2048]{1,0:T(8,128)(2,1)S(1)} collective-permute-done((bf16[192,2048]{1,0:T(8,128)(2,1)S(1)}, bf16[192,2048]{1,0:T(8,128)(2,1)S(1)}, u32[]{:S(2)}, u32[]{:S(2)}) %collective-permute-start.66) | collective-permute-done | bytes 786464 | tf_op jit(solution)/shard_map/ppermute | solution.py:305
  405.4 19.6 %attend_back.1 = (bf16[2,512,384]{2,1,0:T(8,128)(2,1)S(1)}, bf16[4,2,512,384]{3,2,1,0:T(8,128)(2,1)}) custom-call(s32[3]{0:T(128)S(1)} %pad_add_fusion.info_ref, bf16[2,512,512]{2,1,0:T(8,128)(2,1)S(1)} %bitcast.512, bf16[4,2,512,384]{3,2,1,0:T(8,128)(2,1)} %pad_maximum_fusion.2.kv_ref, bf16[2,512,384]{2,1,0:T(8,128)(2,1)S(1)} %bitcast.515, ...), custom_call_target="tpu_custom_call" | custom-call | flops 10737418240 | bytes 10485760 | tf_op jit(solution)/shard_map/attend_back/pallas_call | solution.py:250
  431.4 20.5 %collective-permute-start.72 = (bf16[192,2048]{1,0:T(8,128)(2,1)S(1)}, bf16[192,2048]{1,0:T(8,128)(2,1)S(1)}, u32[]{:S(2)}, u32[]{:S(2)}) collective-permute-start(bf16[192,2048]{1,0:T(8,128)(2,1)S(1)} %copy-done.41), channel_id=1, source_target_pairs={{0,12},{4,0},{8,4},{12,8},{1,13},{5,1},{9,5},{13,9},{2,14},{6,2},{... | collective-permute-start | bytes 2359304 | tf_op jit(solution)/shard_map/ppermute | solution.py:305
  459.0 10.3 %collective-permute-done.72 = bf16[192,2048]{1,0:T(8,128)(2,1)S(1)} collective-permute-done((bf16[192,2048]{1,0:T(8,128)(2,1)S(1)}, bf16[192,2048]{1,0:T(8,128)(2,1)S(1)}, u32[]{:S(2)}, u32[]{:S(2)}) %collective-permute-start.72) | collective-permute-done | bytes 786464 | tf_op jit(solution)/shard_map/ppermute | solution.py:305
  485.2 13.7 %collective-permute-done.75 = bf16[192,2048]{1,0:T(8,128)(2,1)S(1)} collective-permute-done((bf16[192,2048]{1,0:T(8,128)(2,1)S(1)}, bf16[192,2048]{1,0:T(8,128)(2,1)S(1)}, u32[]{:S(2)}, u32[]{:S(2)}) %collective-permute-start.75) | collective-permute-done | bytes 786464 | tf_op jit(solution)/shard_map/ppermute | solution.py:305
  500.2 13.8 %collective-permute-done.74 = bf16[2,512,384]{2,1,0:T(8,128)(2,1)S(1)} collective-permute-done((bf16[2,512,384]{2,1,0:T(8,128)(2,1)S(1)}, bf16[2,512,384]{2,1,0:T(8,128)(2,1)S(1)}, u32[]{:S(2)}, u32[]{:S(2)}) %collective-permute-start.74) | collective-permute-done | bytes 786464 | tf_op jit(solution)/shard_map/ppermute | solution.py:305
  525.7 10.9 %collective-permute-done.77 = bf16[2,512,384]{2,1,0:T(8,128)(2,1)} collective-permute-done((bf16[2,512,384]{2,1,0:T(8,128)(2,1)}, bf16[2,512,384]{2,1,0:T(8,128)(2,1)}, u32[]{:S(2)}, u32[]{:S(2)}) %collective-permute-start.77) | collective-permute-done | bytes 786464 | tf_op jit(solution)/shard_map/ppermute | solution.py:305
  547.7 11.9 %collective-permute-done.78 = bf16[2,512,384]{2,1,0:T(8,128)(2,1)} collective-permute-done((bf16[2,512,384]{2,1,0:T(8,128)(2,1)}, bf16[2,512,384]{2,1,0:T(8,128)(2,1)}, u32[]{:S(2)}, u32[]{:S(2)}) %collective-permute-start.78) | collective-permute-done | bytes 786464 | tf_op jit(solution)/shard_map/ppermute | solution.py:305
  583.7 8.0 %collective-permute-done.79 = bf16[2,128,1536]{2,1,0:T(8,128)(2,1)} collective-permute-done((bf16[2,128,1536]{2,1,0:T(8,128)(2,1)}, bf16[2,128,1536]{2,1,0:T(8,128)(2,1)}, u32[]{:S(2)}, u32[]{:S(2)}) %collective-permute-start.79) | collective-permute-done | bytes 786464 | tf_op jit(solution)/shard_map/ppermute | solution.py:295
  (546 shorter events, 375.8 us)
Async XLA Ops:
  4.7 27.4 %all-to-all-start = ((bf16[48,4,768]{2,0,1:T(8,128)(2,1)}), bf16[48,4,768]{2,0,1:T(8,128)(2,1)}, u32[]{:S(2)}, u32[]{:S(2)}) async-start(bf16[48,4,768]{2,0,1:T(8,128)(2,1)} %copy.74), calls=%async_computation | async-start | bytes 589824 | tf_op jit(solution)/shard_map/all_to_all | solution.py:373
  51.5 27.3 %collective-permute-start.3 = (bf16[2,128,1536]{2,1,0:T(8,128)(2,1)}, bf16[2,128,1536]{2,1,0:T(8,128)(2,1)}, u32[]{:S(2)}, u32[]{:S(2)}) collective-permute-start(bf16[2,128,1536]{2,1,0:T(8,128)(2,1)} %pad_maximum_fusion.14), channel_id=1, source_target_pairs={{0,1},{1,0},{2,3},{3,2},{4,5},{5,4},{6,7},{7,6},{8,9},{9,8},{10,11... | collective-permute-start | bytes 2359304 | tf_op jit(solution)/shard_map/ppermute | solution.py:295
  55.5 26.1 %collective-permute-start.1 = (bf16[2,128,1536]{2,1,0:T(8,128)(2,1)}, bf16[2,128,1536]{2,1,0:T(8,128)(2,1)}, u32[]{:S(2)}, u32[]{:S(2)}) collective-permute-start(bf16[2,128,1536]{2,1,0:T(8,128)(2,1)} %pad_maximum_fusion.13), channel_id=1, source_target_pairs={{0,2},{1,3},{2,0},{3,1},{4,6},{5,7},{6,4},{7,5},{8,10},{9,11},{10,... | collective-permute-start | bytes 2359304 | tf_op jit(solution)/shard_map/ppermute | solution.py:295
  86.2 25.6 %collective-permute-start.54 = (bf16[128,1536]{1,0:T(8,128)(2,1)S(1)}, bf16[128,1536]{1,0:T(8,128)(2,1)S(1)}, u32[]{:S(2)}, u32[]{:S(2)}) collective-permute-start(bf16[128,1536]{1,0:T(8,128)(2,1)S(1)} %get-tuple-element.182), channel_id=1, source_target_pairs={{0,2},{1,3},{2,0},{3,1},{4,6},{5,7},{6,4},{7,5},{8,10},{9,11},{10,... | collective-permute-start | bytes 1179656 | tf_op jit(solution)/shard_map/ppermute | solution.py:295
  87.6 45.3 %collective-permute-start.52 = (bf16[128,1536]{1,0:T(8,128)(2,1)S(1)}, bf16[128,1536]{1,0:T(8,128)(2,1)S(1)}, u32[]{:S(2)}, u32[]{:S(2)}) collective-permute-start(bf16[128,1536]{1,0:T(8,128)(2,1)S(1)} %get-tuple-element.181), channel_id=1, source_target_pairs={{0,1},{1,0},{2,3},{3,2},{4,5},{5,4},{6,7},{7,6},{8,9},{9,8},{10,11... | collective-permute-start | bytes 1179656 | tf_op jit(solution)/shard_map/ppermute | solution.py:295
  112.8 26.6 %collective-permute-start.55 = (bf16[2,128,1536]{2,1,0:T(8,128)(2,1)}, bf16[2,128,1536]{2,1,0:T(8,128)(2,1)}, u32[]{:S(2)}, u32[]{:S(2)}) collective-permute-start(bf16[2,128,1536]{2,1,0:T(8,128)(2,1)} %pad_maximum_fusion.19), channel_id=1, source_target_pairs={{0,1},{1,0},{2,3},{3,2},{4,5},{5,4},{6,7},{7,6},{8,9},{9,8},{10,11... | collective-permute-start | bytes 2359304 | tf_op jit(solution)/shard_map/ppermute | solution.py:295
  133.9 27.1 %collective-permute-start.53 = (bf16[2,128,1536]{2,1,0:T(8,128)(2,1)}, bf16[2,128,1536]{2,1,0:T(8,128)(2,1)}, u32[]{:S(2)}, u32[]{:S(2)}) collective-permute-start(bf16[2,128,1536]{2,1,0:T(8,128)(2,1)} %pad_maximum_fusion.18), channel_id=1, source_target_pairs={{0,2},{1,3},{2,0},{3,1},{4,6},{5,7},{6,4},{7,5},{8,10},{9,11},{10,... | collective-permute-start | bytes 2359304 | tf_op jit(solution)/shard_map/ppermute | solution.py:295
  135.1 30.6 %all-to-all-start.2 = ((bf16[4,384,384]{2,1,0:T(8,128)(2,1)}), bf16[4,384,384]{2,1,0:T(8,128)(2,1)}, u32[]{:S(2)}, u32[]{:S(2)}) async-start(bf16[4,384,384]{2,1,0:T(8,128)(2,1)} %bitcast.527), calls=%async_computation.2 | async-start | bytes 2359296 | tf_op jit(solution)/shard_map/all_to_all | solution.py:373
  169.4 25.2 %collective-permute-start.40 = (bf16[128,1536]{1,0:T(8,128)(2,1)}, bf16[128,1536]{1,0:T(8,128)(2,1)}, u32[]{:S(2)}, u32[]{:S(2)}) collective-permute-start(bf16[128,1536]{1,0:T(8,128)(2,1)} %param.28), channel_id=1, source_target_pairs={{0,4},{4,8},{8,12},{12,0},{1,5},{5,9},{9,13},{13,1},{2,6},{6,10},{... | collective-permute-start | bytes 1179656 | tf_op jit(solution)/shard_map/ppermute | solution.py:305
  171.9 28.6 %collective-permute-start.39 = (bf16[192,2048]{1,0:T(8,128)(2,1)S(1)}, bf16[192,2048]{1,0:T(8,128)(2,1)S(1)}, u32[]{:S(2)}, u32[]{:S(2)}) collective-permute-start(bf16[192,2048]{1,0:T(8,128)(2,1)S(1)} %copy-done.30), channel_id=1, source_target_pairs={{0,4},{4,8},{8,12},{12,0},{1,5},{5,9},{9,13},{13,1},{2,6},{6,10},{... | collective-permute-start | bytes 2359304 | tf_op jit(solution)/shard_map/ppermute | solution.py:305
  174.4 40.5 %collective-permute-start.38 = (bf16[192,2048]{1,0:T(8,128)(2,1)S(1)}, bf16[192,2048]{1,0:T(8,128)(2,1)S(1)}, u32[]{:S(2)}, u32[]{:S(2)}) collective-permute-start(bf16[192,2048]{1,0:T(8,128)(2,1)S(1)} %copy-done.30), channel_id=1, source_target_pairs={{0,16},{16,0},{1,17},{17,1},{2,18},{18,2},{3,19},{19,3},{4,20},{20... | collective-permute-start | bytes 2359304 | tf_op jit(solution)/shard_map/ppermute | solution.py:299
  200.5 25.9 %collective-permute-start.49 = (bf16[128,1536]{1,0:T(8,128)(2,1)}, bf16[128,1536]{1,0:T(8,128)(2,1)S(1)}, u32[]{:S(2)}, u32[]{:S(2)}) collective-permute-start(bf16[128,1536]{1,0:T(8,128)(2,1)} %collective-permute-done.40), channel_id=1, source_target_pairs={{0,16},{16,0},{1,17},{17,1},{2,18},{18,2},{3,19},{19,3},{4,20},{20... | collective-permute-start | bytes 1179656 | tf_op jit(solution)/shard_map/ppermute | solution.py:299
  200.5 25.9 %collective-permute-start.43 = (bf16[128,1536]{1,0:T(8,128)(2,1)}, bf16[128,1536]{1,0:T(8,128)(2,1)S(1)}, u32[]{:S(2)}, u32[]{:S(2)}) collective-permute-start(bf16[128,1536]{1,0:T(8,128)(2,1)} %collective-permute-done.40), channel_id=1, source_target_pairs={{0,4},{4,8},{8,12},{12,0},{1,5},{5,9},{9,13},{13,1},{2,6},{6,10},{... | collective-permute-start | bytes 1179656 | tf_op jit(solution)/shard_map/ppermute | solution.py:305
  212.1 26.1 %collective-permute-start.42 = (bf16[192,2048]{1,0:T(8,128)(2,1)S(1)}, bf16[192,2048]{1,0:T(8,128)(2,1)S(1)}, u32[]{:S(2)}, u32[]{:S(2)}) collective-permute-start(bf16[192,2048]{1,0:T(8,128)(2,1)S(1)} %collective-permute-done.39), channel_id=1, source_target_pairs={{0,4},{4,8},{8,12},{12,0},{1,5},{5,9},{9,13},{13,1},{2,6},{6,10},{... | collective-permute-start | bytes 2359304 | tf_op jit(solution)/shard_map/ppermute | solution.py:305
  238.2 30.2 %collective-permute-start.45 = (bf16[192,2048]{1,0:T(8,128)(2,1)S(1)}, bf16[192,2048]{1,0:T(8,128)(2,1)S(1)}, u32[]{:S(2)}, u32[]{:S(2)}) collective-permute-start(bf16[192,2048]{1,0:T(8,128)(2,1)S(1)} %collective-permute-done.42), channel_id=1, source_target_pairs={{0,4},{4,8},{8,12},{12,0},{1,5},{5,9},{9,13},{13,1},{2,6},{6,10},{... | collective-permute-start | bytes 2359304 | tf_op jit(solution)/shard_map/ppermute | solution.py:305
  238.6 30.3 %collective-permute-start.44 = (bf16[192,2048]{1,0:T(8,128)(2,1)S(1)}, bf16[192,2048]{1,0:T(8,128)(2,1)S(1)}, u32[]{:S(2)}, u32[]{:S(2)}) collective-permute-start(bf16[192,2048]{1,0:T(8,128)(2,1)S(1)} %collective-permute-done.42), channel_id=1, source_target_pairs={{0,16},{16,0},{1,17},{17,1},{2,18},{18,2},{3,19},{19,3},{4,20},{20... | collective-permute-start | bytes 2359304 | tf_op jit(solution)/shard_map/ppermute | solution.py:299
  330.1 41.7 %collective-permute-start.64 = (bf16[4,192,2048]{2,1,0:T(8,128)(2,1)}, bf16[4,192,2048]{2,1,0:T(8,128)(2,1)}, u32[]{:S(2)}, u32[]{:S(2)}) collective-permute-start(bf16[4,192,2048]{2,1,0:T(8,128)(2,1)} %dynamic-slice_bitcast_fusion), channel_id=1, source_target_pairs={{0,16},{16,0},{1,17},{17,1},{2,18},{18,2},{3,19},{19,3},{4,20},{20... | collective-permute-start | bytes 9437192 | tf_op jit(solution)/shard_map/ppermute | solution.py:299
  367.5 62.6 %all-to-all-start.3 = ((bf16[384,4,384]{2,0,1:T(8,128)(2,1)}), bf16[384,4,384]{2,0,1:T(8,128)(2,1)}, u32[]{:S(2)}, u32[]{:S(2)}) async-start(bf16[384,4,384]{2,0,1:T(8,128)(2,1)} %bitcast.526), calls=%async_computation.3 | async-start | bytes 2359296 | tf_op jit(solution)/shard_map/all_to_all | solution.py:373
  402.6 53.4 %collective-permute-start.73 = (bf16[128,1536]{1,0:T(8,128)(2,1)}, bf16[128,1536]{1,0:T(8,128)(2,1)}, u32[]{:S(2)}, u32[]{:S(2)}) collective-permute-start(bf16[128,1536]{1,0:T(8,128)(2,1)} %fusion.43), channel_id=1, source_target_pairs={{0,12},{4,0},{8,4},{12,8},{1,13},{5,1},{9,5},{13,9},{2,14},{6,2},{... | collective-permute-start | bytes 1179656 | tf_op jit(solution)/shard_map/ppermute | solution.py:305
  428.1 29.0 %collective-permute-start.68 = (bf16[2,128,1536]{2,1,0:T(8,128)(2,1)}, bf16[2,128,1536]{2,1,0:T(8,128)(2,1)}, u32[]{:S(2)}, u32[]{:S(2)}) collective-permute-start(bf16[2,128,1536]{2,1,0:T(8,128)(2,1)} %pad_maximum_fusion.23), channel_id=1, source_target_pairs={{0,1},{1,0},{2,3},{3,2},{4,5},{5,4},{6,7},{7,6},{8,9},{9,8},{10,11... | collective-permute-start | bytes 2359304 | tf_op jit(solution)/shard_map/ppermute | solution.py:295
  431.3 86.3 %collective-permute-start.84 = (bf16[4,192,384]{2,1,0:T(8,128)(2,1)S(1)}, bf16[4,192,384]{2,1,0:T(8,128)(2,1)}, u32[]{:S(2)}, u32[]{:S(2)}) collective-permute-start(bf16[4,192,384]{2,1,0:T(8,128)(2,1)S(1)} %dynamic-slice_bitcast_fusion.4), channel_id=1, source_target_pairs={{0,16},{16,0},{1,17},{17,1},{2,18},{18,2},{3,19},{19,3},{4,20},{20... | collective-permute-start | bytes 1769480 | tf_op jit(solution)/shard_map/ppermute | solution.py:299
  431.4 37.9 %collective-permute-start.72 = (bf16[192,2048]{1,0:T(8,128)(2,1)S(1)}, bf16[192,2048]{1,0:T(8,128)(2,1)S(1)}, u32[]{:S(2)}, u32[]{:S(2)}) collective-permute-start(bf16[192,2048]{1,0:T(8,128)(2,1)S(1)} %copy-done.41), channel_id=1, source_target_pairs={{0,12},{4,0},{8,4},{12,8},{1,13},{5,1},{9,5},{13,9},{2,14},{6,2},{... | collective-permute-start | bytes 2359304 | tf_op jit(solution)/shard_map/ppermute | solution.py:305
  474.0 40.0 %collective-permute-start.74 = (bf16[2,512,384]{2,1,0:T(8,128)(2,1)S(1)}, bf16[2,512,384]{2,1,0:T(8,128)(2,1)S(1)}, u32[]{:S(2)}, u32[]{:S(2)}) collective-permute-start(bf16[2,512,384]{2,1,0:T(8,128)(2,1)S(1)} %slice_bitcast_fusion), channel_id=1, source_target_pairs={{4,0},{8,4},{12,8},{5,1},{9,5},{13,9},{6,2},{10,6},{14,10},{7,3},{... | collective-permute-start | bytes 2359304 | tf_op jit(solution)/shard_map/ppermute | solution.py:305
  483.9 40.2 %collective-permute-start.71 = (bf16[128,1536]{1,0:T(8,128)(2,1)}, bf16[128,1536]{1,0:T(8,128)(2,1)}, u32[]{:S(2)}, u32[]{:S(2)}) collective-permute-start(bf16[128,1536]{1,0:T(8,128)(2,1)} %get-tuple-element.157), channel_id=1, source_target_pairs={{0,1},{1,0},{2,3},{3,2},{4,5},{5,4},{6,7},{7,6},{8,9},{9,8},{10,11... | collective-permute-start | bytes 1179656 | tf_op jit(solution)/shard_map/ppermute | solution.py:295
  (143 other events, 1740.1 us)

commit v3 on v1

v3 whole, which is shorter than its diff:
```python
import math

import jax
import jax.numpy as jnp
import numpy as np
from jax import lax
from jax.experimental import pallas as pl
from jax.experimental.pallas import tpu as pltpu
from jax.sharding import Mesh
from jax.sharding import PartitionSpec as P

HQ = 16
HK = 8
DH = 96
PLANE = 4
LANES = 128
VMEM_BYTES = 50 * 1024 * 1024

epsilon = 1e-05
rope_base = 100000.0
masked_score = -1e30
score_scale = 1.0 / math.sqrt(DH)
exp2_scale = score_scale * math.log2(math.e)

f32 = jnp.float32
bf16 = jnp.bfloat16


def spread(heads):
    table = np.zeros((heads * DH, heads * LANES), np.float32)
    for head in range(heads):
        for i in range(DH):
            lane = i if i < DH // 2 else i + (LANES - DH) // 2
            table[head * DH + i, head * LANES + lane] = 1.0
    return jnp.asarray(table, bf16)


def rms_scale(values):
    return lax.rsqrt(jnp.mean(values * values, axis=-1, keepdims=True) + epsilon)


def dot(a, b):
    return jnp.dot(a, b, preferred_element_type=f32)


def dot_nt(a, b):
    return lax.dot_general(a, b, (((1,), (1,)), ((), ())), preferred_element_type=f32)


def dot_tn(a, b):
    return lax.dot_general(a, b, (((0,), (0,)), ((), ())), preferred_element_type=f32)


def project_kernel(size, info_ref, x_ref, cos_ref, sin_ref, e4_ref, e8_ref, *rest):
    blocks, (n_ref, q_ref, kv_ref, w_ref, out_w_ref, gains_ref, pad_s) = rest[: 2 * size], rest[2 * size :]
    rows = blocks[0].shape[0]
    heads = 8 * DH

    @pl.when(pl.program_id(0) == 0)
    def _():
        for i, block in enumerate(blocks):
            core = info_ref[1] if i < size else 1 - info_ref[1]
            start = pl.multiple_of((core * size + lax.rem(info_ref[0] - i % size + size, size)) * rows, rows)
            w_ref[pl.ds(start, rows), :] = block[:, : heads + LANES]
            out_w_ref[pl.ds(start, rows), :] = block[:, heads + LANES :]
            pad_s[pl.ds(start, rows), :] = dot(block[:, :heads], e8_ref[...]).astype(bf16)
        rows_to = lax.broadcasted_iota(jnp.int32, (LANES, LANES), 0)
        same = (rows_to == lax.broadcasted_iota(jnp.int32, (LANES, LANES), 1)).astype(bf16)
        gains_ref[...] = dot_nt(same[:8], w_ref[:, heads:])

    x = x_ref[...].astype(f32)
    normed = (x * rms_scale(x) * gains_ref[0:1, :]).astype(bf16)
    n_ref[...] = normed
    pre = dot(normed, pad_s[...])
    cos, sin = cos_ref[...], sin_ref[...]
    parts = []
    for head in range(8):
        piece = pre[:, head * LANES : (head + 1) * LANES]
        if head < 6:
            piece = piece * cos + pltpu.roll(piece, LANES // 2, 1) * sin
        parts.append(piece.astype(bf16))
    q_ref[...] = jnp.concatenate(parts[:4], axis=1)
    kv_ref[...] = dot_nt(jnp.concatenate(parts[4:], axis=1), e4_ref[...]).astype(bf16)


def project(info, x, blocks, cos, sin, e4, e8):
    rows, width = x.shape
    step = min(256, rows)
    size = len(blocks) // 2
    cols = blocks[0].shape[1]
    first = 8 * DH + LANES
    whole = lambda a: pl.BlockSpec(a.shape, lambda i, n: (0,) * a.ndim)
    by_row = lambda c: pl.BlockSpec((step, c), lambda i, n: (i, 0))
    return pl.pallas_call(
        lambda *refs: project_kernel(size, *refs),
        grid_spec=pltpu.PrefetchScalarGridSpec(
            num_scalar_prefetch=1,
            grid=(rows // step,),
            in_specs=[by_row(width), by_row(LANES), by_row(LANES), whole(e4), whole(e8)] + [whole(b) for b in blocks],
            out_specs=[
                by_row(width),
                by_row(4 * LANES),
                by_row(4 * DH),
                pl.BlockSpec((width, first), lambda i, n: (0, 0)),
                pl.BlockSpec((width, cols - first), lambda i, n: (0, 0)),
                pl.BlockSpec((8, width), lambda i, n: (0, 0)),
            ],
            scratch_shapes=[pltpu.VMEM((width, 8 * LANES), bf16)],
        ),
        out_shape=[
            jax.ShapeDtypeStruct((rows, width), bf16),
            jax.ShapeDtypeStruct((rows, 4 * LANES), bf16),
            jax.ShapeDtypeStruct((rows, 4 * DH), bf16),
            jax.ShapeDtypeStruct((width, first), bf16),
            jax.ShapeDtypeStruct((width, cols - first), bf16),
            jax.ShapeDtypeStruct((8, width), f32),
        ],
        compiler_params=pltpu.CompilerParams(vmem_limit_bytes=VMEM_BYTES),
        cost_estimate=pl.CostEstimate(
            flops=2 * rows * width * 8 * LANES, bytes_accessed=2 * (2 * rows * width + 2 * width * cols), transcendentals=0
        ),
        name="project",
    )(info, x, cos, sin, e4, e8, *blocks)


def assemble_kernel(size, info_ref, *rest):
    blocks, out_ref = rest[: 2 * size], rest[2 * size]
    rows = blocks[0].shape[0]
    for i, block in enumerate(blocks):
        core = info_ref[1] if i < size else 1 - info_ref[1]
        start = pl.multiple_of((core * size + lax.rem(info_ref[0] - i % size + size, size)) * rows, rows)
        out_ref[pl.ds(start, rows), :] = block[...]


def assemble(info, blocks):
    size = len(blocks) // 2
    rows, width = blocks[0].shape
    step = width // 3 if width % 384 == 0 else width // 4
    return pl.pallas_call(
        lambda *refs: assemble_kernel(size, *refs),
        grid_spec=pltpu.PrefetchScalarGridSpec(
            num_scalar_prefetch=1,
            grid=(width // step,),
            in_specs=[pl.BlockSpec((rows, step), lambda i, n: (0, i)) for _ in blocks],
            out_specs=pl.BlockSpec((len(blocks) * rows, step), lambda i, n: (0, i)),
        ),
        out_shape=jax.ShapeDtypeStruct((len(blocks) * rows, width), blocks[0].dtype),
        compiler_params=pltpu.CompilerParams(vmem_limit_bytes=VMEM_BYTES),
        cost_estimate=pl.CostEstimate(flops=0, bytes_accessed=4 * len(blocks) * rows * width, transcendentals=0),
        name="assemble",
    )(info, *blocks)


def allowed_of(info_ref, k, chunk, qpos_ref, qbeg_ref, kpos_ref):
    kpos = kpos_ref[...] + (info_ref[0] - k) * chunk
    return (kpos <= qpos_ref[...]) & (kpos >= qbeg_ref[...])


def useful_of(info_ref, m, k, chunk):
    z = info_ref[0]
    return (k <= z) & ((z - k + 1) * chunk - 1 >= info_ref[2 + m])


def stack_heads(block, h):
    return jnp.concatenate(
        [block[:, (2 * h) * LANES : (2 * h + 1) * LANES], block[:, (2 * h + 1) * LANES : (2 * h + 2) * LANES]], axis=0
    )


def run_kernel(body, info, inputs, outs, aliases, flops, transcendentals, name):
    whole = lambda shape: pl.BlockSpec(shape, lambda i, n: (0,) * len(shape))
    moved = sum(a.size * a.dtype.itemsize for a in inputs) + sum(math.prod(o.shape) * o.dtype.itemsize for o in outs)
    return list(
        pl.pallas_call(
        body,
        grid_spec=pltpu.PrefetchScalarGridSpec(
            num_scalar_prefetch=1,
            grid=(1,),
            in_specs=[whole(a.shape) for a in inputs],
            out_specs=[whole(o.shape) for o in outs],
        ),
        out_shape=outs,
        input_output_aliases=aliases,
        compiler_params=pltpu.CompilerParams(vmem_limit_bytes=VMEM_BYTES),
        cost_estimate=pl.CostEstimate(flops=flops, bytes_accessed=moved, transcendentals=transcendentals),
        name=name,
    )(info, *inputs)
    )


def attend_kernel(m, k, last, info_ref, q_ref, kv_ref, qpos_ref, qbeg_ref, kpos_ref, e_ref, *rest):
    chunk = kv_ref.shape[0]
    if k > 0:
        top_in, acc_in, rest = rest[0], rest[1], rest[2:]
    top_ref, acc_ref = rest[0], rest[1]

    def run():
        allowed = allowed_of(info_ref, k, chunk, qpos_ref, qbeg_ref, kpos_ref)
        kv = kv_ref[...]
        q = q_ref[...]
        one_lane = (lax.broadcasted_iota(jnp.int32, (1, LANES), 1) == DH // 2).astype(f32)
        for h in range(2):
            keys = dot(kv, e_ref[:, h * LANES : (h + 1) * LANES]).astype(bf16)
            vals = (dot(kv, e_ref[:, (2 + h) * LANES : (3 + h) * LANES]) + one_lane).astype(bf16)
            s = jnp.where(allowed, dot_nt(keys, stack_heads(q, h)), masked_score)
            new = jnp.max(s, axis=0, keepdims=True)
            if k > 0:
                old = top_in[h]
                new = jnp.maximum(old, new)
            w = jnp.where(allowed, jnp.exp2((s - new) * exp2_scale), 0.0).astype(bf16)
            acc = dot_tn(vals, w)
            if k > 0:
                acc = acc_in[h] * jnp.exp2((old - new) * exp2_scale) + acc
            acc_ref[h] = acc
            top_ref[h] = new

    if k == 0:
        run()
    else:
        useful = useful_of(info_ref, m, k, chunk)
        pl.when(useful)(run)

        @pl.when(jnp.logical_not(useful))
        def _():
            top_ref[...] = top_in[...]
            acc_ref[...] = acc_in[...]

    if last:
        att_ref, low_ref, lse_ref = rest[2:]
        parts = []
        for h in range(2):
            acc = acc_ref[h]
            total = acc[DH // 2 : DH // 2 + 1, :]
            lse_ref[h] = top_ref[h] * exp2_scale + jnp.log2(total)
            flat = (acc / total).T
            rows = flat.shape[0] // 2
            parts += [flat[:rows], flat[rows:]]
        att = jnp.concatenate(parts, axis=1)
        att_ref[...] = att
        low_ref[...] = dot_nt(att.astype(bf16), e_ref[...]).astype(bf16)


def attend(m, k, last, info, q, kv, qpos, qbeg, kpos, e4, state):
    rows, chunk = q.shape[0], kv.shape[0]
    outs = [jax.ShapeDtypeStruct((2, 1, 2 * rows), f32), jax.ShapeDtypeStruct((2, LANES, 2 * rows), f32)]
    if last:
        outs += [
            jax.ShapeDtypeStruct((rows, 4 * LANES), f32),
            jax.ShapeDtypeStruct((rows, 4 * DH), bf16),
            jax.ShapeDtypeStruct((2, 1, 2 * rows), f32),
        ]
    return run_kernel(
        lambda *refs: attend_kernel(m, k, last, *refs),
        info,
        [q, kv, qpos, qbeg, kpos, e4] + state,
        outs,
        {7: 0, 8: 1} if k > 0 else {},
        16 * rows * chunk * LANES,
        4 * rows * chunk,
        "attend",
    )


def attend_back_kernel(
    m, k, first, last, info_ref, q_ref, kv_ref, lse_ref, qpos_ref, qbeg_ref, kpos_ref, cosk_ref, sink_ref, e_ref, *rest
):
    chunk = kv_ref.shape[0]
    if first:
        g_ref, att_ref, rest = rest[0], rest[1], rest[2:]
        go_ref, delta_ref, dq_ref, dkv_ref = rest[:4]
        go = dot(g_ref[...], e_ref[...])
        for h in range(2):
            go_h = stack_heads(go, h)
            go_ref[h] = go_h.astype(bf16)
            prod = go_h * stack_heads(att_ref[...], h)
            delta_ref[h] = jnp.sum(prod.T, axis=0, keepdims=True)
    else:
        go_ref, delta_ref, dq_in, rest = rest[0], rest[1], rest[2], rest[3:]
        dq_ref, dkv_ref = rest[:2]

    def run():
        allowed = allowed_of(info_ref, k, chunk, qpos_ref, qbeg_ref, kpos_ref)
        kv = kv_ref[...]
        q = q_ref[...]
        cosk, sink = cosk_ref[...], sink_ref[...]
        grad_keys, grad_vals = [], []
        for h in range(2):
            keys = dot(kv, e_ref[:, h * LANES : (h + 1) * LANES]).astype(bf16)
            vals = dot(kv, e_ref[:, (2 + h) * LANES : (3 + h) * LANES]).astype(bf16)
            q_h = stack_heads(q, h)
            go_h = go_ref[h]
            s = dot_nt(keys, q_h)
            w = jnp.where(allowed, jnp.exp2(s * exp2_scale - lse_ref[h]), 0.0)
            grad_vals.append(dot(w.astype(bf16), go_h).astype(bf16))
            ds = (w * (dot_nt(vals, go_h) - delta_ref[h])).astype(bf16)
            dq = dot_tn(keys, ds)
            dq_ref[h] = dq if first else dq_in[h] + dq
            gk = dot(ds, q_h) * score_scale
            gk = gk * cosk + pltpu.roll(gk * sink, LANES // 2, 1)
            grad_keys.append(gk.astype(bf16))
        dkv_ref[...] = dot_nt(jnp.concatenate(grad_keys + grad_vals, axis=1), e_ref[...]).astype(bf16)

    if k == 0:
        run()
    else:
        useful = useful_of(info_ref, m, k, chunk)
        pl.when(useful)(run)

        @pl.when(jnp.logical_not(useful))
        def _():
            dkv_ref[...] = jnp.zeros(dkv_ref.shape, bf16)
            dq_ref[...] = jnp.zeros(dq_ref.shape, f32) if first else dq_in[...]

    if last:
        out_ref = rest[-1]
        parts = []
        for h in range(2):
            flat = dq_ref[h].T * score_scale
            rows = flat.shape[0] // 2
            for piece in (flat[:rows], flat[rows:]):
                parts.append((piece * cosk_ref[...] + pltpu.roll(piece * sink_ref[...], LANES // 2, 1)).astype(bf16))
        out_ref[...] = dot_nt(jnp.concatenate(parts, axis=1), e_ref[...]).astype(bf16)


def attend_back(m, k, first, last, info, q, kv, lse, qpos, qbeg, kpos, cosk, sink, e4, state):
    rows, chunk = q.shape[0], kv.shape[0]
    outs = []
    if first:
        outs += [jax.ShapeDtypeStruct((2, 2 * rows, LANES), bf16), jax.ShapeDtypeStruct((2, 1, 2 * rows), f32)]
    outs += [jax.ShapeDtypeStruct((2, LANES, 2 * rows), f32), jax.ShapeDtypeStruct(kv.shape, bf16)]
    if last:
        outs += [jax.ShapeDtypeStruct((rows, 4 * DH), bf16)]
    return run_kernel(
        lambda *refs: attend_back_kernel(m, k, first, last, *refs),
        info,
        [q, kv, lse, qpos, qbeg, kpos, cosk, sink, e4] + state,
        outs,
        {} if first else {12: 0},
        40 * rows * chunk * LANES,
        4 * rows * chunk,
        "attend_back",
    )


def beside(value, bit):
    return lax.ppermute(value, "plane", [(i, i ^ bit) for i in range(PLANE)])


def other_core(value):
    return lax.ppermute(value, "stream", [(0, 1), (1, 0)])


def along(value, step, wrap):
    size = lax.axis_size("zed")
    pairs = [(i, (i + step) % size) for i in range(size) if wrap or 0 <= i + step < size]
    return lax.ppermute(value, "zed", pairs)


def plane_gather_start(own):
    return [own[0], own[1], beside(own[0], 1), beside(own[1], 2)]


def plane_gather_more(first, second, first_got, second_got):
    pair_one, pair_two = jnp.stack([first, first_got]), jnp.stack([second, second_got])
    return [pair_one, pair_two, beside(pair_one, 2), beside(pair_two, 1)]


def plane_gather_end(pair_one, pair_two, first_more, second_more):
    blocks = [pair_one, first_more, pair_two[:1], second_more[:1], pair_two[1:], second_more[1:]]
    return jnp.concatenate(blocks).reshape(-1, pair_one.shape[-1])


def plane_sum_start(terms):
    got_first = beside(jnp.stack([terms[0, 1], terms[0, 3]]).astype(bf16), 1)
    got_second = beside(terms[1, 2:4].astype(bf16), 2)
    return [got_first, got_second]


def plane_sum_more(terms, got_first, got_second):
    first, second = terms[0], terms[1]
    more_first = beside((first[2] + got_first[1]).astype(bf16), 2)
    more_second = beside((second[1] + got_second[1]).astype(bf16), 1)
    return [got_first[0], got_second[0], more_first, more_second]


def plane_sum_end(terms, got_first, got_second, more_first, more_second):
    return jnp.stack([terms[0, 0] + got_first + more_first, terms[1, 0] + got_second + more_second])


def after(value, *earlier):
    return lax.optimization_barrier((value,) + earlier)[0]


def sync(*values):
    return list(lax.optimization_barrier(values))


def core_halves(full):
    size = lax.axis_size("zed")
    s = lax.axis_index("stream")
    full = full.reshape((2, size, -1) + full.shape[1:])
    mine = lax.dynamic_index_in_dim(full, s, 0, keepdims=False)
    theirs = lax.dynamic_index_in_dim(full, 1 - s, 0, keepdims=False)
    return mine, other_core(theirs)


def core_sum(mine, other):
    return (mine.astype(f32) + other.astype(f32)).astype(bf16)


def ring_part(half, k):
    size = lax.axis_size("zed")
    z = lax.axis_index("zed")
    return lax.dynamic_index_in_dim(half, lax.rem(z - k + size, size), 0, keepdims=False)


def ring_add(half, moved, k):
    return (moved.astype(f32) + ring_part(half, k).astype(f32)).astype(bf16)


def plane_swap(value, split, concat):
    return lax.all_to_all(value, "plane", split_axis=split, concat_axis=concat, tiled=True)


def on_device(inputs, cotangent, seq_lengths, gain_attn, gain_ffn, w_query, w_key, w_value, w_out, w_gate, w_up, w_down):
    size = lax.axis_size("zed")
    s, z, p = lax.axis_index("stream"), lax.axis_index("zed"), lax.axis_index("plane")
    micro, _, tok_rows, width = inputs.shape
    chunk = PLANE * tok_rows
    tokens = micro * chunk
    shard_rows = w_query.shape[0]
    ff_block = w_down.shape[0]
    ff_blocks = 2 * size
    ff_part = ff_blocks * ff_block
    q_part, kv_part = HQ * DH // PLANE, HK * DH // PLANE
    out_part = width // PLANE
    e4, e8 = spread(4), spread(8)

    def by_part(weight):
        return weight.reshape(shard_rows, PLANE, -1)

    def by_ff_part(weight):
        return weight.reshape(shard_rows, ff_blocks, PLANE, ff_block).transpose(0, 2, 1, 3).reshape(shard_rows, PLANE, -1)

    def from_ff_parts(term):
        return term.reshape(shard_rows, PLANE, ff_blocks, ff_block).transpose(0, 2, 1, 3).reshape(shard_rows, -1)

    own_in = inputs[:, 0]
    own_cot = cotangent[:, 0]
    gains = jnp.stack([gain_attn, gain_ffn], axis=1)
    gains = jnp.broadcast_to(jnp.pad(gains, ((0, 0), (0, LANES - 2)))[:, None], (shard_rows, PLANE, LANES))
    qkv_bundle = jnp.concatenate([by_part(w_query), by_part(w_key), by_part(w_value), gains, by_part(w_out)], axis=2)
    qkv_block = plane_swap(qkv_bundle.reshape(shard_rows, -1), 1, 0)
    ffn_bundle = jnp.concatenate([by_ff_part(w_gate), by_ff_part(w_up)], axis=2).reshape(shard_rows, -1)
    qkv_blocks = [qkv_block]
    for _ in range(size - 1):
        qkv_blocks.append(along(qkv_blocks[-1], 1, True))
    qkv_other = [other_core(block) for block in qkv_blocks]
    ffn_block = plane_swap(after(ffn_bundle, qkv_block), 1, 0)
    pieces = sync(*plane_gather_start(after(own_in, qkv_block)))
    gathered_in = plane_gather_end(*sync(*plane_gather_more(*pieces)))
    gu_blocks = [after(ffn_block, qkv_blocks[-1])]
    gu_blocks.append(along(gu_blocks[0], 1, True))

    slot_place = ((jnp.arange(PLANE, dtype=jnp.int32) ^ p)[:, None] * tok_rows + jnp.arange(tok_rows, dtype=jnp.int32)[None, :]).reshape(chunk)
    chunk_place = (z - jnp.arange(size, dtype=jnp.int32))[:, None] * chunk + slot_place[None, :]
    lengths = seq_lengths[:, 0]
    seq_ends = jnp.cumsum(lengths, axis=1)
    begins = jnp.sum(
        jnp.where(seq_ends[:, None, None, :] <= chunk_place[None, :, :, None], lengths[:, None, None, :], 0), axis=-1
    )
    own_begin = begins[:, 0]
    lane = np.arange(LANES)
    place_in_half = lane % (LANES // 2)
    real = place_in_half < DH // 2
    frequency = jnp.where(
        real, rope_base ** (-2.0 * jnp.asarray(np.minimum(place_in_half, DH // 2 - 1), f32) / DH), 0.0
    )
    rope_place = (chunk_place[None] - begins).astype(f32)

    def tables(place):
        angles = jnp.maximum(place, 0.0)[..., None] * frequency
        signs = jnp.asarray(np.where(real, np.where(lane < LANES // 2, -1.0, 1.0), 0.0), f32)
        return jnp.where(real, jnp.cos(angles), 0.0), jnp.sin(angles) * signs

    cos, sin = tables(after(rope_place[:, 0], qkv_block))
    index = jnp.stack([z, s]).astype(jnp.int32)
    info = jnp.concatenate([index, jnp.min(own_begin, axis=1)])
    qpos = jnp.tile(chunk_place[0], 2)[None]
    qbeg = jnp.tile(own_begin, (1, 2))[:, None]
    kpos = slot_place[:, None]

    normed_one, q_rot, kv_own, full_qkv, full_oc, full_gains = project(
        index, gathered_in, qkv_blocks + qkv_other, cos.reshape(tokens, LANES), sin.reshape(tokens, LANES), e4, e8
    )
    full_qkv = full_qkv[:, : q_part + 2 * kv_part]
    gain_one, gain_two = full_gains[0:1], full_gains[1:2]
    q_rot = q_rot.reshape(micro, chunk, 4 * LANES)
    full_out = plane_swap(full_oc, 0, 1)
    cot_pieces = plane_gather_start(after(own_cot, gathered_in, kv_own))
    kv_pieces = [[piece] for piece in kv_own.reshape(micro, chunk, 4 * DH)]
    states = [[] for _ in range(micro)]
    for k in range(size):
        if k < size - 1:
            arrived = [along(kv_pieces[m][k], 1, False) for m in range(micro)]
            if k == 0:
                *cot_pieces, arrived[0], arrived[1], gu_blocks[1] = sync(*cot_pieces, *arrived, gu_blocks[1])
                cot_pieces = plane_gather_more(*cot_pieces)
            elif k == 1:
                *cot_pieces, arrived[0], arrived[1], full_out = sync(*cot_pieces, *arrived, full_out)
            else:
                arrived = sync(*arrived)
        for m in range(micro):
            states[m] = attend(m, k, k == size - 1, info, q_rot[m], kv_pieces[m][k], qpos, qbeg[m], kpos, e4, states[m])
            if k < size - 1:
                kv_pieces[m].append(arrived[m])
    kv_there = [pieces[-1] for pieces in kv_pieces]
    attended, lse = [state[2] for state in states], [state[4] for state in states]
    attn_low = jnp.concatenate([state[3] for state in states], axis=0)
    gathered_cot = plane_gather_end(*cot_pieces)

    gu_blocks[1], down_block, rope_place = sync(gu_blocks[1], w_down, rope_place, *kv_there)[:3]
    down_blocks = [down_block]
    branch_terms = dot(attn_low, full_out).reshape(micro, PLANE, tok_rows, width)
    gu_blocks.append(along(gu_blocks[1], 1, True))
    *got, gu_blocks[2] = sync(*plane_sum_start(branch_terms), gu_blocks[2])
    down_blocks.append(along(after(down_blocks[0], gu_blocks[2]), 1, True))
    cos_all, sin_all = tables(after(rope_place, gu_blocks[2]))
    *got, down_blocks[1], cos_all, sin_all = sync(*plane_sum_more(branch_terms, *got), down_blocks[1], cos_all, sin_all)
    layer_in = own_in.astype(f32)
    middle = layer_in + plane_sum_end(branch_terms, *got)
    scale_two = rms_scale(middle)
    pieces = plane_gather_start((middle * scale_two * gain_two).astype(bf16))
    down_blocks.append(along(down_blocks[1], 1, True))
    *pieces, down_blocks[2] = sync(*pieces, down_blocks[2])
    for k in range(2, size - 1):
        gu_blocks.append(along(after(gu_blocks[k], down_blocks[2]), 1, True))
    *pieces, gu_blocks[-1] = sync(*plane_gather_more(*pieces), gu_blocks[-1])
    for k in range(2, size - 1):
        down_blocks.append(along(after(down_blocks[k], gu_blocks[-1]), 1, True))
    full_gu = assemble(index, gu_blocks + [other_core(block) for block in gu_blocks])
    normed_two = plane_gather_end(*pieces)

    pre = dot(normed_two, full_gu)
    gate_pre, up_pre = pre[:, :ff_part], pre[:, ff_part:]
    full_down = assemble(index, down_blocks + [other_core(block) for block in down_blocks])
    sigmoid_gate = jax.nn.sigmoid(gate_pre)
    silu_gate = gate_pre * sigmoid_gate
    hidden = (silu_gate * up_pre).astype(bf16)
    grad_hidden = dot_nt(gathered_cot, full_down)
    grad_gate = (grad_hidden * up_pre * sigmoid_gate * (1.0 + gate_pre * (1.0 - sigmoid_gate))).astype(bf16)
    grad_up = (grad_hidden * silu_gate).astype(bf16)
    grad_gu = jnp.concatenate([grad_gate, grad_up], axis=1)
    normed_terms = dot_nt(grad_gu, full_gu).reshape(micro, PLANE, tok_rows, width)
    got = plane_sum_start(normed_terms)
    gu_mine, gu_other = core_halves(dot_tn(after(normed_two, normed_terms), grad_gu).astype(bf16))
    *got, gu_mine = sync(*got, gu_mine)
    gu_half = core_sum(gu_mine, gu_other)
    down_mine, down_other = core_halves(dot_tn(after(hidden, gu_mine), gathered_cot).astype(bf16))
    gu_total = ring_part(gu_half, size - 1)
    *got, gu_total, down_mine = sync(*plane_sum_more(normed_terms, *got), gu_total, down_mine)
    grad_normed_two = plane_sum_end(normed_terms, *got)
    down_half = core_sum(down_mine, down_other)
    down_total = ring_part(down_half, size - 1)
    result_terms = dot(after(hidden, gu_total), full_down)

    grad_y = own_cot.astype(f32)
    grad_gain_two = jnp.sum(grad_normed_two * middle * scale_two, axis=(0, 1))
    weighted = grad_normed_two * gain_two
    grad_middle = (
        grad_y
        + scale_two * weighted
        - middle * scale_two**3 * jnp.mean(middle * weighted, axis=-1, keepdims=True)
    )
    pieces = plane_gather_start(grad_middle.astype(bf16))
    gu_moved = along(gu_total, -1, True)
    *pieces, gu_moved, down_total, result_terms = sync(*pieces, gu_moved, down_total, result_terms)
    gu_total = ring_add(gu_half, gu_moved, size - 2)
    gu_moved, down_moved = along(gu_total, -1, True), along(down_total, -1, True)
    *pieces, gu_moved, down_moved = sync(*plane_gather_more(*pieces), gu_moved, down_moved)
    grad_branch = plane_gather_end(*pieces)
    for k in range(size - 3, 0, -1):
        gu_moved = along(ring_add(gu_half, gu_moved, k), -1, True)
        down_moved = along(ring_add(down_half, down_moved, k + 1), -1, True)
    grad_attn = dot_nt(grad_branch, full_out).astype(bf16).reshape(micro, chunk, q_part)

    states = [[grad_attn[m], attended[m]] for m in range(micro)]
    grad_kv = [None] * micro
    grad_query = [None] * micro
    result_terms = result_terms.reshape(micro, PLANE, tok_rows, width)
    for k in range(size - 1, -1, -1):
        first = k == size - 1
        for m in range(micro):
            outs = attend_back(
                m, k, first, k == 0, info, q_rot[m], kv_pieces[m][k], lse[m], qpos, qbeg[m], kpos, cos_all[m, k], sin_all[m, k],
                e4, states[m],
            )
            if first:
                states[m] = outs[:3]
                grad_kv[m] = outs[3]
            else:
                states[m] = states[m][:2] + [outs[0]]
                grad_kv[m] = (grad_kv[m].astype(f32) + outs[1].astype(f32)).astype(bf16)
            if k == 0:
                grad_query[m] = outs[-1]
        if first:
            got = plane_sum_start(after(result_terms, *grad_kv))
        if k > 0:
            moved = [along(grad_kv[m], -1, False) for m in range(micro)]
        if k == size - 1:
            *got, gu_moved, down_moved = sync(*got, gu_moved, down_moved)
            sum_gu, down_last = ring_add(gu_half, gu_moved, 0), ring_add(down_half, down_moved, 1)
            down_moved = along(down_last, -1, True)
            got = plane_sum_more(result_terms, *got)
            term_out = plane_swap(dot_tn(attn_low, after(grad_branch, down_last)).astype(bf16), 1, 0)
        elif k == size - 2:
            *got, down_moved, term_out = sync(*got, down_moved, term_out)
            output = (middle + plane_sum_end(result_terms, *got)).astype(bf16)
            sum_down = ring_add(down_half, down_moved, 0)
            sum_gu = plane_swap(after(sum_gu, sum_down), 0, 1)
            out_mine, out_other = core_halves(term_out)
        if k > 0:
            grad_kv = moved
            if not first:
                *flat, grad_kv[0], grad_kv[1] = sync(*[states[m][2] for m in range(micro)], *grad_kv)
                for m in range(micro):
                    states[m] = states[m][:2] + [flat[m]]
    sum_gu = sum_gu.astype(f32).reshape(shard_rows, PLANE, 2, ff_part)

    grad_qkv = jnp.concatenate([jnp.concatenate(grad_query, axis=0), jnp.concatenate(grad_kv, axis=0)], axis=1)
    term_qkv = dot_tn(normed_one, grad_qkv).astype(bf16)
    qkv_mine, qkv_other = core_halves(term_qkv)
    grad_normed_part = dot_nt(after(grad_qkv, qkv_mine), full_qkv)
    part_terms = grad_normed_part.reshape(micro, PLANE, tok_rows, width)
    got = plane_sum_start(part_terms)
    full_in = gathered_in.astype(f32)
    grad_gain_one = jnp.sum(grad_normed_part * full_in * rms_scale(full_in), axis=0)
    gain_terms = jnp.stack([grad_gain_one, grad_gain_two]).astype(bf16)
    gain_terms = jnp.pad(gain_terms, ((0, LANES - 2), (0, 0))).T
    gain_mine, gain_other = core_halves(gain_terms)
    last_half = jnp.concatenate(
        [core_sum(qkv_mine, qkv_other), core_sum(out_mine, out_other), core_sum(gain_mine, gain_other)], axis=-1
    )
    last_total = ring_part(last_half, size - 1)
    for k in range(size - 2, -1, -1):
        last_moved = along(last_total, -1, True)
        if k == size - 2:
            *got, last_moved = sync(*got, last_moved)
            got = plane_sum_more(part_terms, *got)
        elif k == size - 3:
            *got, last_moved = sync(*got, last_moved)
        last_total = ring_add(last_half, last_moved, k)
    grad_normed_one = plane_sum_end(part_terms, *got)
    last_total = plane_swap(last_total, 0, 1).astype(f32).reshape(shard_rows, PLANE, -1)
    scale_one = rms_scale(layer_in)
    weighted = grad_normed_one * gain_one
    input_grad = (
        grad_middle
        + scale_one * weighted
        - layer_in * scale_one**3 * jnp.mean(layer_in * weighted, axis=-1, keepdims=True)
    )
    cuts = np.cumsum([q_part, kv_part, kv_part, out_part])
    sum_query, sum_key, sum_value, sum_out, gain_sum = jnp.split(last_total, cuts, axis=2)
    gain_sum = jnp.sum(gain_sum, axis=1)
    return (
        output[:, None],
        input_grad[:, None],
        gain_sum[:, 0],
        gain_sum[:, 1],
        sum_query.reshape(shard_rows, -1),
        sum_key.reshape(shard_rows, -1),
        sum_value.reshape(shard_rows, -1),
        sum_out.reshape(shard_rows, -1),
        from_ff_parts(sum_gu[:, :, 0]),
        from_ff_parts(sum_gu[:, :, 1]),
        sum_down.astype(f32),
    )


def solution(mesh):
    blocks = mesh.shape["blk"]
    grid = Mesh(mesh.devices.reshape(2, blocks // PLANE, PLANE), ("stream", "zed", "plane"))
    tokens = P(None, "stream", ("zed", "plane"), None)
    vector = P(("stream", "zed", "plane"))
    matrix = P(("stream", "zed", "plane"), None)
    return jax.shard_map(
        on_device,
        mesh=grid,
        in_specs=(tokens, tokens, P(None, "stream", None), vector, vector) + (matrix,) * 7,
        out_specs=(tokens, tokens, vector, vector) + (matrix,) * 7,
        check_vma=False,
    )
```

time: 736 us -> 621 us (0.84)
  waiting for transfers between devices: 286 us -> 172 us
  starting transfers between devices: 173 us -> 137 us
  Pallas kernels: 39.6 us -> 68.9 us
  other arithmetic: 75.8 us -> 86.8 us
  matrix products: 74.4 us -> 64 us
    ppermute x36 -> x32, waiting for transfers between devices: 126 us -> 52.3 us  [beside(): return lax.ppermute(value, 'plane', [(i, i ^ bit) for i in range(PLANE)])]
    ppermute x36 -> x30, waiting for transfers between devices: 155 us -> 109 us  [along(): return lax.ppermute(value, 'zed', pairs)]
    pallas_call x3 -> x19, Pallas kernels: 39.6 us -> 68.9 us  [the longest x16 46.2 us: run_kernel(): pl.pallas_call(body, grid_spec=pltpu.PrefetchScalarGridSpec(num_scalar_pr...]
    ppermute x36 -> x30, starting transfers between devices: 102 us -> 73.5 us  [along(): return lax.ppermute(value, 'zed', pairs)]
    dynamic_update_slice x39 -> x0, local copies, waits for them, and re-layouts: 27.3 us -> none  [the longest x19 13.7 us: weight_gather(): full = lax.dynamic_update_slice(full, block[None], (s * size + place, 0, 0))]
    unnamed x140 -> x238, local copies, waits for them, and re-layouts: 4.29 us -> 27.9 us
    all_to_all x7 -> x6, waiting for transfers between devices: 0.58 us -> 10.1 us  [plane_swap(): lax.all_to_all(value, 'plane', split_axis=split, concat_axis=concat, tile...]
    convert_element_type x26 -> x30, other arithmetic: 27.8 us -> 36.4 us  [the longest x8 9.03 us: ring_add(): return (moved.astype(f32) + ring_part(half, k).astype(f32)).astype(bf16)]
  transfers between devices with their start and end apart: 104 -> 85, of which waited for: 47 -> 33; matrix products, arithmetic and copies ran while one was open for 22% -> 28% of each run, Pallas kernels for 5% -> 9%
where the time goes in v3:
time: 621 us; the launch traced here: 612 us
  waiting for transfers between devices  172 us (28%)
  starting transfers between devices  137 us (22%)
  other arithmetic  86.8 us (14%)
  local copies, waits for them, and re-layouts  80.2 us (13%)
  Pallas kernels  68.9 us (11%)
  matrix products  64 us (10%)
    ppermute x30, waiting for transfers between devices, along(): return lax.ppermute(value, 'zed', pairs)  109 us
    ppermute x30, starting transfers between devices, along(): return lax.ppermute(value, 'zed', pairs)  73.5 us
    ppermute x32, waiting for transfers between devices, beside(): return lax.ppermute(value, 'plane', [(i, i ^ bit) for i in range(PLANE)])  52.3 us
    pallas_call x16, Pallas kernels, run_kernel(): pl.pallas_call(body, grid_spec=pltpu.PrefetchScalarGridSpec(num_scalar_pr...  46.2 us
    ppermute x32, starting transfers between devices, beside(): return lax.ppermute(value, 'plane', [(i, i ^ bit) for i in range(PLANE)])  35.2 us
    unnamed x238, local copies, waits for them, and re-layouts  27.9 us
    dot_general x4, matrix products, dot_nt(): lax.dot_general(a, b, (((1,), (1,)), ((), ())), preferred_element_type=f32)  27 us
    all_to_all x6, starting transfers between devices, plane_swap(): lax.all_to_all(value, 'plane', split_axis=split, concat_axis=concat, tile...  25.3 us
  transfers between devices with their start and end apart: 85, of which 33 were waited for; matrix products, arithmetic and copies ran while one was open for 28% of the time, Pallas kernels for 9%

profile of v3, /device:TPU:0, one launch (start us, length us, event | category | flops | bytes accessed | tf_op | source)
XLA Modules:
  0.0 611.9 jit_solution(17069036872187133287)
XLA Ops:
  10.9 7.6 %all-to-all-done = bf16[48,4,1280]{2,0,1:T(8,128)(2,1)S(1)} async-done(((bf16[48,4,1280]{2,0,1:T(8,128)(2,1)}), bf16[48,4,1280]{2,0,1:T(8,128)(2,1)S(1)}, u32[]{:S(2)}, u32[]{:S(2)}) %all-to-all-start) | async-done | bytes 491552 | tf_op jit(solution)/shard_map/all_to_all | solution.py:422
  49.2 7.6 %collective-permute-done.2 = bf16[2,128,1536]{2,1,0:T(8,128)(2,1)} collective-permute-done((bf16[2,128,1536]{2,1,0:T(8,128)(2,1)}, bf16[2,128,1536]{2,1,0:T(8,128)(2,1)}, u32[]{:S(2)}, u32[]{:S(2)}) %collective-permute-start.2) | collective-permute-done | bytes 786464 | tf_op jit(solution)/shard_map/ppermute | solution.py:346
  67.7 13.4 %project.1 = (bf16[1024,1536]{1,0:T(8,128)(2,1)}, bf16[1024,512]{1,0:T(8,128)(2,1)}, bf16[1024,384]{1,0:T(8,128)(2,1)}, bf16[1536,896]{1,0:T(8,128)(2,1)}, bf16[...) custom-call(s32[2]{0:T(128)S(1)} %pad_add_fusion.1.refs_0_, bf16[1024,1536]{1,0:T(8,128)(2,1)} %bitcast.15.refs_1_, ...), custom_call_target="tpu_custom_call" | custom-call | flops 3221225472 | bytes 14155776 | tf_op jit(solution)/shard_map/project/pallas_call | solution.py:94
  168.4 5.7 collective-permute-start.24
  183.2 7.1 %collective-permute-done.24.refs_3_ = bf16[192,2048]{1,0:T(8,128)(2,1)S(1)} collective-permute-done((bf16[192,2048]{1,0:T(8,128)(2,1)S(1)}, bf16[192,2048]{1,0:T(8,128)(2,1)S(1)}, u32[]{:S(2)}, u32[]{:S(2)}) %collective-permute-start.24) | collective-permute-done | bytes 786464 | tf_op jit(solution)/shard_map/ppermute | solution.py:356
  192.8 8.9 %fusion.5 = (f32[2,4,512,128]{3,2,1,0:T(8,128)}, f32[2,4,512,128]{3,2,1,0:T(8,128)}) fusion(f32[128]{0:T(128)S(1)} %copy-done.96, f32[128]{0:T(128)S(1)} %copy-done.97, f32[2,4,512]{2,1,0:T(4,128)S(1)} %broadcast_maximum_fusion, pred[128]{0:T(512)(128)(4,1)S(1)} %copy-done.95), kind=kLoop, calls=%fused_computation.26 | loop fusion | flops 1572864 | bytes 4211840 | tf_op jit(solution)/shard_map/mul | solution.py:484
  209.4 7.2 %collective-permute-done.28 = bf16[128,1536]{1,0:T(8,128)(2,1)S(1)} collective-permute-done((bf16[128,1536]{1,0:T(8,128)(2,1)S(1)}, bf16[128,1536]{1,0:T(8,128)(2,1)S(1)}, u32[]{:S(2)}, u32[]{:S(2)}) %collective-permute-start.28) | collective-permute-done | bytes 393248 | tf_op jit(solution)/shard_map/ppermute | solution.py:346
  224.3 14.6 %collective-permute-done.33.refs_4_ = bf16[192,2048]{1,0:T(8,128)(2,1)S(1)} collective-permute-done((bf16[192,2048]{1,0:T(8,128)(2,1)S(1)}, bf16[192,2048]{1,0:T(8,128)(2,1)S(1)}, u32[]{:S(2)}, u32[]{:S(2)}) %collective-permute-start.33) | collective-permute-done | bytes 786464 | tf_op jit(solution)/shard_map/ppermute | solution.py:356
  241.4 11.0 %collective-permute-done.34.refs_4_ = bf16[128,1536]{1,0:T(8,128)(2,1)S(1)} collective-permute-done((bf16[128,1536]{1,0:T(8,128)(2,1)S(1)}, bf16[128,1536]{1,0:T(8,128)(2,1)S(1)}, u32[]{:S(2)}, u32[]{:S(2)}) %collective-permute-start.34) | collective-permute-done | bytes 393248 | tf_op jit(solution)/shard_map/ppermute | solution.py:356
  253.3 5.9 assemble.3
  259.1 11.9 %fusion.83 = f32[1024,2048]{0,1:T(8,128)} fusion(bf16[1024,1536]{1,0:T(8,128)(2,1)} %bitcast.507, bf16[1536,2048]{1,0:T(8,128)(2,1)} %assemble.3), kind=kOutput, calls=%fused_computation.282 | convolution fusion | flops 6442450944 | bytes 17825792 | tf_op jit(solution)/shard_map/dot_general | solution.py:43
  274.5 11.7 %multiply_convert_fusion.2 = (bf16[1024,1024]{0,1:T(8,128)(2,1)S(1)}, bf16[1024,1024]{0,1:T(8,128)(2,1)S(1)}, bf16[1024,1024]{0,1:T(8,128)(2,1)}) fusion(f32[1024,2048]{0,1:T(8,128)} %fusion.83, bf16[1024,1536]{1,0:T(8,128)(2,1)} %bitcast.505, bf16[1024,1536]{1,0:T(8,128)(2,1)} %assemble.2), kind=kOutput, calls=%fused_computation.7 | convolution fusion | flops 3236954112 | bytes 20971520 | tf_op jit(solution)/shard_map/dot_general | solution.py:47
  286.2 6.8 %fusion.1 = f32[1024,1536]{1,0:T(8,128)S(1)} fusion(bf16[1536,2048]{1,0:T(8,128)(2,1)S(1)} %bitcast.474, bf16[1024,1024]{0,1:T(8,128)(2,1)S(1)} %get-tuple-element.333, bf16[1024,1024]{0,1:T(8,128)(2,1)S(1)} %get-tuple-element.332), kind=kOutput, calls=%fused_computation.18 | convolution fusion | flops 6450839552 | bytes 16777216 | tf_op jit(solution)/shard_map/dot_general | solution.py:47
  297.9 7.5 %convolution_convert_fusion = bf16[1536,2048]{1,0:T(8,128)(2,1)S(1)} fusion(bf16[1024,1536]{1,0:T(8,128)(2,1)S(1)} %bitcast.508, bf16[1024,1024]{0,1:T(8,128)(2,1)S(1)} %get-tuple-element.333, bf16[1024,1024]{0,1:T(8,128)(2,1)S(1)} %get-tuple-element.332), kind=kOutput, calls=%fused_computation | convolution fusion | flops 6453985280 | bytes 13631488 | tf_op jit(solution)/shard_map/dot_general | solution.py:51
  314.9 11.6 %collective-permute-done.43 = bf16[2,128,1536]{2,1,0:T(8,128)(2,1)S(1)} collective-permute-done((bf16[2,128,1536]{2,1,0:T(8,128)(2,1)}, bf16[2,128,1536]{2,1,0:T(8,128)(2,1)S(1)}, u32[]{:S(2)}, u32[]{:S(2)}) %collective-permute-start.43) | collective-permute-done | bytes 786464 | tf_op jit(solution)/shard_map/ppermute | solution.py:346
  348.5 6.0 fusion.84
  365.9 19.3 %collective-permute-done.55 = bf16[128,1536]{1,0:T(8,128)(2,1)S(1)} collective-permute-done((bf16[128,1536]{1,0:T(8,128)(2,1)S(1)}, bf16[128,1536]{1,0:T(8,128)(2,1)S(1)}, u32[]{:S(2)}, u32[]{:S(2)}) %collective-permute-start.55) | collective-permute-done | bytes 393248 | tf_op jit(solution)/shard_map/ppermute | solution.py:356
  405.0 9.1 %collective-permute-start.58 = (bf16[192,2048]{1,0:T(8,128)(2,1)S(1)}, bf16[192,2048]{1,0:T(8,128)(2,1)S(1)}, u32[]{:S(2)}, u32[]{:S(2)}) collective-permute-start(bf16[192,2048]{1,0:T(8,128)(2,1)S(1)} %fusion.17), channel_id=1, source_target_pairs={{0,12},{4,0},{8,4},{12,8},{1,13},{5,1},{9,5},{13,9},{2,14},{6,2},{... | collective-permute-start | bytes 2359304 | tf_op jit(solution)/shard_map/ppermute | solution.py:356
  432.0 17.7 %collective-permute-done.59 = bf16[128,1536]{1,0:T(8,128)(2,1)S(1)} collective-permute-done((bf16[128,1536]{1,0:T(8,128)(2,1)S(1)}, bf16[128,1536]{1,0:T(8,128)(2,1)S(1)}, u32[]{:S(2)}, u32[]{:S(2)}) %collective-permute-start.59) | collective-permute-done | bytes 393248 | tf_op jit(solution)/shard_map/ppermute | solution.py:356
  453.2 8.3 %collective-permute-start.62 = (bf16[128,1536]{1,0:T(8,128)(2,1)}, bf16[128,1536]{1,0:T(8,128)(2,1)}, u32[]{:S(2)}, u32[]{:S(2)}) collective-permute-start(bf16[128,1536]{1,0:T(8,128)(2,1)} %fusion.50), channel_id=1, source_target_pairs={{0,12},{4,0},{8,4},{12,8},{1,13},{5,1},{9,5},{13,9},{2,14},{6,2},{... | collective-permute-start | bytes 1179656 | tf_op jit(solution)/shard_map/ppermute | solution.py:356
  497.2 6.4 %attend_back.14 = (f32[2,128,1024]{2,1,0:T(8,128)}, bf16[512,384]{1,0:T(8,128)(2,1)S(1)}, bf16[512,384]{1,0:T(8,128)(2,1)S(1)}) custom-call(s32[4]{0:T(128)S(1)} %pad_add_fusion.refs_0_, bf16[512,512]{1,0:T(8,128)(2,1)S(1)} %get-tuple-element.394.refs_1_, bf16[512,384]{1,0:T(8,128)(2,1)S(1)} %copy-done.7, ...), custom_call_target="tpu_custom_call", output_to_operand_aliasing={{0}: (12, {})} | custom-call | flops 1342177280 | bytes 5269504 | tf_op jit(solution)/shard_map/attend_back/pallas_call | solution.py:174
  503.7 6.7 %attend_back.15 = (f32[2,128,1024]{2,1,0:T(8,128)}, bf16[512,384]{1,0:T(8,128)(2,1)S(1)}, bf16[512,384]{1,0:T(8,128)(2,1)S(1)}) custom-call(s32[4]{0:T(128)S(1)} %pad_add_fusion.refs_0_, bf16[512,512]{1,0:T(8,128)(2,1)S(1)} %get-tuple-element.393.refs_1_, bf16[512,384]{1,0:T(8,128)(2,1)S(1)} %copy-done.4, ...), custom_call_target="tpu_custom_call", output_to_operand_aliasing={{0}: (12, {})} | custom-call | flops 1342177280 | bytes 5269504 | tf_op jit(solution)/shard_map/attend_back/pallas_call | solution.py:174
  576.4 8.5 %collective-permute-done.75 = bf16[128,1536]{1,0:T(8,128)(2,1)S(1)} collective-permute-done((bf16[128,1536]{1,0:T(8,128)(2,1)S(1)}, bf16[128,1536]{1,0:T(8,128)(2,1)S(1)}, u32[]{:S(2)}, u32[]{:S(2)}) %collective-permute-start.75) | collective-permute-done | bytes 393248 | tf_op jit(solution)/shard_map/ppermute | solution.py:346
  590.5 5.9 collective-permute-done.78
  (568 shorter events, 382.6 us)
Async XLA Ops:
  37.2 30.5 %collective-permute-start.7 = (bf16[192,1280]{1,0:T(8,128)(2,1)S(1)}, bf16[192,1280]{1,0:T(8,128)(2,1)}, u32[]{:S(2)}, u32[]{:S(2)}) collective-permute-start(bf16[192,1280]{1,0:T(8,128)(2,1)S(1)} %bitcast.429), channel_id=1, source_target_pairs={{0,16},{16,0},{1,17},{17,1},{2,18},{18,2},{3,19},{19,3},{4,20},{20... | collective-permute-start | bytes 1474568 | tf_op jit(solution)/shard_map/ppermute | solution.py:350
  38.3 27.8 %all-to-all-start.1 = ((bf16[48,4,2048]{2,0,1:T(8,128)(2,1)}), bf16[48,4,2048]{2,0,1:T(8,128)(2,1)S(1)}, u32[]{:S(2)}, u32[]{:S(2)}) async-start(bf16[48,4,2048]{2,0,1:T(8,128)(2,1)} %bitcast.477), calls=%async_computation.1 | async-start | bytes 1572864 | tf_op jit(solution)/shard_map/all_to_all | solution.py:422
  66.1 33.5 %collective-permute-start.15 = (bf16[192,2048]{1,0:T(8,128)(2,1)S(1)}, bf16[192,2048]{1,0:T(8,128)(2,1)S(1)}, u32[]{:S(2)}, u32[]{:S(2)}) collective-permute-start(bf16[192,2048]{1,0:T(8,128)(2,1)S(1)} %bitcast.425), channel_id=1, source_target_pairs={{0,4},{4,8},{8,12},{12,0},{1,5},{5,9},{9,13},{13,1},{2,6},{6,10},{... | collective-permute-start | bytes 2359304 | tf_op jit(solution)/shard_map/ppermute | solution.py:356
  95.3 35.9 %all-to-all-start.2 = ((bf16[4,384,384]{1,2,0:T(8,128)(2,1)}), bf16[4,384,384]{1,2,0:T(8,128)(2,1)}, u32[]{:S(2)}, u32[]{:S(2)}) async-start(bf16[4,384,384]{1,2,0:T(8,128)(2,1)} %copy.187), calls=%async_computation.2 | async-start | bytes 2359296 | tf_op jit(solution)/shard_map/all_to_all | solution.py:422
  107.4 23.9 %collective-permute-start.17 = (bf16[2,128,1536]{2,1,0:T(8,128)(2,1)}, bf16[2,128,1536]{2,1,0:T(8,128)(2,1)}, u32[]{:S(2)}, u32[]{:S(2)}) collective-permute-start(bf16[2,128,1536]{2,1,0:T(8,128)(2,1)} %pad_maximum_fusion.9), channel_id=1, source_target_pairs={{0,1},{1,0},{2,3},{3,2},{4,5},{5,4},{6,7},{7,6},{8,9},{9,8},{10,11... | collective-permute-start | bytes 2359304 | tf_op jit(solution)/shard_map/ppermute | solution.py:346
  120.5 119.3 %collective-permute-start.39 = (bf16[192,2048]{1,0:T(8,128)(2,1)S(1)}, bf16[192,2048]{1,0:T(8,128)(2,1)}, u32[]{:S(2)}, u32[]{:S(2)}) collective-permute-start(bf16[192,2048]{1,0:T(8,128)(2,1)S(1)} %bitcast.426), channel_id=1, source_target_pairs={{0,16},{16,0},{1,17},{17,1},{2,18},{18,2},{3,19},{19,3},{4,20},{20... | collective-permute-start | bytes 2359304 | tf_op jit(solution)/shard_map/ppermute | solution.py:350
  131.3 24.0 %collective-permute-start.20 = (bf16[512,384]{1,0:T(8,128)(2,1)}, bf16[512,384]{1,0:T(8,128)(2,1)S(1)}, u32[]{:S(2)}, u32[]{:S(2)}) collective-permute-start(bf16[512,384]{1,0:T(8,128)(2,1)} %collective-permute-done.18.refs_2_), channel_id=1, source_target_pairs={{0,4},{4,8},{8,12},{1,5},{5,9},{9,13},{2,6},{6,10},{10,14},{3,7},{... | collective-permute-start | bytes 1179656 | tf_op jit(solution)/shard_map/ppermute | solution.py:356
  239.8 31.3 %collective-permute-start.35 = (bf16[128,1536]{1,0:T(8,128)(2,1)S(1)}, bf16[128,1536]{1,0:T(8,128)(2,1)S(1)}, u32[]{:S(2)}, u32[]{:S(2)}) collective-permute-start(bf16[128,1536]{1,0:T(8,128)(2,1)S(1)} %copy-done.1), channel_id=1, source_target_pairs={{0,16},{16,0},{1,17},{17,1},{2,18},{18,2},{3,19},{19,3},{4,20},{20... | collective-permute-start | bytes 1179656 | tf_op jit(solution)/shard_map/ppermute | solution.py:350
  239.9 31.1 %collective-permute-start.36 = (bf16[128,1536]{1,0:T(8,128)(2,1)S(1)}, bf16[128,1536]{1,0:T(8,128)(2,1)S(1)}, u32[]{:S(2)}, u32[]{:S(2)}) collective-permute-start(bf16[128,1536]{1,0:T(8,128)(2,1)S(1)} %collective-permute-done.27.refs_2_), channel_id=1, source_target_pairs={{0,16},{16,0},{1,17},{17,1},{2,18},{18,2},{3,19},{19,3},{4,20},{20... | collective-permute-start | bytes 1179656 | tf_op jit(solution)/shard_map/ppermute | solution.py:350
  241.2 29.8 %collective-permute-start.37 = (bf16[128,1536]{1,0:T(8,128)(2,1)S(1)}, bf16[128,1536]{1,0:T(8,128)(2,1)S(1)}, u32[]{:S(2)}, u32[]{:S(2)}) collective-permute-start(bf16[128,1536]{1,0:T(8,128)(2,1)S(1)} %collective-permute-done.30.refs_3_), channel_id=1, source_target_pairs={{0,16},{16,0},{1,17},{17,1},{2,18},{18,2},{3,19},{19,3},{4,20},{20... | collective-permute-start | bytes 1179656 | tf_op jit(solution)/shard_map/ppermute | solution.py:350
  359.1 26.1 %collective-permute-start.54 = (bf16[192,2048]{1,0:T(8,128)(2,1)S(1)}, bf16[192,2048]{1,0:T(8,128)(2,1)S(1)}, u32[]{:S(2)}, u32[]{:S(2)}) collective-permute-start(bf16[192,2048]{1,0:T(8,128)(2,1)S(1)} %fusion.18), channel_id=1, source_target_pairs={{0,12},{4,0},{8,4},{12,8},{1,13},{5,1},{9,5},{13,9},{2,14},{6,2},{... | collective-permute-start | bytes 2359304 | tf_op jit(solution)/shard_map/ppermute | solution.py:356
  403.4 25.5 %collective-permute-start.63 = (bf16[512,384]{1,0:T(8,128)(2,1)S(1)}, bf16[512,384]{1,0:T(8,128)(2,1)}, u32[]{:S(2)}, u32[]{:S(2)}) collective-permute-start(bf16[512,384]{1,0:T(8,128)(2,1)S(1)} %get-tuple-element.265), channel_id=1, source_target_pairs={{4,0},{8,4},{12,8},{5,1},{9,5},{13,9},{6,2},{10,6},{14,10},{7,3},{... | collective-permute-start | bytes 1179656 | tf_op jit(solution)/shard_map/ppermute | solution.py:356
  405.0 46.0 %collective-permute-start.58 = (bf16[192,2048]{1,0:T(8,128)(2,1)S(1)}, bf16[192,2048]{1,0:T(8,128)(2,1)S(1)}, u32[]{:S(2)}, u32[]{:S(2)}) collective-permute-start(bf16[192,2048]{1,0:T(8,128)(2,1)S(1)} %fusion.17), channel_id=1, source_target_pairs={{0,12},{4,0},{8,4},{12,8},{1,13},{5,1},{9,5},{13,9},{2,14},{6,2},{... | collective-permute-start | bytes 2359304 | tf_op jit(solution)/shard_map/ppermute | solution.py:356
  414.1 36.9 %collective-permute-start.56 = (bf16[2,128,1536]{2,1,0:T(8,128)(2,1)S(1)}, bf16[2,128,1536]{2,1,0:T(8,128)(2,1)S(1)}, u32[]{:S(2)}, u32[]{:S(2)}) collective-permute-start(bf16[2,128,1536]{2,1,0:T(8,128)(2,1)S(1)} %pad_maximum_fusion.16), channel_id=1, source_target_pairs={{0,1},{1,0},{2,3},{3,2},{4,5},{5,4},{6,7},{7,6},{8,9},{9,8},{10,11... | collective-permute-start | bytes 2359304 | tf_op jit(solution)/shard_map/ppermute | solution.py:346
  416.4 34.7 %collective-permute-start.57 = (bf16[2,128,1536]{2,1,0:T(8,128)(2,1)}, bf16[2,128,1536]{2,1,0:T(8,128)(2,1)S(1)}, u32[]{:S(2)}, u32[]{:S(2)}) collective-permute-start(bf16[2,128,1536]{2,1,0:T(8,128)(2,1)} %slice_bitcast_fusion.4), channel_id=1, source_target_pairs={{0,2},{1,3},{2,0},{3,1},{4,6},{5,7},{6,4},{7,5},{8,10},{9,11},{10,... | collective-permute-start | bytes 2359304 | tf_op jit(solution)/shard_map/ppermute | solution.py:346
  422.7 27.0 %collective-permute-start.59 = (bf16[128,1536]{1,0:T(8,128)(2,1)S(1)}, bf16[128,1536]{1,0:T(8,128)(2,1)S(1)}, u32[]{:S(2)}, u32[]{:S(2)}) collective-permute-start(bf16[128,1536]{1,0:T(8,128)(2,1)S(1)} %copy-done.78), channel_id=1, source_target_pairs={{0,12},{4,0},{8,4},{12,8},{1,13},{5,1},{9,5},{13,9},{2,14},{6,2},{... | collective-permute-start | bytes 1179656 | tf_op jit(solution)/shard_map/ppermute | solution.py:356
  428.8 46.1 %collective-permute-start.66 = (bf16[512,384]{1,0:T(8,128)(2,1)}, bf16[512,384]{1,0:T(8,128)(2,1)}, u32[]{:S(2)}, u32[]{:S(2)}) collective-permute-start(bf16[512,384]{1,0:T(8,128)(2,1)} %add_convert_fusion.7), channel_id=1, source_target_pairs={{4,0},{8,4},{12,8},{5,1},{9,5},{13,9},{6,2},{10,6},{14,10},{7,3},{... | collective-permute-start | bytes 1179656 | tf_op jit(solution)/shard_map/ppermute | solution.py:356
  449.7 25.2 %collective-permute-start.64 = (bf16[512,384]{1,0:T(8,128)(2,1)}, bf16[512,384]{1,0:T(8,128)(2,1)}, u32[]{:S(2)}, u32[]{:S(2)}) collective-permute-start(bf16[512,384]{1,0:T(8,128)(2,1)} %add_convert_fusion.8), channel_id=1, source_target_pairs={{4,0},{8,4},{12,8},{5,1},{9,5},{13,9},{6,2},{10,6},{14,10},{7,3},{... | collective-permute-start | bytes 1179656 | tf_op jit(solution)/shard_map/ppermute | solution.py:356
  453.2 62.8 %collective-permute-start.62 = (bf16[128,1536]{1,0:T(8,128)(2,1)}, bf16[128,1536]{1,0:T(8,128)(2,1)}, u32[]{:S(2)}, u32[]{:S(2)}) collective-permute-start(bf16[128,1536]{1,0:T(8,128)(2,1)} %fusion.50), channel_id=1, source_target_pairs={{0,12},{4,0},{8,4},{12,8},{1,13},{5,1},{9,5},{13,9},{2,14},{6,2},{... | collective-permute-start | bytes 1179656 | tf_op jit(solution)/shard_map/ppermute | solution.py:356
  464.1 51.9 %all-to-all-start.3 = ((bf16[384,4,384]{2,0,1:T(8,128)(2,1)}), bf16[384,4,384]{2,0,1:T(8,128)(2,1)}, u32[]{:S(2)}, u32[]{:S(2)}) async-start(bf16[384,4,384]{2,0,1:T(8,128)(2,1)} %bitcast.476), calls=%async_computation.3 | async-start | bytes 2359296 | tf_op jit(solution)/shard_map/all_to_all | solution.py:422
  470.6 45.5 %collective-permute-start.60 = (bf16[128,1536]{1,0:T(8,128)(2,1)S(1)}, bf16[128,1536]{1,0:T(8,128)(2,1)}, u32[]{:S(2)}, u32[]{:S(2)}) collective-permute-start(bf16[128,1536]{1,0:T(8,128)(2,1)S(1)} %get-tuple-element.358), channel_id=1, source_target_pairs={{0,2},{1,3},{2,0},{3,1},{4,6},{5,7},{6,4},{7,5},{8,10},{9,11},{10,... | collective-permute-start | bytes 1179656 | tf_op jit(solution)/shard_map/ppermute | solution.py:346
  472.7 43.3 %collective-permute-start.61 = (bf16[128,1536]{1,0:T(8,128)(2,1)S(1)}, bf16[128,1536]{1,0:T(8,128)(2,1)}, u32[]{:S(2)}, u32[]{:S(2)}) collective-permute-start(bf16[128,1536]{1,0:T(8,128)(2,1)S(1)} %get-tuple-element.357), channel_id=1, source_target_pairs={{0,1},{1,0},{2,3},{3,2},{4,5},{5,4},{6,7},{7,6},{8,9},{9,8},{10,11... | collective-permute-start | bytes 1179656 | tf_op jit(solution)/shard_map/ppermute | solution.py:346
  518.1 31.4 %all-to-all-start.5 = ((bf16[4,48,2048]{2,1,0:T(8,128)(2,1)}), bf16[4,48,2048]{2,1,0:T(8,128)(2,1)}, u32[]{:S(2)}, u32[]{:S(2)}) async-start(bf16[4,48,2048]{2,1,0:T(8,128)(2,1)} %bitcast.155), calls=%async_computation.5 | async-start | bytes 1572864 | tf_op jit(solution)/shard_map/all_to_all | solution.py:422
  542.6 25.6 %collective-permute-start.69 = (bf16[2,128,1536]{2,1,0:T(8,128)(2,1)}, bf16[2,128,1536]{2,1,0:T(8,128)(2,1)}, u32[]{:S(2)}, u32[]{:S(2)}) collective-permute-start(bf16[2,128,1536]{2,1,0:T(8,128)(2,1)} %pad_maximum_fusion.17), channel_id=1, source_target_pairs={{0,1},{1,0},{2,3},{3,2},{4,5},{5,4},{6,7},{7,6},{8,9},{9,8},{10,11... | collective-permute-start | bytes 2359304 | tf_op jit(solution)/shard_map/ppermute | solution.py:346
  (165 other events, 2411.9 us)
